TPU v7x, 32 devices: a whole 2x2x4 slice. The times are simulated.
32 devices in a mesh: dp: 4 (over y, core), expert: 8 (over z, x).
Axes of the slice: x: 2, y: 2, z: 4, core: 2. Of those that a mesh axis runs over, the one named last changes fastest.
Arguments:
- tokens: bfloat16 [4096, 5120], P(('dp', 'expert')), may hold values from -6 to 6
- grad_out: bfloat16 [4096, 5120], P(('dp', 'expert')), may hold values from -1.5 to 1.5
- expert_ids: int32 [4096, 2], P(('dp', 'expert')), may hold values from 0 to 7, as said below
- gate_codes: int32 [4096, 2], P(('dp', 'expert')), may hold values from 1 to 1023
- w_up: bfloat16 [8, 5120, 768], P('expert', 'dp'), may hold values from -0.078125 to 0.078125
- w_down: bfloat16 [8, 5120, 768], P('expert', 'dp'), may hold values from -2.5 to 2.5
Outputs:
- layer_output: bfloat16 [4096, 5120], P(('dp', 'expert'))
- grad_tokens: bfloat16 [4096, 5120], P(('dp', 'expert'))
- grad_up: bfloat16 [8, 5120, 768], P('expert', 'dp')
- grad_down: bfloat16 [8, 5120, 768], P('expert', 'dp')
Inputs may be any that keep to these rules, and one draw needn't show every extreme that they name: `expert_ids`: each row names two different experts. Among the rows of one device no expert is named more than 38 times, and in every draw one expert is named exactly 38 times by the rows of every device.
All inputs are finite; a program needn't handle non-finite values.
Results may differ from a plain program's by a relative error of at most 0.0065.
Values may be sent and summed in bfloat16 or wider, within the bound.
No kernel may reach another device: no remote copies, remote signals or barrier semaphores. Data moves between devices by JAX's collectives and lax.ppermute only.
A program may use at most 192 MiB of HBM per device.

v0:
```python
import math

import jax
import jax.numpy as jnp
from jax import lax
from jax.sharding import PartitionSpec as P

LAYERS = 40


def activate(values):
    return jax.nn.gelu(values, approximate=True)


def contract_rows(former, latter):
    return lax.dot_general(
        former, latter, (((0,), (0,)), ((), ())), preferred_element_type=jnp.float32
    )


def contract_columns(former, latter):
    return lax.dot_general(
        former, latter, (((1,), (1,)), ((), ())), preferred_element_type=jnp.float32
    )


def expert_forward(recv_rows, up_weight, down_weight):
    pre_act = jnp.dot(recv_rows, up_weight, preferred_element_type=jnp.float32)
    hidden = activate(pre_act).astype(jnp.bfloat16)
    expert_out = contract_columns(hidden, down_weight).astype(jnp.bfloat16)
    return (pre_act, hidden, expert_out)


def expert_backward(recv_grads, pre_act, up_weight, down_weight):
    hidden_grad = jnp.dot(recv_grads, down_weight, preferred_element_type=jnp.float32)
    pre_grad = jax.vjp(activate, pre_act)[1](hidden_grad)[0].astype(jnp.bfloat16)
    row_grad = contract_columns(pre_grad, up_weight).astype(jnp.bfloat16)
    return (pre_grad, row_grad)


def combine_slots(returned, slot_index, weights, n_rows):
    picked_rows = returned[slot_index].astype(jnp.float32) * weights[:, None]
    return jnp.sum(picked_rows.reshape(n_rows, 2, returned.shape[1]), axis=1).astype(jnp.bfloat16)


def local(tokens, grad_out, expert_ids, gate_codes, w_up, w_down):
    n_expert = lax.axis_size("expert")
    n_rows = tokens.shape[0]
    capacity = max(2, 12 * n_rows // (5 * n_expert))
    out_scale = 1.0 / math.sqrt(2.0 * LAYERS)
    flat_ids = expert_ids.reshape(-1)
    gate_values = gate_codes.astype(jnp.float32)
    flat_gates = (gate_values / jnp.sum(gate_values, axis=1, keepdims=True)).reshape(-1)
    onehot = (flat_ids[:, None] == jnp.arange(n_expert, dtype=jnp.int32)[None, :]).astype(jnp.int32)
    before = jnp.sum((jnp.cumsum(onehot, axis=0) - onehot) * onehot, axis=1)
    slot_index = flat_ids * capacity + before
    source_rows = jnp.arange(2 * n_rows, dtype=jnp.int32) // 2
    buffer_rows = n_expert * capacity
    picked = jnp.zeros((buffer_rows,), jnp.int32).at[slot_index].set(source_rows)
    filled = jnp.zeros((buffer_rows,), jnp.bool_).at[slot_index].set(True)
    slot_gates = jnp.zeros((buffer_rows,), jnp.float32).at[slot_index].set(flat_gates)
    send_rows = jnp.where(filled[:, None], tokens[picked], jnp.zeros((), tokens.dtype))
    send_grads = (out_scale * slot_gates[:, None] * grad_out[picked].astype(jnp.float32)).astype(
        jnp.bfloat16
    )
    up_full, down_full = (
        lax.all_gather(w_up, "dp", axis=1, tiled=True),
        lax.all_gather(w_down, "dp", axis=1, tiled=True),
    )
    up_weight = up_full[0]
    down_weight = down_full[0]
    recv_rows = lax.all_to_all(send_rows, "expert", split_axis=0, concat_axis=0, tiled=True)
    pre_act, hidden, expert_out = expert_forward(recv_rows, up_weight, down_weight)
    back_out = lax.all_to_all(expert_out, "expert", split_axis=0, concat_axis=0, tiled=True)
    recv_grads = lax.all_to_all(send_grads, "expert", split_axis=0, concat_axis=0, tiled=True)
    pre_grad, row_grad = expert_backward(recv_grads, pre_act, up_weight, down_weight)
    back_grad = lax.all_to_all(row_grad, "expert", split_axis=0, concat_axis=0, tiled=True)
    layer_output = combine_slots(back_out, slot_index, out_scale * flat_gates, n_rows)
    grad_tokens = combine_slots(back_grad, slot_index, jnp.ones_like(flat_gates), n_rows)
    rows_all, grads_all = (
        lax.all_to_all(recv_rows, "dp", split_axis=1, concat_axis=0, tiled=True),
        lax.all_to_all(recv_grads, "dp", split_axis=1, concat_axis=0, tiled=True),
    )
    up_sum = contract_rows(rows_all, lax.all_gather(pre_grad, "dp", axis=0, tiled=True))
    down_sum = contract_rows(grads_all, lax.all_gather(hidden, "dp", axis=0, tiled=True))
    grad_up = up_sum.astype(jnp.bfloat16)[None]
    grad_down = down_sum.astype(jnp.bfloat16)[None]
    return (layer_output, grad_tokens, grad_up, grad_down)


def solution(mesh):
    in_specs = (
        P(("dp", "expert"), None),
        P(("dp", "expert"), None),
        P(("dp", "expert"), None),
        P(("dp", "expert"), None),
        P("expert", "dp", None),
        P("expert", "dp", None),
    )
    out_specs = (
        P(("dp", "expert"), None),
        P(("dp", "expert"), None),
        P("expert", "dp", None),
        P("expert", "dp", None),
    )
    return jax.shard_map(local, mesh=mesh, in_specs=in_specs, out_specs=out_specs, check_vma=False)
```

profile of v0, /device:TPU:0, one launch (start us, length us, event | category | flops | bytes accessed | tf_op | source)
XLA Modules:
  0.0 459.5 jit_solution(5944173518729407429)
XLA Ops:
  12.3 4.4 gather_fusion
  22.9 7.5 %all-to-all-start = ((bf16[8,38,5120]{2,1,0:T(8,128)(2,1)}), bf16[8,38,5120]{2,1,0:T(8,128)(2,1)}, u32[]{:S(2)}, u32[]{:S(2)}) async-start(bf16[8,38,5120]{2,1,0:T(8,128)(2,1)} %broadcast_select_fusion), calls=%async_computation | async-start | bytes 6553600 | tf_op jit(solution)/shard_map/all_to_all | solution.py:72
  31.2 4.4 gather_fusion.2
  35.6 4.5 reshape.109
  41.9 5.4 %multiply_convert_fusion = bf16[8,38,5120]{2,1,0:T(8,128)(2,1)} fusion(f32[8,38,5120]{2,1,0:T(8,128)} %reshape.109, f32[8,38]{1,0:T(8,128)S(1)} %mul.117), kind=kLoop, calls=%fused_computation.17 | loop fusion | flops 3112960 | bytes 9340096 | tf_op jit(solution)/shard_map/convert_element_type | solution.py:63
  47.3 56.9 %all-to-all-done = bf16[8,38,5120]{2,1,0:T(8,128)(2,1)} async-done(((bf16[8,38,5120]{2,1,0:T(8,128)(2,1)}), bf16[8,38,5120]{2,1,0:T(8,128)(2,1)}, u32[]{:S(2)}, u32[]{:S(2)}) %all-to-all-start) | async-done | bytes 3112992 | tf_op jit(solution)/shard_map/all_to_all | solution.py:72
  104.2 3.7 all-to-all-start.2
  107.8 5.0 %all_to_all.66 = bf16[304,4,1280]{2,1,0:T(4,128)(2,1)} reshape(bf16[8,38,5120]{2,1,0:T(8,128)(2,1)} %all-to-all-done) | data formatting | bytes 6225920 | tf_op jit(solution)/shard_map/all_to_all | solution.py:81
  112.8 4.0 copy.23
  116.8 64.7 %all-to-all-done.2 = bf16[8,38,5120]{2,1,0:T(8,128)(2,1)S(1)} async-done(((bf16[8,38,5120]{2,1,0:T(8,128)(2,1)}), bf16[8,38,5120]{2,1,0:T(8,128)(2,1)S(1)}, u32[]{:S(2)}, u32[]{:S(2)}) %all-to-all-start.2) | async-done | bytes 3112992 | tf_op jit(solution)/shard_map/all_to_all | solution.py:75
  181.5 4.8 %all-to-all-start.4 = ((bf16[304,4,1280]{2,0,1:T(8,128)(2,1)}), bf16[304,4,1280]{2,0,1:T(8,128)(2,1)}, u32[]{:S(2)}, u32[]{:S(2)}) async-start(bf16[304,4,1280]{2,0,1:T(8,128)(2,1)} %copy.23), calls=%async_computation.4 | async-start | bytes 6225920 | tf_op jit(solution)/shard_map/all_to_all | solution.py:81
  189.4 3.9 copy.24
  199.1 23.9 %all-to-all-done.4 = bf16[304,4,1280]{2,0,1:T(8,128)(2,1)} async-done(((bf16[304,4,1280]{2,0,1:T(8,128)(2,1)}), bf16[304,4,1280]{2,0,1:T(8,128)(2,1)}, u32[]{:S(2)}, u32[]{:S(2)}) %all-to-all-start.4) | async-done | bytes 3112992 | tf_op jit(solution)/shard_map/all_to_all | solution.py:81
  223.0 3.7 all-to-all-start.5
  226.7 7.9 %multiply_convert_fusion.1 = (bf16[304,768]{1,0:T(8,128)(2,1)}, f32[304,768]{1,0:T(8,128)}) fusion(bf16[304,5120]{1,0:T(8,128)(2,1)} %all_to_all.57, bf16[1,5120,768]{2,1,0:T(8,128)(2,1)} %all-gather.5.cloned.1.call-done), kind=kOutput, calls=%fused_computation.33 | convolution fusion | flops 2392854528 | bytes 12378112 | tf_op jit(solution)/shard_map/dot_general | solution.py:28
  234.6 7.9 %fusion.22 = bf16[304,768]{1,0:T(8,128)(2,1)} fusion(f32[304,768]{1,0:T(8,128)} %get-tuple-element.7, bf16[304,5120]{1,0:T(8,128)(2,1)} %all_to_all.62, bf16[1,5120,768]{2,1,0:T(8,128)(2,1)} %all-gather.7.cloned.1.call-done), kind=kOutput, calls=%fused_computation.32 | convolution fusion | flops 2395422720 | bytes 12378112 | tf_op jit(solution)/shard_map/dot_general | solution.py:35
  242.5 7.7 %fusion.8 = bf16[304,5120]{1,0:T(8,128)(2,1)} fusion(bf16[304,768]{1,0:T(8,128)(2,1)} %fusion.22, bf16[1,5120,768]{2,1,0:T(8,128)(2,1)} %all-gather.5.cloned.1.call-done), kind=kOutput, calls=%fused_computation.15 | convolution fusion | flops 2392309760 | bytes 11444224 | tf_op jit(solution)/shard_map/dot_general | solution.py:22
  250.2 3.6 all_to_all.63
  253.8 9.4 %all-to-all-done.5 = bf16[304,4,1280]{2,0,1:T(8,128)(2,1)S(1)} async-done(((bf16[304,4,1280]{2,0,1:T(8,128)(2,1)}), bf16[304,4,1280]{2,0,1:T(8,128)(2,1)S(1)}, u32[]{:S(2)}, u32[]{:S(2)}) %all-to-all-start.5) | async-done | bytes 3112992 | tf_op jit(solution)/shard_map/all_to_all | solution.py:82
  265.0 3.7 all-to-all-start.3
  269.4 7.7 %fusion.11 = bf16[304,5120]{1,0:T(8,128)(2,1)} fusion(bf16[304,768]{1,0:T(8,128)(2,1)} %get-tuple-element.6, bf16[1,5120,768]{2,1,0:T(8,128)(2,1)} %all-gather.7.cloned.1.call-done), kind=kOutput, calls=%fused_computation.16 | convolution fusion | flops 2392309760 | bytes 11444224 | tf_op jit(solution)/shard_map/dot_general | solution.py:22
  277.0 3.7 all_to_all.58
  280.7 61.4 %all-to-all-done.3 = bf16[8,38,5120]{2,1,0:T(8,128)(2,1)S(1)} async-done(((bf16[8,38,5120]{2,1,0:T(8,128)(2,1)}), bf16[8,38,5120]{2,1,0:T(8,128)(2,1)S(1)}, u32[]{:S(2)}, u32[]{:S(2)}) %all-to-all-start.3) | async-done | bytes 3112992 | tf_op jit(solution)/shard_map/all_to_all | solution.py:77
  342.1 4.5 all-to-all-start.1
  347.3 6.5 %fusion.14 = bf16[1,1280,768]{2,1,0:T(8,128)(2,1)} fusion(bf16[1216,1280]{1,0:T(8,128)(2,1)} %bitcast.7, bf16[1216,768]{1,0:T(8,128)(2,1)} %all-gather.9.cloned.1.call-done), kind=kOutput, calls=%fused_computation.22 | convolution fusion | flops 2391736320 | bytes 6946816 | tf_op jit(solution)/shard_map/dot_general | solution.py:16
  353.8 17.2 %all-gather.11.cloned.1.call-done = bf16[1216,768]{1,0:T(8,128)(2,1)} async-done(((bf16[304,768]{1,0:T(8,128)(2,1)}), bf16[1216,768]{1,0:T(8,128)(2,1)}) %all-gather.11.cloned.1.call-update) | async-done | bytes 1867792 | tf_op jit(solution)/shard_map/all_gather | solution.py:85
  371.1 6.5 %fusion.15 = bf16[1,1280,768]{2,1,0:T(8,128)(2,1)} fusion(bf16[1216,1280]{1,0:T(8,128)(2,1)} %bitcast.46, bf16[1216,768]{1,0:T(8,128)(2,1)} %all-gather.11.cloned.1.call-done), kind=kOutput, calls=%fused_computation.23 | convolution fusion | flops 2391736320 | bytes 6946816 | tf_op jit(solution)/shard_map/dot_general | solution.py:16
  383.5 6.3 %gather.21 = bf16[128,2,5120]{2,1,0:T(2,128)(2,1)} reshape(bf16[256,5120]{1,0:T(8,128)(2,1)} %gather_fusion.3) | data formatting | bytes 5242880 | tf_op jit(solution)/shard_map/gather | solution.py:42
  389.8 29.8 %all-to-all-done.1 = bf16[8,38,5120]{2,1,0:T(8,128)(2,1)} async-done(((bf16[8,38,5120]{2,1,0:T(8,128)(2,1)}), bf16[8,38,5120]{2,1,0:T(8,128)(2,1)}, u32[]{:S(2)}, u32[]{:S(2)}) %all-to-all-start.1) | async-done | bytes 3112992 | tf_op jit(solution)/shard_map/all_to_all | solution.py:74
  425.5 6.8 %reshape.108 = f32[128,2,5120]{2,1,0:T(2,128)} reshape(bf16[256,5120]{1,0:T(8,128)(2,1)} %gather_fusion.1) | data formatting | bytes 7864320 | tf_op jit(solution)/shard_map/convert_element_type | solution.py:42
  432.3 9.3 %reduce_sum.45 = bf16[128,5120]{1,0:T(8,128)(2,1)} reduce(bf16[128,2,5120]{2,1,0:T(2,128)(2,1)} %gather.21, bf16[]{:T(256)} %constant.45.clone.1), dimensions={1}, to_apply=%region_8.9 | reduce | flops 655360 | bytes 3932162 | tf_op jit(solution)/shard_map/reduce_sum | solution.py:43
  441.6 11.2 %multiply_reduce_fusion = bf16[128,5120]{1,0:T(8,128)(2,1)} fusion(f32[128,2,5120]{2,1,0:T(2,128)} %reshape.108, f32[128,2]{1,0:T(8,128)S(1)} %copy.21), kind=kLoop, calls=%fused_computation.18 | loop fusion | flops 1966080 | bytes 6554624 | tf_op jit(solution)/shard_map/reduce_sum | solution.py:43
  (61 shorter events, 37.6 us)
Async XLA Ops:
  7.2 5.2 %copy-start = (bf16[128,5120]{1,0:T(8,128)(2,1)S(1)}, bf16[128,5120]{1,0:T(8,128)(2,1)}, u32[]{:S(2)}) copy-start(bf16[128,5120]{1,0:T(8,128)(2,1)} %param.6) | copy-start | bytes 3932164
  7.2 219.5 %all-gather.5.cloned.1.call-start = ((), (), s32[]{:S(2)}) async-start(), calls=%async_computation.6 | async-start | bytes 9830400 | tf_op jit(solution)/shard_map/all_gather | solution.py:67
  22.9 8.3 %copy-start.2 = (bf16[128,5120]{1,0:T(8,128)(2,1)S(1)}, bf16[128,5120]{1,0:T(8,128)(2,1)}, u32[]{:S(2)}) copy-start(bf16[128,5120]{1,0:T(8,128)(2,1)} %param.7) | copy-start | bytes 3932164
  22.9 81.3 %all-to-all-start = ((bf16[8,38,5120]{2,1,0:T(8,128)(2,1)}), bf16[8,38,5120]{2,1,0:T(8,128)(2,1)}, u32[]{:S(2)}, u32[]{:S(2)}) async-start(bf16[8,38,5120]{2,1,0:T(8,128)(2,1)} %broadcast_select_fusion), calls=%async_computation | async-start | bytes 6553600 | tf_op jit(solution)/shard_map/all_to_all | solution.py:72
  30.4 204.1 %all-gather.7.cloned.1.call-start = ((), (), s32[]{:S(2)}) async-start(), calls=%async_computation.7 | async-start | bytes 9830400 | tf_op jit(solution)/shard_map/all_gather | solution.py:68
  35.6 4.5 copy-start.5
  104.2 77.3 %all-to-all-start.2 = ((bf16[8,38,5120]{2,1,0:T(8,128)(2,1)}), bf16[8,38,5120]{2,1,0:T(8,128)(2,1)S(1)}, u32[]{:S(2)}, u32[]{:S(2)}) async-start(bf16[8,38,5120]{2,1,0:T(8,128)(2,1)} %multiply_convert_fusion), calls=%async_computation.2 | async-start | bytes 6553600 | tf_op jit(solution)/shard_map/all_to_all | solution.py:75
  181.5 41.5 %all-to-all-start.4 = ((bf16[304,4,1280]{2,0,1:T(8,128)(2,1)}), bf16[304,4,1280]{2,0,1:T(8,128)(2,1)}, u32[]{:S(2)}, u32[]{:S(2)}) async-start(bf16[304,4,1280]{2,0,1:T(8,128)(2,1)} %copy.23), calls=%async_computation.4 | async-start | bytes 6225920 | tf_op jit(solution)/shard_map/all_to_all | solution.py:81
  223.0 40.3 %all-to-all-start.5 = ((bf16[304,4,1280]{2,0,1:T(8,128)(2,1)}), bf16[304,4,1280]{2,0,1:T(8,128)(2,1)S(1)}, u32[]{:S(2)}, u32[]{:S(2)}) async-start(bf16[304,4,1280]{2,0,1:T(8,128)(2,1)} %copy.24), calls=%async_computation.5 | async-start | bytes 6225920 | tf_op jit(solution)/shard_map/all_to_all | solution.py:82
  263.2 1.7 copy-start.4
  265.0 77.2 %all-to-all-start.3 = ((bf16[8,38,5120]{2,1,0:T(8,128)(2,1)}), bf16[8,38,5120]{2,1,0:T(8,128)(2,1)S(1)}, u32[]{:S(2)}, u32[]{:S(2)}) async-start(bf16[8,38,5120]{2,1,0:T(8,128)(2,1)} %all_to_all.63), calls=%async_computation.3 | async-start | bytes 6553600 | tf_op jit(solution)/shard_map/all_to_all | solution.py:77
  268.6 78.7 %all-gather.9.cloned.1.call-start = ((), (), s32[]{:S(2)}) async-start(), calls=%async_computation.8 | async-start | bytes 2334720 | tf_op jit(solution)/shard_map/all_gather | solution.py:84
  342.1 11.7 %copy-start.3 = (bf16[8,38,5120]{2,1,0:T(8,128)(2,1)}, bf16[8,38,5120]{2,1,0:T(8,128)(2,1)S(1)}, u32[]{:S(2)}) copy-start(bf16[8,38,5120]{2,1,0:T(8,128)(2,1)S(1)} %all-to-all-done.3) | copy-start | bytes 9338884
  342.1 77.4 %all-to-all-start.1 = ((bf16[8,38,5120]{2,1,0:T(8,128)(2,1)}), bf16[8,38,5120]{2,1,0:T(8,128)(2,1)}, u32[]{:S(2)}, u32[]{:S(2)}) async-start(bf16[8,38,5120]{2,1,0:T(8,128)(2,1)} %all_to_all.58), calls=%async_computation.1 | async-start | bytes 6553600 | tf_op jit(solution)/shard_map/all_to_all | solution.py:74
  346.6 24.5 %all-gather.11.cloned.1.call-start = ((), (), s32[]{:S(2)}) async-start(), calls=%async_computation.9 | async-start | bytes 2334720 | tf_op jit(solution)/shard_map/all_gather | solution.py:85
  432.3 20.5 %copy-start.1 = (bf16[128,5120]{1,0:T(8,128)(2,1)S(1)}, bf16[128,5120]{1,0:T(8,128)(2,1)}, u32[]{:S(2)}) copy-start(bf16[128,5120]{1,0:T(8,128)(2,1)} %param.6) | copy-start | bytes 3932164
Sparse Core Ops, SparseCore 0:
  9.6 58.0 all-gather.4
  69.2 55.3 all-gather.6
  271.6 21.7 all-gather.8
  349.3 21.7 all-gather.10
where the time goes:
time: 468 us; the launch traced here: 460 us
  waiting for transfers between devices  266 us (57%)
  local copies, waits for them, and re-layouts  77.9 us (17%)
  matrix products  44.2 us (9%)
  other arithmetic  29.4 us (6%)
  starting transfers between devices  28.4 us (6%)
  between operations  14.2 us (3%)
    all_to_all x1, waiting for transfers between devices, local(): lax.all_to_all(send_grads, 'expert', split_axis=0, concat_axis=0, tiled=T...  64.7 us
    all_to_all x1, waiting for transfers between devices, local(): lax.all_to_all(row_grad, 'expert', split_axis=0, concat_axis=0, tiled=True)  61.4 us
    all_to_all x1, waiting for transfers between devices, local(): lax.all_to_all(send_rows, 'expert', split_axis=0, concat_axis=0, tiled=True)  56.9 us
    all_to_all x1, waiting for transfers between devices, local(): lax.all_to_all(expert_out, 'expert', split_axis=0, concat_axis=0, tiled=T...  29.8 us
    all_to_all x1, waiting for transfers between devices, local(): lax.all_to_all(recv_rows, 'dp', split_axis=1, concat_axis=0, tiled=True)  23.9 us
    reduce_sum x2, other arithmetic, combine_slots(): jnp.sum(picked_rows.reshape(n_rows, 2, returned.shape[1]), axis=1)  20.5 us
    all_gather x1, waiting for transfers between devices, local(): lax.all_gather(hidden, 'dp', axis=0, tiled=True)  17.2 us
    dot_general x2, matrix products, contract_columns(): lax.dot_general(former, latter, (((1,), (1,)), ((), ())), preferred_eleme...  15.3 us
  transfers between devices with their start and end apart: 10, of which 7 were waited for; matrix products, arithmetic and copies ran while one was open for 20% of the time, Pallas kernels for 0%

commit v1 on v0

v1 whole, which is shorter than its diff:
```python
import math

import jax
import jax.numpy as jnp
from jax import lax
from jax.sharding import PartitionSpec as P

LAYERS = 40
ROW_TILE = 8


def activate(values):
    return jax.nn.gelu(values, approximate=True)


def contract_rows(former, latter):
    return lax.dot_general(
        former, latter, (((0,), (0,)), ((), ())), preferred_element_type=jnp.float32
    )


def contract_columns(former, latter):
    return lax.dot_general(
        former, latter, (((1,), (1,)), ((), ())), preferred_element_type=jnp.float32
    )


def permute_xor(values, axis, mask):
    size = lax.axis_size(axis)
    return lax.ppermute(values, axis, [(i, i ^ mask) for i in range(size)])


def plan_slots(routing, experts, block):
    n_rows = routing.shape[0]
    ids = routing[:, :2]
    codes = routing[:, 2:].astype(jnp.float32)
    gates = codes / jnp.sum(codes, axis=1, keepdims=True)
    match = ids[:, :, None] == experts[None, None, :]
    named = jnp.any(match, axis=1)
    order = jnp.arange(n_rows, dtype=jnp.int32)
    earlier = (order[None, :] < order[:, None]).astype(jnp.bfloat16)
    before = jnp.dot(earlier, named.astype(jnp.bfloat16), preferred_element_type=jnp.float32)
    place = before.astype(jnp.int32)[:, :, None] == jnp.arange(block, dtype=jnp.int32)
    picks = [
        (match[:, k, :, None] & place).reshape(n_rows, experts.shape[0] * block) for k in (0, 1)
    ]
    either = (picks[0] | picks[1]).astype(jnp.bfloat16)
    slot_gates = jnp.sum(
        jnp.where(picks[0], gates[:, :1], 0.0) + jnp.where(picks[1], gates[:, 1:], 0.0), axis=0
    )
    return [pick.astype(jnp.bfloat16) for pick in picks], either, gates, slot_gates


def exchange(blocks, n_group, block):
    parts = [blocks[:block]]
    for k in range(1, n_group):
        parts.append(permute_xor(blocks[k * block : (k + 1) * block], "expert", k))
    return jnp.concatenate(parts, axis=0)


def spread_columns(rows):
    n_dp = lax.axis_size("dp")
    me = lax.axis_index("dp")
    width = rows.shape[1] // n_dp
    parts = []
    for k in range(n_dp):
        piece = lax.dynamic_slice(rows, (0, (me ^ k) * width), (rows.shape[0], width))
        parts.append(permute_xor(piece, "dp", k) if k else piece)
    return jnp.concatenate(parts, axis=0)


def gather_rows(rows):
    n_dp = lax.axis_size("dp")
    return jnp.concatenate(
        [rows] + [permute_xor(rows, "dp", k) for k in range(1, n_dp)], axis=0
    )


def local(tokens, grad_out, expert_ids, gate_codes, w_up, w_down):
    n_expert = lax.axis_size("expert")
    n_rows = tokens.shape[0]
    capacity = max(2, 12 * n_rows // (5 * n_expert))
    block = -(-capacity // ROW_TILE) * ROW_TILE
    half = n_expert // 2
    out_scale = 1.0 / math.sqrt(2.0 * LAYERS)
    me = lax.axis_index("expert")
    experts = me ^ jnp.arange(half, dtype=jnp.int32)

    routing = jnp.concatenate([expert_ids, gate_codes], axis=1)
    far_routing = permute_xor(routing, "expert", half)
    far_tokens = permute_xor(tokens, "expert", half)
    far_grads = permute_xor(grad_out, "expert", half)
    up_weight = lax.all_gather(w_up, "dp", axis=1, tiled=True)[0]
    down_weight = lax.all_gather(w_down, "dp", axis=1, tiled=True)[0]

    plans = [plan_slots(routing, experts, block), plan_slots(far_routing, experts, block)]

    def dispatch_rows(plan, rows):
        return exchange(contract_rows(plan[1], rows).astype(jnp.bfloat16), half, block)

    def dispatch_grads(plan, grads):
        picked = contract_rows(plan[1], grads)
        scaled = (out_scale * plan[3])[:, None] * picked
        return exchange(scaled.astype(jnp.bfloat16), half, block)

    def combine_out(plan, back):
        first, second = (
            jnp.dot(pick, back, preferred_element_type=jnp.float32) for pick in plan[0]
        )
        weights = out_scale * plan[2]
        return weights[:, :1] * first + weights[:, 1:] * second

    def combine_grad(plan, back):
        return jnp.dot(plan[1], back, preferred_element_type=jnp.float32)

    rows, grads, hiddens, pre_grads, outs, row_grads = [], [], [], [], [], []
    for plan, token_rows, cotangents in zip(plans, (tokens, far_tokens), (grad_out, far_grads)):
        recv_rows = dispatch_rows(plan, token_rows)
        recv_grads = dispatch_grads(plan, cotangents)
        pre_act = jnp.dot(recv_rows, up_weight, preferred_element_type=jnp.float32)
        hidden = activate(pre_act).astype(jnp.bfloat16)
        expert_out = contract_columns(hidden, down_weight).astype(jnp.bfloat16)
        outs.append(exchange(expert_out, half, block))
        hidden_grad = jnp.dot(recv_grads, down_weight, preferred_element_type=jnp.float32)
        pre_grad = jax.vjp(activate, pre_act)[1](hidden_grad)[0].astype(jnp.bfloat16)
        row_grad = contract_columns(pre_grad, up_weight).astype(jnp.bfloat16)
        row_grads.append(exchange(row_grad, half, block))
        rows.append(recv_rows)
        grads.append(recv_grads)
        hiddens.append(hidden)
        pre_grads.append(pre_grad)

    far_out = permute_xor(combine_out(plans[1], outs[1]).astype(jnp.bfloat16), "expert", half)
    layer_output = (combine_out(plans[0], outs[0]) + far_out.astype(jnp.float32)).astype(
        jnp.bfloat16
    )
    far_grad = permute_xor(
        combine_grad(plans[1], row_grads[1]).astype(jnp.bfloat16), "expert", half
    )
    grad_tokens = (combine_grad(plans[0], row_grads[0]) + far_grad.astype(jnp.float32)).astype(
        jnp.bfloat16
    )

    join = lambda parts: jnp.concatenate(parts, axis=0)
    up_sum = contract_rows(spread_columns(join(rows)), gather_rows(join(pre_grads)))
    down_sum = contract_rows(spread_columns(join(grads)), gather_rows(join(hiddens)))
    grad_up = up_sum.astype(jnp.bfloat16)[None]
    grad_down = down_sum.astype(jnp.bfloat16)[None]
    return (layer_output, grad_tokens, grad_up, grad_down)


def solution(mesh):
    in_specs = (
        P(("dp", "expert"), None),
        P(("dp", "expert"), None),
        P(("dp", "expert"), None),
        P(("dp", "expert"), None),
        P("expert", "dp", None),
        P("expert", "dp", None),
    )
    out_specs = (
        P(("dp", "expert"), None),
        P(("dp", "expert"), None),
        P("expert", "dp", None),
        P("expert", "dp", None),
    )
    return jax.shard_map(local, mesh=mesh, in_specs=in_specs, out_specs=out_specs, check_vma=False)
```

time: 468 us -> 452 us (0.966); the launches traced: 460 us -> 452 us
  local copies, waits for them, and re-layouts: 77.9 us -> 19.8 us
  waiting for transfers between devices: 266 us -> 317 us
  other arithmetic: 29.4 us -> 1.99 us
  starting transfers between devices: 28.4 us -> 46.4 us
  matrix products: 44.2 us -> 51.6 us
    ppermute x0 -> x41, waiting for transfers between devices: none -> 317 us  [permute_xor(): return lax.ppermute(values, axis, [(i, i ^ mask) for i in range(size)])]
    all_to_all x6 -> x0, waiting for transfers between devices: 246 us -> none  [the longest x1 64.7 us: local(): lax.all_to_all(send_grads, 'expert', split_axis=0, concat_axis=0, tiled=T...]
    ppermute x0 -> x41, starting transfers between devices: none -> 46.3 us  [permute_xor(): return lax.ppermute(values, axis, [(i, i ^ mask) for i in range(size)])]
    all_to_all x10 -> x0, local copies, waits for them, and re-layouts: 33.8 us -> none  [the longest x2 8.99 us: local(): lax.all_to_all(recv_rows, 'dp', split_axis=1, concat_axis=0, tiled=True)]
    all_to_all x6 -> x0, starting transfers between devices: 27.8 us -> none  [the longest x1 7.53 us: local(): lax.all_to_all(send_rows, 'expert', split_axis=0, concat_axis=0, tiled=True)]
    gather x6 -> x0, local copies, waits for them, and re-layouts: 24.7 us -> none  [the longest x3 13.4 us: combine_slots(): picked_rows = returned[slot_index].astype(jnp.float32) * weights[:, None]]
    reduce_sum x4, other arithmetic: 20.6 us -> 0.27 us  [the longest x2 0.23 us: plan_slots(): jnp.sum(jnp.where(picks[0], gates[:, :1], 0.0) + jnp.where(picks[1], gate...]
    all_gather x4 -> x2, waiting for transfers between devices: 17.3 us -> 0.01 us  [the longest x1 0.01 us: local(): up_weight = lax.all_gather(w_up, 'dp', axis=1, tiled=True)[0]]
  transfers between devices with their start and end apart: 10 -> 43, of which waited for: 7 -> 21; matrix products, arithmetic and copies ran while one was open for 20% -> 12% of each run, Pallas kernels for 0% -> 0%
where the time goes in v1:
time: 452 us
  waiting for transfers between devices  317 us (70%)
  matrix products  51.6 us (11%)
  starting transfers between devices  46.4 us (10%)
  local copies, waits for them, and re-layouts  19.8 us (4%)
  between operations  14.7 us (3%)
    ppermute x41, waiting for transfers between devices, permute_xor(): return lax.ppermute(values, axis, [(i, i ^ mask) for i in range(size)])  317 us
    ppermute x41, starting transfers between devices, permute_xor(): return lax.ppermute(values, axis, [(i, i ^ mask) for i in range(size)])  46.3 us
    dot_general x6, matrix products, contract_rows(): lax.dot_general(former, latter, (((0,), (0,)), ((), ())), preferred_eleme...  14.8 us
    unnamed x104, local copies, waits for them, and re-layouts  14.6 us
    dot_general x4, matrix products, contract_columns(): lax.dot_general(former, latter, (((1,), (1,)), ((), ())), preferred_eleme...  14.2 us
  transfers between devices with their start and end apart: 43, of which 21 were waited for; matrix products, arithmetic and copies ran while one was open for 12% of the time, Pallas kernels for 0%

profile of v1, /device:TPU:0, one launch (start us, length us, event | category | flops | bytes accessed | tf_op | source)
XLA Modules:
  0.0 451.7 jit_solution(18384266885553211402)
XLA Ops:
  8.7 4.0 collective-permute-start.6
  12.8 2.9 collective-permute-start.7
  25.5 6.1 %collective-permute-done.15 = bf16[40,5120]{1,0:T(8,128)(2,1)} collective-permute-done((bf16[40,5120]{1,0:T(8,128)(2,1)}, bf16[40,5120]{1,0:T(8,128)(2,1)}, u32[]{:S(2)}, u32[]{:S(2)}) %collective-permute-start.15) | collective-permute-done | bytes 409632 | tf_op jit(solution)/shard_map/ppermute | solution.py:30
  34.2 45.1 %collective-permute-done.16 = bf16[40,5120]{1,0:T(8,128)(2,1)} collective-permute-done((bf16[40,5120]{1,0:T(8,128)(2,1)}, bf16[40,5120]{1,0:T(8,128)(2,1)}, u32[]{:S(2)}, u32[]{:S(2)}) %collective-permute-start.16) | collective-permute-done | bytes 409632 | tf_op jit(solution)/shard_map/ppermute | solution.py:30
  79.2 2.5 collective-permute-start.1
  82.7 5.3 %collective-permute-done.17 = bf16[40,5120]{1,0:T(8,128)(2,1)} collective-permute-done((bf16[40,5120]{1,0:T(8,128)(2,1)}, bf16[40,5120]{1,0:T(8,128)(2,1)}, u32[]{:S(2)}, u32[]{:S(2)}) %collective-permute-start.17) | collective-permute-done | bytes 409632 | tf_op jit(solution)/shard_map/ppermute | solution.py:30
  88.0 3.4 collective-permute-start.2
  93.3 44.0 %collective-permute-done.1 = bf16[40,5120]{1,0:T(8,128)(2,1)S(1)} collective-permute-done((bf16[40,5120]{1,0:T(8,128)(2,1)}, bf16[40,5120]{1,0:T(8,128)(2,1)S(1)}, u32[]{:S(2)}, u32[]{:S(2)}) %collective-permute-start.1) | collective-permute-done | bytes 409632 | tf_op jit(solution)/shard_map/ppermute | solution.py:30
  138.1 8.7 %collective-permute-done.2 = bf16[40,5120]{1,0:T(8,128)(2,1)S(1)} collective-permute-done((bf16[40,5120]{1,0:T(8,128)(2,1)}, bf16[40,5120]{1,0:T(8,128)(2,1)S(1)}, u32[]{:S(2)}, u32[]{:S(2)}) %collective-permute-start.2) | collective-permute-done | bytes 409632 | tf_op jit(solution)/shard_map/ppermute | solution.py:30
  151.1 3.0 collective-permute-start.24
  158.4 5.6 %collective-permute-done.22 = bf16[40,5120]{1,0:T(8,128)(2,1)S(1)} collective-permute-done((bf16[40,5120]{1,0:T(8,128)(2,1)S(1)}, bf16[40,5120]{1,0:T(8,128)(2,1)S(1)}, u32[]{:S(2)}, u32[]{:S(2)}) %collective-permute-start.22) | collective-permute-done | bytes 409632 | tf_op jit(solution)/shard_map/ppermute | solution.py:30
  164.0 9.3 %collective-permute-done.24 = bf16[40,5120]{1,0:T(8,128)(2,1)S(1)} collective-permute-done((bf16[40,5120]{1,0:T(8,128)(2,1)S(1)}, bf16[40,5120]{1,0:T(8,128)(2,1)S(1)}, u32[]{:S(2)}, u32[]{:S(2)}) %collective-permute-start.24) | collective-permute-done | bytes 409632 | tf_op jit(solution)/shard_map/ppermute | solution.py:30
  173.3 15.0 %collective-permute-done.8 = bf16[40,5120]{1,0:T(8,128)(2,1)S(1)} collective-permute-done((bf16[40,5120]{1,0:T(8,128)(2,1)S(1)}, bf16[40,5120]{1,0:T(8,128)(2,1)S(1)}, u32[]{:S(2)}, u32[]{:S(2)}) %collective-permute-start.8) | collective-permute-done | bytes 409632 | tf_op jit(solution)/shard_map/ppermute | solution.py:30
  193.7 5.9 %constant_dynamic-update-slice_fusion.25 = (bf16[1280,768]{1,0:T(8,128)(2,1)}, bf16[160,768]{1,0:T(8,128)(2,1)S(1)}, f32[160,768]{1,0:T(8,128)}) fusion(bf16[1,5120,768]{2,1,0:T(8,128)(2,1)} %all-gather.3.cloned.1.call-done, bf16[40,5120]{1,0:T(8,128)(2,1)} %copy-done.17, bf16[40,5120]{1,0:T(8,128)(2,1)} %copy-done.16, ...), kind=kOutput, calls=%fused_computation.164 | convolution fusion | flops 1265950720 | bytes 10485760 | tf_op jit(solution)/shard_map/dot_general | solution.py:120
  202.2 6.1 %constant_dynamic-update-slice_fusion.12 = (bf16[1280,768]{1,0:T(8,128)(2,1)}, bf16[160,768]{1,0:T(8,128)(2,1)S(1)}) fusion(f32[160,768]{1,0:T(8,128)} %get-tuple-element.83, bf16[1,5120,768]{2,1,0:T(8,128)(2,1)} %all-gather.5.cloned.1.call-done, bf16[40,5120]{1,0:T(8,128)(2,1)} %collective-permute-done.17, bf16[40,5120]{1,0:T(8,128)(2,1)} %collective-permute-done.16, ...), kind=kOutput, calls=%fused_computation.151 | convolution fusion | flops 1267302400 | bytes 10485760 | tf_op jit(solution)/shard_map/dot_general | solution.py:124
  211.0 6.1 %fusion.22 = bf16[160,5120]{1,0:T(8,128)(2,1)S(1)} fusion(bf16[160,768]{1,0:T(8,128)(2,1)S(1)} %get-tuple-element.88, bf16[1,5120,768]{2,1,0:T(8,128)(2,1)} %all-gather.3.cloned.1.call-done), kind=kOutput, calls=%fused_computation.27 | convolution fusion | flops 1259110400 | bytes 9748480 | tf_op jit(solution)/shard_map/dot_general | solution.py:23
  218.6 2.7 fusion.19
  221.5 2.7 fusion.28
  227.8 2.7 fusion.25
  234.0 22.0 %collective-permute-done.11 = bf16[40,5120]{1,0:T(8,128)(2,1)S(1)} collective-permute-done((bf16[40,5120]{1,0:T(8,128)(2,1)S(1)}, bf16[40,5120]{1,0:T(8,128)(2,1)S(1)}, u32[]{:S(2)}, u32[]{:S(2)}) %collective-permute-start.11) | collective-permute-done | bytes 409632 | tf_op jit(solution)/shard_map/ppermute | solution.py:30
  260.6 2.4 collective-permute-done.3
  263.7 4.5 %collective-permute-done.4 = bf16[40,5120]{1,0:T(8,128)(2,1)S(1)} collective-permute-done((bf16[40,5120]{1,0:T(8,128)(2,1)S(1)}, bf16[40,5120]{1,0:T(8,128)(2,1)S(1)}, u32[]{:S(2)}, u32[]{:S(2)}) %collective-permute-start.4) | collective-permute-done | bytes 409632 | tf_op jit(solution)/shard_map/ppermute | solution.py:30
  268.3 8.8 %collective-permute-done.5 = bf16[40,5120]{1,0:T(8,128)(2,1)S(1)} collective-permute-done((bf16[40,5120]{1,0:T(8,128)(2,1)S(1)}, bf16[40,5120]{1,0:T(8,128)(2,1)S(1)}, u32[]{:S(2)}, u32[]{:S(2)}) %collective-permute-start.5) | collective-permute-done | bytes 409632 | tf_op jit(solution)/shard_map/ppermute | solution.py:30
  279.8 2.9 collective-permute-done.40
  287.8 13.4 %collective-permute-done.36 = bf16[320,1280]{1,0:T(8,128)(2,1)S(1)} collective-permute-done((bf16[320,1280]{1,0:T(8,128)(2,1)S(1)}, bf16[320,1280]{1,0:T(8,128)(2,1)S(1)}, u32[]{:S(2)}, u32[]{:S(2)}) %collective-permute-start.36) | collective-permute-done | bytes 819232 | tf_op jit(solution)/shard_map/ppermute | solution.py:30
  302.8 15.1 %collective-permute-done.37 = bf16[320,1280]{1,0:T(8,128)(2,1)S(1)} collective-permute-done((bf16[320,1280]{1,0:T(8,128)(2,1)S(1)}, bf16[320,1280]{1,0:T(8,128)(2,1)S(1)}, u32[]{:S(2)}, u32[]{:S(2)}) %collective-permute-start.37) | collective-permute-done | bytes 819232 | tf_op jit(solution)/shard_map/ppermute | solution.py:30
  319.8 9.5 %collective-permute-done.33 = bf16[320,768]{1,0:T(8,128)(2,1)S(1)} collective-permute-done((bf16[320,768]{1,0:T(8,128)(2,1)S(1)}, bf16[320,768]{1,0:T(8,128)(2,1)S(1)}, u32[]{:S(2)}, u32[]{:S(2)}) %collective-permute-start.33) | collective-permute-done | bytes 491552 | tf_op jit(solution)/shard_map/ppermute | solution.py:30
  329.3 5.9 %fusion.53 = bf16[1,1280,768]{2,1,0:T(8,128)(2,1)} fusion(bf16[1280,768]{1,0:T(8,128)(2,1)} %constant_dynamic-update-slice_fusion.21, bf16[320,1280]{1,0:T(8,128)(2,1)S(1)} %collective-permute-done.37, bf16[320,1280]{1,0:T(8,128)(2,1)S(1)} %collective-permute-done.36, bf16[320,1280]{1,0:T(8,128)(2,1)S(1)} %collective-permute-done.35, ...), kind=kOutput, calls=%fused_computation.55 | convolution fusion | flops 2530672640 | bytes 7208960 | tf_op jit(solution)/shard_map/dot_general | solution.py:17
  335.3 37.8 %collective-permute-done.34 = bf16[320,768]{1,0:T(8,128)(2,1)S(1)} collective-permute-done((bf16[320,768]{1,0:T(8,128)(2,1)S(1)}, bf16[320,768]{1,0:T(8,128)(2,1)S(1)}, u32[]{:S(2)}, u32[]{:S(2)}) %collective-permute-start.34) | collective-permute-done | bytes 491552 | tf_op jit(solution)/shard_map/ppermute | solution.py:30
  376.7 4.0 fusion.50
  380.7 34.7 %collective-permute-done.14 = bf16[128,5120]{1,0:T(8,128)(2,1)S(1)} collective-permute-done((bf16[128,5120]{1,0:T(8,128)(2,1)S(1)}, bf16[128,5120]{1,0:T(8,128)(2,1)S(1)}, u32[]{:S(2)}, u32[]{:S(2)}) %collective-permute-start.14) | collective-permute-done | bytes 1310752 | tf_op jit(solution)/shard_map/ppermute | solution.py:30
  419.5 23.8 %collective-permute-done.28 = bf16[128,5120]{1,0:T(8,128)(2,1)S(1)} collective-permute-done((bf16[128,5120]{1,0:T(8,128)(2,1)S(1)}, bf16[128,5120]{1,0:T(8,128)(2,1)S(1)}, u32[]{:S(2)}, u32[]{:S(2)}) %collective-permute-start.28) | collective-permute-done | bytes 1310752 | tf_op jit(solution)/shard_map/ppermute | solution.py:30
  (217 shorter events, 71.4 us)
Async XLA Ops:
  7.2 186.4 %all-gather.3.cloned.1.call-start = ((), (), s32[]{:S(2)}) async-start(), calls=%async_computation | async-start | bytes 9830400 | tf_op jit(solution)/shard_map/all_gather | solution.py:93
  7.9 194.2 %all-gather.5.cloned.1.call-start = ((), (), s32[]{:S(2)}) async-start(), calls=%async_computation.1 | async-start | bytes 9830400 | tf_op jit(solution)/shard_map/all_gather | solution.py:94
  12.7 134.9 %collective-permute-start.21 = (bf16[128,5120]{1,0:T(8,128)(2,1)}, bf16[128,5120]{1,0:T(8,128)(2,1)}, u32[]{:S(2)}, u32[]{:S(2)}) collective-permute-start(bf16[128,5120]{1,0:T(8,128)(2,1)} %param.7), channel_id=1, source_target_pairs={{0,4},{1,5},{2,6},{3,7},{4,0},{5,1},{6,2},{7,3},{8,12},{9,13},{10,... | collective-permute-start | bytes 3932168 | tf_op jit(solution)/shard_map/ppermute | solution.py:30
  12.8 141.3 %collective-permute-start.7 = (bf16[128,5120]{1,0:T(8,128)(2,1)}, bf16[128,5120]{1,0:T(8,128)(2,1)}, u32[]{:S(2)}, u32[]{:S(2)}) collective-permute-start(bf16[128,5120]{1,0:T(8,128)(2,1)} %param.6), channel_id=1, source_target_pairs={{0,4},{1,5},{2,6},{3,7},{4,0},{5,1},{6,2},{7,3},{8,12},{9,13},{10,... | collective-permute-start | bytes 3932168 | tf_op jit(solution)/shard_map/ppermute | solution.py:30
  21.3 57.9 %collective-permute-start.16 = (bf16[40,5120]{1,0:T(8,128)(2,1)}, bf16[40,5120]{1,0:T(8,128)(2,1)}, u32[]{:S(2)}, u32[]{:S(2)}) collective-permute-start(bf16[40,5120]{1,0:T(8,128)(2,1)} %get-tuple-element.31), channel_id=1, source_target_pairs={{0,2},{1,3},{2,0},{3,1},{4,6},{5,7},{6,4},{7,5},{8,10},{9,11},{10,... | collective-permute-start | bytes 1228808 | tf_op jit(solution)/shard_map/ppermute | solution.py:30
  22.9 65.1 %collective-permute-start.17 = (bf16[40,5120]{1,0:T(8,128)(2,1)}, bf16[40,5120]{1,0:T(8,128)(2,1)}, u32[]{:S(2)}, u32[]{:S(2)}) collective-permute-start(bf16[40,5120]{1,0:T(8,128)(2,1)} %get-tuple-element.30), channel_id=1, source_target_pairs={{0,3},{1,2},{2,1},{3,0},{4,7},{5,6},{6,5},{7,4},{8,11},{9,10},{10,... | collective-permute-start | bytes 1228808 | tf_op jit(solution)/shard_map/ppermute | solution.py:30
  31.6 60.8 %collective-permute-start = (bf16[40,5120]{1,0:T(8,128)(2,1)}, bf16[40,5120]{1,0:T(8,128)(2,1)S(1)}, u32[]{:S(2)}, u32[]{:S(2)}) collective-permute-start(bf16[40,5120]{1,0:T(8,128)(2,1)} %get-tuple-element.42), channel_id=1, source_target_pairs={{0,1},{1,0},{2,3},{3,2},{4,5},{5,4},{6,7},{7,6},{8,9},{9,8},{10,11... | collective-permute-start | bytes 1228808 | tf_op jit(solution)/shard_map/ppermute | solution.py:30
  79.2 58.0 %collective-permute-start.1 = (bf16[40,5120]{1,0:T(8,128)(2,1)}, bf16[40,5120]{1,0:T(8,128)(2,1)S(1)}, u32[]{:S(2)}, u32[]{:S(2)}) collective-permute-start(bf16[40,5120]{1,0:T(8,128)(2,1)} %get-tuple-element.41), channel_id=1, source_target_pairs={{0,2},{1,3},{2,0},{3,1},{4,6},{5,7},{6,4},{7,5},{8,10},{9,11},{10,... | collective-permute-start | bytes 1228808 | tf_op jit(solution)/shard_map/ppermute | solution.py:30
  88.0 58.8 %collective-permute-start.2 = (bf16[40,5120]{1,0:T(8,128)(2,1)}, bf16[40,5120]{1,0:T(8,128)(2,1)S(1)}, u32[]{:S(2)}, u32[]{:S(2)}) collective-permute-start(bf16[40,5120]{1,0:T(8,128)(2,1)} %get-tuple-element.40), channel_id=1, source_target_pairs={{0,3},{1,2},{2,1},{3,0},{4,7},{5,6},{6,5},{7,4},{8,11},{9,10},{10,... | collective-permute-start | bytes 1228808 | tf_op jit(solution)/shard_map/ppermute | solution.py:30
  151.1 22.2 %collective-permute-start.24 = (bf16[40,5120]{1,0:T(8,128)(2,1)S(1)}, bf16[40,5120]{1,0:T(8,128)(2,1)S(1)}, u32[]{:S(2)}, u32[]{:S(2)}) collective-permute-start(bf16[40,5120]{1,0:T(8,128)(2,1)S(1)} %get-tuple-element.25), channel_id=1, source_target_pairs={{0,3},{1,2},{2,1},{3,0},{4,7},{5,6},{6,5},{7,4},{8,11},{9,10},{10,... | collective-permute-start | bytes 1228808 | tf_op jit(solution)/shard_map/ppermute | solution.py:30
  156.9 34.8 %collective-permute-start.10 = (bf16[40,5120]{1,0:T(8,128)(2,1)S(1)}, bf16[40,5120]{1,0:T(8,128)(2,1)S(1)}, u32[]{:S(2)}, u32[]{:S(2)}) collective-permute-start(bf16[40,5120]{1,0:T(8,128)(2,1)S(1)} %get-tuple-element.35), channel_id=1, source_target_pairs={{0,3},{1,2},{2,1},{3,0},{4,7},{5,6},{6,5},{7,4},{8,11},{9,10},{10,... | collective-permute-start | bytes 1228808 | tf_op jit(solution)/shard_map/ppermute | solution.py:30
  156.9 31.4 %collective-permute-start.8 = (bf16[40,5120]{1,0:T(8,128)(2,1)S(1)}, bf16[40,5120]{1,0:T(8,128)(2,1)S(1)}, u32[]{:S(2)}, u32[]{:S(2)}) collective-permute-start(bf16[40,5120]{1,0:T(8,128)(2,1)S(1)} %get-tuple-element.37), channel_id=1, source_target_pairs={{0,1},{1,0},{2,3},{3,2},{4,5},{5,4},{6,7},{7,6},{8,9},{9,8},{10,11... | collective-permute-start | bytes 1228808 | tf_op jit(solution)/shard_map/ppermute | solution.py:30
  164.0 24.7 %collective-permute-start.9 = (bf16[40,5120]{1,0:T(8,128)(2,1)S(1)}, bf16[40,5120]{1,0:T(8,128)(2,1)S(1)}, u32[]{:S(2)}, u32[]{:S(2)}) collective-permute-start(bf16[40,5120]{1,0:T(8,128)(2,1)S(1)} %get-tuple-element.36), channel_id=1, source_target_pairs={{0,2},{1,3},{2,0},{3,1},{4,6},{5,7},{6,4},{7,5},{8,10},{9,11},{10,... | collective-permute-start | bytes 1228808 | tf_op jit(solution)/shard_map/ppermute | solution.py:30
  224.3 31.7 %collective-permute-start.11 = (bf16[40,5120]{1,0:T(8,128)(2,1)S(1)}, bf16[40,5120]{1,0:T(8,128)(2,1)S(1)}, u32[]{:S(2)}, u32[]{:S(2)}) collective-permute-start(bf16[40,5120]{1,0:T(8,128)(2,1)S(1)} %get-tuple-element.55), channel_id=1, source_target_pairs={{0,1},{1,0},{2,3},{3,2},{4,5},{5,4},{6,7},{7,6},{8,9},{9,8},{10,11... | collective-permute-start | bytes 1228808 | tf_op jit(solution)/shard_map/ppermute | solution.py:30
  225.0 31.0 %collective-permute-start.12 = (bf16[40,5120]{1,0:T(8,128)(2,1)S(1)}, bf16[40,5120]{1,0:T(8,128)(2,1)S(1)}, u32[]{:S(2)}, u32[]{:S(2)}) collective-permute-start(bf16[40,5120]{1,0:T(8,128)(2,1)S(1)} %get-tuple-element.54), channel_id=1, source_target_pairs={{0,2},{1,3},{2,0},{3,1},{4,6},{5,7},{6,4},{7,5},{8,10},{9,11},{10,... | collective-permute-start | bytes 1228808 | tf_op jit(solution)/shard_map/ppermute | solution.py:30
  227.0 29.0 %collective-permute-start.13 = (bf16[40,5120]{1,0:T(8,128)(2,1)S(1)}, bf16[40,5120]{1,0:T(8,128)(2,1)S(1)}, u32[]{:S(2)}, u32[]{:S(2)}) collective-permute-start(bf16[40,5120]{1,0:T(8,128)(2,1)S(1)} %get-tuple-element.53), channel_id=1, source_target_pairs={{0,3},{1,2},{2,1},{3,0},{4,7},{5,6},{6,5},{7,4},{8,11},{9,10},{10,... | collective-permute-start | bytes 1228808 | tf_op jit(solution)/shard_map/ppermute | solution.py:30
  230.7 28.3 %collective-permute-start.27 = (bf16[40,5120]{1,0:T(8,128)(2,1)S(1)}, bf16[40,5120]{1,0:T(8,128)(2,1)S(1)}, u32[]{:S(2)}, u32[]{:S(2)}) collective-permute-start(bf16[40,5120]{1,0:T(8,128)(2,1)S(1)} %get-tuple-element.49), channel_id=1, source_target_pairs={{0,3},{1,2},{2,1},{3,0},{4,7},{5,6},{6,5},{7,4},{8,11},{9,10},{10,... | collective-permute-start | bytes 1228808 | tf_op jit(solution)/shard_map/ppermute | solution.py:30
  232.9 30.1 %collective-permute-start.3 = (bf16[40,5120]{1,0:T(8,128)(2,1)S(1)}, bf16[40,5120]{1,0:T(8,128)(2,1)S(1)}, u32[]{:S(2)}, u32[]{:S(2)}) collective-permute-start(bf16[40,5120]{1,0:T(8,128)(2,1)S(1)} %get-tuple-element.59), channel_id=1, source_target_pairs={{0,1},{1,0},{2,3},{3,2},{4,5},{5,4},{6,7},{7,6},{8,9},{9,8},{10,11... | collective-permute-start | bytes 1228808 | tf_op jit(solution)/shard_map/ppermute | solution.py:30
  256.0 22.6 %collective-permute-start.38 = (bf16[320,768]{1,0:T(8,128)(2,1)S(1)}, bf16[320,768]{1,0:T(8,128)(2,1)S(1)}, u32[]{:S(2)}, u32[]{:S(2)}) collective-permute-start(bf16[320,768]{1,0:T(8,128)(2,1)S(1)} %pad_maximum_fusion.3), channel_id=1, source_target_pairs={{0,8},{8,0},{16,24},{24,16},{1,9},{9,1},{17,25},{25,17},{2,10},{10... | collective-permute-start | bytes 1474568 | tf_op jit(solution)/shard_map/ppermute | solution.py:30
  277.1 24.2 %collective-permute-start.36 = (bf16[320,1280]{1,0:T(8,128)(2,1)S(1)}, bf16[320,1280]{1,0:T(8,128)(2,1)S(1)}, u32[]{:S(2)}, u32[]{:S(2)}) collective-permute-start(bf16[320,1280]{1,0:T(8,128)(2,1)S(1)} %copy-done.8), channel_id=1, source_target_pairs={{0,16},{8,24},{16,0},{24,8},{1,17},{9,25},{17,1},{25,9},{2,18},{10... | collective-permute-start | bytes 2457608 | tf_op jit(solution)/shard_map/ppermute | solution.py:30
  278.6 39.3 %collective-permute-start.37 = (bf16[320,1280]{1,0:T(8,128)(2,1)S(1)}, bf16[320,1280]{1,0:T(8,128)(2,1)S(1)}, u32[]{:S(2)}, u32[]{:S(2)}) collective-permute-start(bf16[320,1280]{1,0:T(8,128)(2,1)S(1)} %copy-done.7), channel_id=1, source_target_pairs={{0,24},{8,16},{16,8},{24,0},{1,25},{9,17},{17,9},{25,1},{2,26},{10... | collective-permute-start | bytes 2457608 | tf_op jit(solution)/shard_map/ppermute | solution.py:30
  279.2 40.6 %collective-permute-start.32 = (bf16[320,768]{1,0:T(8,128)(2,1)S(1)}, bf16[320,768]{1,0:T(8,128)(2,1)S(1)}, u32[]{:S(2)}, u32[]{:S(2)}) collective-permute-start(bf16[320,768]{1,0:T(8,128)(2,1)S(1)} %pad_maximum_fusion.2), channel_id=1, source_target_pairs={{0,8},{8,0},{16,24},{24,16},{1,9},{9,1},{17,25},{25,17},{2,10},{10... | collective-permute-start | bytes 1474568 | tf_op jit(solution)/shard_map/ppermute | solution.py:30
  282.8 46.6 %collective-permute-start.33 = (bf16[320,768]{1,0:T(8,128)(2,1)S(1)}, bf16[320,768]{1,0:T(8,128)(2,1)S(1)}, u32[]{:S(2)}, u32[]{:S(2)}) collective-permute-start(bf16[320,768]{1,0:T(8,128)(2,1)S(1)} %pad_maximum_fusion.2), channel_id=1, source_target_pairs={{0,16},{8,24},{16,0},{24,8},{1,17},{9,25},{17,1},{25,9},{2,18},{10... | collective-permute-start | bytes 1474568 | tf_op jit(solution)/shard_map/ppermute | solution.py:30
  286.2 86.9 %collective-permute-start.29 = (bf16[320,1280]{1,0:T(8,128)(2,1)S(1)}, bf16[320,1280]{1,0:T(8,128)(2,1)S(1)}, u32[]{:S(2)}, u32[]{:S(2)}) collective-permute-start(bf16[320,1280]{1,0:T(8,128)(2,1)S(1)} %copy-done.5), channel_id=1, source_target_pairs={{0,8},{8,0},{16,24},{24,16},{1,9},{9,1},{17,25},{25,17},{2,10},{10... | collective-permute-start | bytes 2457608 | tf_op jit(solution)/shard_map/ppermute | solution.py:30
  301.2 73.0 %collective-permute-start.30 = (bf16[320,1280]{1,0:T(8,128)(2,1)S(1)}, bf16[320,1280]{1,0:T(8,128)(2,1)S(1)}, u32[]{:S(2)}, u32[]{:S(2)}) collective-permute-start(bf16[320,1280]{1,0:T(8,128)(2,1)S(1)} %get-tuple-element.22), channel_id=1, source_target_pairs={{0,16},{8,24},{16,0},{24,8},{1,17},{9,25},{17,1},{25,9},{2,18},{10... | collective-permute-start | bytes 2457608 | tf_op jit(solution)/shard_map/ppermute | solution.py:30
  317.9 57.0 %collective-permute-start.31 = (bf16[320,1280]{1,0:T(8,128)(2,1)S(1)}, bf16[320,1280]{1,0:T(8,128)(2,1)S(1)}, u32[]{:S(2)}, u32[]{:S(2)}) collective-permute-start(bf16[320,1280]{1,0:T(8,128)(2,1)S(1)} %get-tuple-element.21), channel_id=1, source_target_pairs={{0,24},{8,16},{16,8},{24,0},{1,25},{9,17},{17,9},{25,1},{2,26},{10... | collective-permute-start | bytes 2457608 | tf_op jit(solution)/shard_map/ppermute | solution.py:30
  319.8 53.3 %collective-permute-start.34 = (bf16[320,768]{1,0:T(8,128)(2,1)S(1)}, bf16[320,768]{1,0:T(8,128)(2,1)S(1)}, u32[]{:S(2)}, u32[]{:S(2)}) collective-permute-start(bf16[320,768]{1,0:T(8,128)(2,1)S(1)} %pad_maximum_fusion.2), channel_id=1, source_target_pairs={{0,24},{8,16},{16,8},{24,0},{1,25},{9,17},{17,9},{25,1},{2,26},{10... | collective-permute-start | bytes 1474568 | tf_op jit(solution)/shard_map/ppermute | solution.py:30
  329.3 86.0 %collective-permute-start.14 = (bf16[128,5120]{1,0:T(8,128)(2,1)S(1)}, bf16[128,5120]{1,0:T(8,128)(2,1)S(1)}, u32[]{:S(2)}, u32[]{:S(2)}) collective-permute-start(bf16[128,5120]{1,0:T(8,128)(2,1)S(1)} %fusion.34), channel_id=1, source_target_pairs={{0,4},{1,5},{2,6},{3,7},{4,0},{5,1},{6,2},{7,3},{8,12},{9,13},{10,... | collective-permute-start | bytes 3932168 | tf_op jit(solution)/shard_map/ppermute | solution.py:30
  373.0 70.2 %collective-permute-start.28 = (bf16[128,5120]{1,0:T(8,128)(2,1)S(1)}, bf16[128,5120]{1,0:T(8,128)(2,1)S(1)}, u32[]{:S(2)}, u32[]{:S(2)}) collective-permute-start(bf16[128,5120]{1,0:T(8,128)(2,1)S(1)} %convolution_convert_fusion.2), channel_id=1, source_target_pairs={{0,4},{1,5},{2,6},{3,7},{4,0},{5,1},{6,2},{7,3},{8,12},{9,13},{10,... | collective-permute-start | bytes 3932168 | tf_op jit(solution)/shard_map/ppermute | solution.py:30
  373.1 44.0 %collective-permute-start.18 = (bf16[40,5120]{1,0:T(8,128)(2,1)S(1)}, bf16[40,5120]{1,0:T(8,128)(2,1)S(1)}, u32[]{:S(2)}, u32[]{:S(2)}) collective-permute-start(bf16[40,5120]{1,0:T(8,128)(2,1)S(1)} %get-tuple-element.47), channel_id=1, source_target_pairs={{0,1},{1,0},{2,3},{3,2},{4,5},{5,4},{6,7},{7,6},{8,9},{9,8},{10,11... | collective-permute-start | bytes 1228808 | tf_op jit(solution)/shard_map/ppermute | solution.py:30
  374.3 42.9 %collective-permute-start.19 = (bf16[40,5120]{1,0:T(8,128)(2,1)S(1)}, bf16[40,5120]{1,0:T(8,128)(2,1)S(1)}, u32[]{:S(2)}, u32[]{:S(2)}) collective-permute-start(bf16[40,5120]{1,0:T(8,128)(2,1)S(1)} %get-tuple-element.46), channel_id=1, source_target_pairs={{0,2},{1,3},{2,0},{3,1},{4,6},{5,7},{6,4},{7,5},{8,10},{9,11},{10,... | collective-permute-start | bytes 1228808 | tf_op jit(solution)/shard_map/ppermute | solution.py:30
  374.8 44.6 %collective-permute-start.20 = (bf16[40,5120]{1,0:T(8,128)(2,1)S(1)}, bf16[40,5120]{1,0:T(8,128)(2,1)S(1)}, u32[]{:S(2)}, u32[]{:S(2)}) collective-permute-start(bf16[40,5120]{1,0:T(8,128)(2,1)S(1)} %get-tuple-element.45), channel_id=1, source_target_pairs={{0,3},{1,2},{2,1},{3,0},{4,7},{5,6},{6,5},{7,4},{8,11},{9,10},{10,... | collective-permute-start | bytes 1228808 | tf_op jit(solution)/shard_map/ppermute | solution.py:30
  (54 other events, 786.8 us)
Sparse Core Ops, SparseCore 0:
  9.6 58.0 all-gather.2
  69.2 55.3 all-gather.4

commit v2 on v0

v2 whole, which is shorter than its diff:
```python
import functools
import math

import jax
import jax.numpy as jnp
from jax import lax
from jax.experimental import pallas as pl
from jax.experimental.pallas import tpu as pltpu
from jax.sharding import PartitionSpec as P

LAYERS = 40
OUT_SCALE = 1.0 / math.sqrt(2.0 * LAYERS)
ROW_TILE = 8
VMEM_LIMIT = 60 * 1024 * 1024
F32, BF16, I32 = jnp.float32, jnp.bfloat16, jnp.int32
GELU_SCALE = math.sqrt(2.0 / math.pi)
GELU_CUBE = 0.044715


def dot(former, latter):
    return jnp.dot(former, latter, preferred_element_type=F32)


def contract_rows(former, latter):
    return lax.dot_general(former, latter, (((0,), (0,)), ((), ())), preferred_element_type=F32)


def contract_columns(former, latter):
    return lax.dot_general(former, latter, (((1,), (1,)), ((), ())), preferred_element_type=F32)


def iota(shape, dim):
    return lax.broadcasted_iota(I32, shape, dim)


def as_bf16(condition):
    return jnp.where(condition, 1.0, 0.0).astype(BF16)


def gelu(v):
    t = jnp.tanh(GELU_SCALE * (v + GELU_CUBE * (v * v * v)))
    return v * (0.5 * (1.0 + t))


def gelu_slope(v):
    t = jnp.tanh(GELU_SCALE * (v + GELU_CUBE * (v * v * v)))
    inner = GELU_SCALE * (1.0 + 3.0 * GELU_CUBE * (v * v))
    return 0.5 * (1.0 + t) + 0.5 * v * (1.0 - t * t) * inner


def stack(pieces):
    return jnp.concatenate([piece.astype(F32) for piece in pieces], axis=0).astype(BF16)


SHORT = pl.CostEstimate(flops=1, bytes_accessed=1, transcendentals=0)


def params(**kwargs):
    return pltpu.CompilerParams(vmem_limit_bytes=VMEM_LIMIT, **kwargs)


def slots_by_row(routing_t, me, half, block):
    n_rows = routing_t.shape[1]
    ids = [routing_t[k : k + 1, :] for k in (0, 1)]
    codes = [routing_t[k : k + 1, :].astype(F32) for k in (2, 3)]
    total = codes[0] + codes[1]
    gates = [code / total for code in codes]
    height = -(-half // 8) * 8
    expert = me ^ iota((height, n_rows), 0)
    named = [ids[k] == expert for k in (0, 1)]
    either = named[0] | named[1]
    earlier = as_bf16(iota((n_rows, n_rows), 0) < iota((n_rows, n_rows), 1))
    before = dot(as_bf16(either), earlier)
    before = jnp.where(either, before, -1.0)
    gate = jnp.where(named[0], gates[0], jnp.where(named[1], gates[1], 0.0))
    place = iota((block, n_rows), 0).astype(F32)
    hot = [jnp.where(place == before[k : k + 1, :], 1.0, 0.0) for k in range(half)]
    slot_gates = [
        jnp.sum(hot[k] * gate[k : k + 1, :], axis=1, keepdims=True) for k in range(half)
    ]
    return jnp.concatenate(hot, axis=0).astype(BF16), jnp.concatenate(slot_gates, axis=0)


def slots_by_column(routing, me, half, block):
    n_rows = routing.shape[0]
    n_slots = half * block
    ids = [routing[:, k : k + 1] for k in (0, 1)]
    codes = [routing[:, k : k + 1].astype(F32) for k in (2, 3)]
    total = codes[0] + codes[1]
    gates = [code / total for code in codes]
    lanes = 128
    expert = me ^ iota((n_rows, lanes), 1)
    within = iota((n_rows, lanes), 1) < half
    either = ((ids[0] == expert) | (ids[1] == expert)) & within
    earlier = as_bf16(iota((n_rows, n_rows), 1) < iota((n_rows, n_rows), 0))
    before = dot(earlier, as_bf16(either))
    slot = iota((lanes, n_slots), 1)
    owner = iota((lanes, n_slots), 0)
    spread = as_bf16((slot >= owner * block) & (slot < (owner + 1) * block))
    before = dot(before.astype(BF16), spread)
    number = dot(as_bf16(iota((n_rows, lanes), 1) >= 0), as_bf16(slot >= (owner + 1) * block))
    slot_row = iota((n_rows, n_slots), 1)
    owner_row = number.astype(I32)
    place = (slot_row - owner_row * block).astype(F32) == before
    slot_expert = me ^ owner_row
    hot = [as_bf16((ids[k] == slot_expert) & place) for k in (0, 1)]
    return hot, gates


def dispatch_kernel(groups, block, gated, n_after, me_ref, routing_ref, *refs):
    source = refs[0]
    out_ref, hot_ref, gate_ref = refs[1 + n_after :]

    @pl.when(pl.program_id(0) == 0)
    def _():
        hot, gate = slots_by_row(routing_ref[...], me_ref[0], groups, block)
        hot_ref[...] = hot
        gate_ref[...] = jnp.broadcast_to(gate, gate_ref.shape)

    rows = dot(hot_ref[...], source[...])
    if gated:
        rows = (OUT_SCALE * gate_ref[:, :1]) * rows
    for k in range(groups):
        out_ref[k] = rows[k * block : (k + 1) * block].astype(BF16)


def dispatch(me, routing_t, source, groups, block, chunk, gated=False, wait_for=()):
    n_rows, width = source.shape
    return pl.pallas_call(
        functools.partial(dispatch_kernel, groups, block, gated, len(wait_for)),
        grid_spec=pltpu.PrefetchScalarGridSpec(
            num_scalar_prefetch=1,
            grid=(width // chunk,),
            in_specs=[
                pl.BlockSpec(routing_t.shape, lambda d, me: (0, 0)),
                pl.BlockSpec((n_rows, chunk), lambda d, me: (0, d)),
            ]
            + [pl.BlockSpec(memory_space=pl.ANY) for _ in wait_for],
            out_specs=pl.BlockSpec((groups, block, chunk), lambda d, me: (0, 0, d)),
            scratch_shapes=[
                pltpu.VMEM((groups * block, n_rows), BF16),
                pltpu.VMEM((groups * block, 128), F32),
            ],
        ),
        out_shape=jax.ShapeDtypeStruct((groups, block, width), BF16),
        compiler_params=params(),
        cost_estimate=SHORT,
        name="dispatch",
    )(me, routing_t, source, *wait_for)


def forward_kernel(n, block, n_chunks, me_ref, rows_ref, up_ref, down_ref, *refs):
    outs = refs[:n]
    sent_ref, hidden_ref, pre_ref = refs[n:]
    step = pl.program_id(0)

    @pl.when(step < n_chunks)
    def _():
        rows = stack([rows_ref[me_ref[0] ^ k] for k in range(n)])
        sent_ref[0] = rows
        part = dot(rows, up_ref[...])

        @pl.when(step == 0)
        def _():
            pre_ref[...] = part

        @pl.when(step > 0)
        def _():
            pre_ref[...] += part

        @pl.when(step == n_chunks - 1)
        def _():
            hidden_ref[...] = gelu(pre_ref[...]).astype(BF16)

    @pl.when(step >= n_chunks)
    def _():
        rows = contract_columns(hidden_ref[...], down_ref[...])
        for k in range(n):
            outs[k][...] = rows[k * block : (k + 1) * block].astype(BF16)


def forward(me, rows_in, up_weight, down_weight, n_chunks):
    n, block, width = rows_in.shape
    hidden = up_weight.shape[1]
    chunk = width // n_chunks
    rows = n * block
    early = lambda i: jnp.minimum(i, n_chunks - 1)
    late = lambda i: jnp.maximum(i - n_chunks, 0)
    whole = pl.BlockSpec((rows, hidden), lambda i, me: (0, 0))
    results = pl.pallas_call(
        functools.partial(forward_kernel, n, block, n_chunks),
        grid_spec=pltpu.PrefetchScalarGridSpec(
            num_scalar_prefetch=1,
            grid=(2 * n_chunks,),
            in_specs=[
                pl.BlockSpec((n, block, chunk), lambda i, me: (0, 0, early(i))),
                pl.BlockSpec((chunk, hidden), lambda i, me: (early(i), 0)),
                pl.BlockSpec((chunk, hidden), lambda i, me: (late(i), 0)),
            ],
            out_specs=[
                pl.BlockSpec((block, chunk), lambda i, me: (0, late(i))) for _ in range(n)
            ]
            + [pl.BlockSpec((1, rows, chunk), lambda i, me: (early(i), 0, 0)), whole, whole],
        ),
        out_shape=[jax.ShapeDtypeStruct((block, width), BF16) for _ in range(n)]
        + [
            jax.ShapeDtypeStruct((n_chunks, 2 * rows, chunk), BF16),
            jax.ShapeDtypeStruct((rows, hidden), BF16),
            jax.ShapeDtypeStruct((rows, hidden), F32),
        ],
        compiler_params=params(),
        cost_estimate=SHORT,
        name="expert_forward",
    )(me, rows_in, up_weight, down_weight)
    return (results[:n],) + tuple(results[n:])


def backward_kernel(n, block, n_chunks, me_ref, grads_ref, down_ref, up_ref, pre_ref, *refs):
    carried = refs[: n // 2]
    outs = refs[n // 2 + 2 : -3]
    sent_ref, middle_ref, sum_ref = refs[-3:]
    step = pl.program_id(0)
    half = n // 2

    @pl.when(step < n_chunks)
    def _():
        rows = stack([grads_ref[me_ref[0] ^ k] for k in range(n)])
        sent_ref[0] = rows
        part = dot(rows, down_ref[...])

        @pl.when(step == 0)
        def _():
            sum_ref[...] = part

        @pl.when(step > 0)
        def _():
            sum_ref[...] += part

        @pl.when(step == n_chunks - 1)
        def _():
            middle_ref[...] = (sum_ref[...] * gelu_slope(pre_ref[...])).astype(BF16)

    @pl.when(step >= n_chunks)
    def _():
        rows = contract_columns(middle_ref[...], up_ref[...])
        for k in range(n):
            piece = rows[k * block : (k + 1) * block]
            if k < half:
                piece = jnp.concatenate([carried[k][...].astype(F32), piece], axis=0)
            outs[k][...] = piece.astype(BF16)


def backward(me, grads, pre_act, down_weight, up_weight, n_chunks, carried, sent, wait_for):
    n, block, width = grads.shape
    half = n // 2
    chunk = width // n_chunks
    rows = n * block
    hidden = up_weight.shape[1]
    early = lambda i: jnp.minimum(i, n_chunks - 1)
    late = lambda i: jnp.maximum(i - n_chunks, 0)
    whole = pl.BlockSpec((rows, hidden), lambda i, me: (0, 0))
    depths = [2 * block if k < half else block for k in range(n)]
    results = pl.pallas_call(
        functools.partial(backward_kernel, n, block, n_chunks),
        grid_spec=pltpu.PrefetchScalarGridSpec(
            num_scalar_prefetch=1,
            grid=(2 * n_chunks,),
            in_specs=[
                pl.BlockSpec((n, block, chunk), lambda i, me: (0, 0, early(i))),
                pl.BlockSpec((chunk, hidden), lambda i, me: (early(i), 0)),
                pl.BlockSpec((chunk, hidden), lambda i, me: (late(i), 0)),
                whole,
            ]
            + [pl.BlockSpec((block, chunk), lambda i, me: (0, late(i))) for _ in carried]
            + [pl.BlockSpec(memory_space=pl.ANY)] * 2,
            out_specs=[
                pl.BlockSpec((depth, chunk), lambda i, me: (0, late(i))) for depth in depths
            ]
            + [
                pl.BlockSpec((1, rows, chunk), lambda i, me: (early(i), 1, 0)),
                whole,
            ],
            scratch_shapes=[pltpu.VMEM((rows, hidden), F32)],
        ),
        out_shape=[jax.ShapeDtypeStruct((depth, width), BF16) for depth in depths]
        + [
            jax.ShapeDtypeStruct(sent.shape, BF16),
            jax.ShapeDtypeStruct((rows, hidden), BF16),
        ],
        input_output_aliases={5 + len(carried): n},
        compiler_params=params(),
        cost_estimate=SHORT,
        name="expert_backward",
    )(me, grads, down_weight, up_weight, pre_act, *carried, sent, wait_for)
    return results[:half], results[half:n], results[n], results[n + 1]


def combine_kernel(groups, block, offset, gated, n_arrived, n_after, me_ref, routing_ref, *refs):
    n_blocks = groups
    blocks = refs[:n_blocks]
    arrived = refs[n_blocks : n_blocks + n_arrived]
    outs = refs[n_blocks + n_arrived + n_after : -3]
    hot_refs = refs[-3:-1]
    gate_ref = refs[-1]

    @pl.when(pl.program_id(0) == 0)
    def _():
        hot, gates = slots_by_column(routing_ref[...], me_ref[0], groups, block)
        if gated:
            for k in (0, 1):
                hot_refs[k][...] = hot[k]
                gate_ref[:, k * 128 : (k + 1) * 128] = jnp.broadcast_to(
                    OUT_SCALE * gates[k], (gates[k].shape[0], 128)
                )
        else:
            hot_refs[0][...] = (hot[0].astype(F32) + hot[1].astype(F32)).astype(BF16)

    rows = stack([ref[...].astype(F32)[offset : offset + block] for ref in blocks])
    total = dot(hot_refs[0][...], rows)
    if gated:
        total = gate_ref[:, :1] * total + gate_ref[:, 128:129] * dot(hot_refs[1][...], rows)
    if arrived:
        total = total + jnp.concatenate([ref[...].astype(F32) for ref in arrived], axis=0)
    at = 0
    for ref in outs:
        ref[...] = total[at : at + ref.shape[0]].astype(BF16)
        at += ref.shape[0]


def combine(
    me, routing, blocks, block, chunk, gated=False, offset=0, arrived=(), wait_for=(), parts=None
):
    n_rows = routing.shape[0]
    groups = len(blocks)
    depth, width = blocks[0].shape
    by_rows = lambda n: pl.BlockSpec((n, chunk), lambda d, me: (0, d))
    results = pl.pallas_call(
        functools.partial(
            combine_kernel, groups, block, offset, gated, len(arrived), len(wait_for)
        ),
        grid_spec=pltpu.PrefetchScalarGridSpec(
            num_scalar_prefetch=1,
            grid=(width // chunk,),
            in_specs=[pl.BlockSpec(routing.shape, lambda d, me: (0, 0))]
            + [by_rows(depth) for _ in blocks]
            + [by_rows(part.shape[0]) for part in arrived]
            + [pl.BlockSpec(memory_space=pl.ANY) for _ in wait_for],
            out_specs=[by_rows(n) for n in parts or (n_rows,)],
            scratch_shapes=[
                pltpu.VMEM((n_rows, groups * block), BF16),
                pltpu.VMEM((n_rows, groups * block), BF16),
                pltpu.VMEM((n_rows, 256), F32),
            ],
        ),
        out_shape=[jax.ShapeDtypeStruct((n, width), BF16) for n in parts or (n_rows,)],
        compiler_params=params(),
        cost_estimate=SHORT,
        name="combine",
    )(me, routing, *blocks, *arrived, *wait_for)
    return results if parts else results[0]


def weight_kernel(n_dp, rows, traded_ref, pre_ref, hidden_ref, up_ref, down_ref):
    sums = [None, None]
    for d in range(n_dp):
        for i, factor_ref in enumerate((pre_ref, hidden_ref)):
            part = contract_rows(
                traded_ref[d, i * rows : (i + 1) * rows, :],
                factor_ref[d * rows : (d + 1) * rows, :],
            )
            sums[i] = part if d == 0 else sums[i] + part
    up_ref[0] = sums[0].astype(BF16)
    down_ref[0] = sums[1].astype(BF16)


def weight_grads(traded, pre_all, hidden_all, lanes):
    n_dp, depth, width = traded.shape
    hidden = pre_all.shape[1]
    whole = pl.BlockSpec(pre_all.shape, lambda i: (0, 0))
    return pl.pallas_call(
        functools.partial(weight_kernel, n_dp, depth // 2),
        grid=(width // lanes,),
        in_specs=[pl.BlockSpec((n_dp, depth, lanes), lambda i: (0, 0, i)), whole, whole],
        out_specs=[pl.BlockSpec((1, lanes, hidden), lambda i: (0, i, 0))] * 2,
        out_shape=[jax.ShapeDtypeStruct((1, width, hidden), BF16)] * 2,
        compiler_params=params(),
        cost_estimate=SHORT,
        name="weight_grads",
    )(traded, pre_all, hidden_all)


def after_kernel(*refs):
    pass


def after(values, *others):
    anywhere = pl.BlockSpec(memory_space=pl.ANY)
    return pl.pallas_call(
        after_kernel,
        in_specs=[anywhere] * (1 + len(others)),
        out_specs=anywhere,
        out_shape=jax.ShapeDtypeStruct(values.shape, values.dtype),
        input_output_aliases={0: 0},
        cost_estimate=SHORT,
        name="after",
    )(values, *others)


def permute_xor(values, axis, mask):
    size = lax.axis_size(axis)
    return lax.ppermute(values, axis, [(i, i ^ mask) for i in range(size)])


def exchange(blocks):
    return [blocks[0]] + [permute_xor(blocks[k], "expert", k) for k in range(1, len(blocks))]


def local(tokens, grad_out, expert_ids, gate_codes, w_up, w_down):
    n_expert = lax.axis_size("expert")
    n_dp = lax.axis_size("dp")
    n_rows, width = tokens.shape
    capacity = max(2, 12 * n_rows // (5 * n_expert))
    block = -(-capacity // ROW_TILE) * ROW_TILE
    half = n_expert // 2
    chunk = width // n_dp
    me = lax.axis_index("expert").astype(I32).reshape(1)
    first = jnp.zeros((1,), I32)

    def turned(routing):
        return jnp.pad(routing.T, ((0, 4), (0, 0)))

    def swap_direct(blocks):
        return lax.all_to_all(blocks, "expert", split_axis=0, concat_axis=0, tiled=True)

    routing = jnp.concatenate([expert_ids, gate_codes], axis=1)
    far_routing = permute_xor(routing, "expert", half)
    up_weight = lax.all_gather(w_up, "dp", axis=1, tiled=True)[0]
    down_weight = lax.all_gather(w_down, "dp", axis=1, tiled=True)[0]

    place = (first, turned(routing))
    rows_out = dispatch(*place, tokens, n_expert, block, chunk)
    rows_in = swap_direct(rows_out)
    grads_out = dispatch(*place, grad_out, n_expert, block, chunk, gated=True, wait_for=(rows_out, far_routing))
    grads_in = swap_direct(after(grads_out, rows_in))

    out, sent, hidden, pre_act = forward(me, rows_in, up_weight, down_weight, n_dp)
    parts = (n_rows // 4, n_rows - n_rows // 4)
    far_mixed = combine(
        me, far_routing, exchange(out[half:]), block, chunk, gated=True, parts=parts
    )
    mixed_in = [permute_xor(far_mixed[0], "expert", half)]
    mixed_in.append(permute_xor(after(far_mixed[1], mixed_in[0]), "expert", half))

    near_back, far_back, sent, pre_grad = backward(
        me, grads_in, pre_act, down_weight, up_weight, n_dp, out[:half], sent, far_mixed[0]
    )
    far_back = exchange([after(rows, mixed_in[0]) for rows in far_back])
    far_sum = combine(me, far_routing, far_back, block, chunk, wait_for=(mixed_in[1],))
    sum_in = permute_xor(far_sum, "expert", half)
    near_back = exchange([after(rows, *far_back[1:]) for rows in near_back])
    traded = lax.all_to_all(
        after(sent, mixed_in[0]), "dp", split_axis=0, concat_axis=0, tiled=True
    )
    pre_grad = after(pre_grad, mixed_in[0])
    hidden_all = lax.all_gather(hidden, "dp", axis=0, tiled=True)
    pre_all = lax.all_gather(pre_grad, "dp", axis=0, tiled=True)

    grad_up, grad_down = weight_grads(traded, pre_all, hidden_all, chunk // 5)
    layer_output = combine(
        me,
        routing,
        near_back,
        block,
        chunk,
        gated=True,
        arrived=mixed_in,
        wait_for=(grad_up, grad_down),
    )
    grad_tokens = combine(
        me,
        routing,
        near_back,
        block,
        chunk,
        offset=block,
        arrived=(sum_in,),
        wait_for=(layer_output,),
    )
    return (layer_output, grad_tokens, grad_up, grad_down)


def solution(mesh):
    in_specs = (
        P(("dp", "expert"), None),
        P(("dp", "expert"), None),
        P(("dp", "expert"), None),
        P(("dp", "expert"), None),
        P("expert", "dp", None),
        P("expert", "dp", None),
    )
    out_specs = (
        P(("dp", "expert"), None),
        P(("dp", "expert"), None),
        P("expert", "dp", None),
        P("expert", "dp", None),
    )
    return jax.shard_map(local, mesh=mesh, in_specs=in_specs, out_specs=out_specs, check_vma=False)
```

time: 468 us -> 350 us (0.75); the launches traced: 460 us -> 349 us
  Pallas kernels: 0 us -> 72.8 us
  local copies, waits for them, and re-layouts: 77.9 us -> 6.63 us
  waiting for transfers between devices: 266 us -> 219 us
  matrix products: 44.2 us -> 0 us
  other arithmetic: 29.4 us -> 0.01 us
  starting transfers between devices: 28.4 us -> 36.6 us
    all_to_all x6 -> x3, waiting for transfers between devices: 246 us -> 28.4 us  [the longest x1 28.4 us: local(): lax.all_to_all(after(sent, mixed_in[0]), 'dp', split_axis=0, concat_axis=...]
    ppermute x0 -> x13, waiting for transfers between devices: none -> 173 us  [permute_xor(): return lax.ppermute(values, axis, [(i, i ^ mask) for i in range(size)])]
    pallas_call x0 -> x21, Pallas kernels: none -> 72.8 us  [the longest x4 19.6 us: combine(): pl.pallas_call(functools.partial(combine_kernel, groups, block, offset, g...]
    dot_general x6 -> x0, matrix products: 44.2 us -> none  [the longest x2 15.3 us: contract_columns(): lax.dot_general(former, latter, (((1,), (1,)), ((), ())), preferred_eleme...]
    all_to_all x10 -> x0, local copies, waits for them, and re-layouts: 33.8 us -> none  [the longest x2 8.99 us: local(): lax.all_to_all(recv_rows, 'dp', split_axis=1, concat_axis=0, tiled=True)]
    gather x6 -> x0, local copies, waits for them, and re-layouts: 24.7 us -> none  [the longest x3 13.4 us: combine_slots(): picked_rows = returned[slot_index].astype(jnp.float32) * weights[:, None]]
    reduce_sum x4 -> x0, other arithmetic: 20.6 us -> none  [the longest x2 20.5 us: combine_slots(): jnp.sum(picked_rows.reshape(n_rows, 2, returned.shape[1]), axis=1)]
    ppermute x0 -> x13, starting transfers between devices: none -> 19.4 us  [permute_xor(): return lax.ppermute(values, axis, [(i, i ^ mask) for i in range(size)])]
  transfers between devices with their start and end apart: 10 -> 20, of which waited for: 7 -> 11; matrix products, arithmetic and copies ran while one was open for 20% -> 0% of each run, Pallas kernels for 0% -> 19%
where the time goes in v2:
time: 350 us; the launch traced here: 349 us
  waiting for transfers between devices  219 us (63%)
  Pallas kernels  72.8 us (21%)
  starting transfers between devices  36.6 us (10%)
  between operations  13.9 us (4%)
  local copies, waits for them, and re-layouts  6.63 us (2%)
    ppermute x13, waiting for transfers between devices, permute_xor(): return lax.ppermute(values, axis, [(i, i ^ mask) for i in range(size)])  173 us
    all_to_all x1, waiting for transfers between devices, local(): lax.all_to_all(after(sent, mixed_in[0]), 'dp', split_axis=0, concat_axis=...  28.4 us
    pallas_call x4, Pallas kernels, combine(): pl.pallas_call(functools.partial(combine_kernel, groups, block, offset, g...  19.6 us
    ppermute x13, starting transfers between devices, permute_xor(): return lax.ppermute(values, axis, [(i, i ^ mask) for i in range(size)])  19.4 us
    pallas_call x1, Pallas kernels, backward(): pl.pallas_call(functools.partial(backward_kernel, n, block, n_chunks), gr...  16.3 us
    all_gather x1, waiting for transfers between devices, local(): up_weight = lax.all_gather(w_up, 'dp', axis=1, tiled=True)[0]  15.2 us
    pallas_call x1, Pallas kernels, forward(): pl.pallas_call(functools.partial(forward_kernel, n, block, n_chunks), gri...  14.8 us
    pallas_call x1, Pallas kernels, weight_grads(): pl.pallas_call(functools.partial(weight_kernel, n_dp, depth // 2), grid=(...  12.5 us
  transfers between devices with their start and end apart: 20, of which 11 were waited for; matrix products, arithmetic and copies ran while one was open for 0% of the time, Pallas kernels for 19%

profile of v2, /device:TPU:0, one launch (start us, length us, event | category | flops | bytes accessed | tf_op | source)
XLA Modules:
  0.0 348.8 jit_solution(13872376183446223807)
XLA Ops:
  9.3 4.7 %dispatch.2.refs_1_ = bf16[8,40,5120]{2,1,0:T(8,128)(2,1)} custom-call(s32[1]{0:T(128)} %constant.1.clone.1.me_ref, s32[8,128]{1,0:T(8,128)} %pad.4.routing_ref, bf16[128,5120]{1,0:T(8,128)(2,1)} %refs_0_.2), custom_call_target="tpu_custom_call" | custom-call | flops 1 | bytes 1 | tf_op jit(solution)/shard_map/dispatch/pallas_call | solution.py:129
  14.0 7.2 %all-to-all-start = ((bf16[8,40,5120]{2,1,0:T(8,128)(2,1)}), bf16[8,40,5120]{2,1,0:T(8,128)(2,1)S(1)}, u32[]{:S(2)}, u32[]{:S(2)}) async-start(bf16[8,40,5120]{2,1,0:T(8,128)(2,1)} %dispatch.2.refs_1_), calls=%async_computation | async-start | bytes 6553600 | tf_op jit(solution)/shard_map/all_to_all | solution.py:433
  21.4 3.0 collective-permute-start
  24.4 73.2 %collective-permute-done.refs_2_.routing_ref = s32[128,4]{1,0:T(8,128)S(1)} collective-permute-done((s32[128,4]{1,0:T(8,128)S(1)}, s32[128,4]{1,0:T(8,128)S(1)}, u32[]{:S(2)}, u32[]{:S(2)}) %collective-permute-start) | collective-permute-done | bytes 2080 | tf_op jit(solution)/shard_map/ppermute | solution.py:411
  98.2 4.9 %dispatch.3.refs_0_ = bf16[8,40,5120]{2,1,0:T(8,128)(2,1)} custom-call(s32[1]{0:T(128)} %constant.1.clone.1.me_ref, s32[8,128]{1,0:T(8,128)} %pad.4.routing_ref, bf16[128,5120]{1,0:T(8,128)(2,1)} %refs_0_.3, bf16[8,40,5120]{2,1,0:T(8,128)(2,1)} %dispatch.2.refs_1_, s32[128,4]{1,0:T(8,128)} %copy-done.9), custom_call_target="tpu_custom_call" | custom-call | flops 1 | bytes 1 | tf_op jit(solution)/shard_map/dispatch/pallas_call | solution.py:129
  103.1 1.7 copy-done
  104.8 4.5 %all-to-all-start.1 = ((bf16[8,40,5120]{2,1,0:T(8,128)(2,1)}), bf16[8,40,5120]{2,1,0:T(8,128)(2,1)}, u32[]{:S(2)}, u32[]{:S(2)}) async-start(bf16[8,40,5120]{2,1,0:T(8,128)(2,1)} %after.12), calls=%async_computation.1 | async-start | bytes 6553600 | tf_op jit(solution)/shard_map/all_to_all | solution.py:433
  109.4 15.2 %all-gather.7.cloned.1.call-done = bf16[1,5120,768]{2,1,0:T(8,128)(2,1)} async-done(((bf16[1,1280,768]{2,1,0:T(8,128)(2,1)}), bf16[1,5120,768]{2,1,0:T(8,128)(2,1)}) %all-gather.7.cloned.1.call-update) | async-done | bytes 7864336 | tf_op jit(solution)/shard_map/all_gather | solution.py:437
  124.6 14.8 %expert_forward.1 = (bf16[40,5120]{1,0:T(8,128)(2,1)}, bf16[40,5120]{1,0:T(8,128)(2,1)}, bf16[40,5120]{1,0:T(8,128)(2,1)}, bf16[40,5120]{1,0:T(8,128)(2,1)}, bf1...) custom-call(s32[1]{0:T(128)} %bitcast.me_ref, ...), custom_call_target="tpu_custom_call" | custom-call | flops 1 | bytes 1 | tf_op jit(solution)/shard_map/expert_forward/pallas_call | solution.py:190
  139.5 1.5 collective-permute-start.1
  141.0 1.5 collective-permute-start.2
  143.0 22.6 %collective-permute-done.1.refs_1_ = bf16[40,5120]{1,0:T(8,128)(2,1)S(1)} collective-permute-done((bf16[40,5120]{1,0:T(8,128)(2,1)}, bf16[40,5120]{1,0:T(8,128)(2,1)S(1)}, u32[]{:S(2)}, u32[]{:S(2)}) %collective-permute-start.1) | collective-permute-done | bytes 409632 | tf_op jit(solution)/shard_map/ppermute | solution.py:411
  165.6 7.4 %collective-permute-done.2.refs_2_ = bf16[40,5120]{1,0:T(8,128)(2,1)S(1)} collective-permute-done((bf16[40,5120]{1,0:T(8,128)(2,1)}, bf16[40,5120]{1,0:T(8,128)(2,1)S(1)}, u32[]{:S(2)}, u32[]{:S(2)}) %collective-permute-start.2) | collective-permute-done | bytes 409632 | tf_op jit(solution)/shard_map/ppermute | solution.py:411
  173.0 7.0 %collective-permute-done.3.refs_3_ = bf16[40,5120]{1,0:T(8,128)(2,1)S(1)} collective-permute-done((bf16[40,5120]{1,0:T(8,128)(2,1)}, bf16[40,5120]{1,0:T(8,128)(2,1)S(1)}, u32[]{:S(2)}, u32[]{:S(2)}) %collective-permute-start.3) | collective-permute-done | bytes 409632 | tf_op jit(solution)/shard_map/ppermute | solution.py:411
  180.7 4.6 %combine.4 = (bf16[32,5120]{1,0:T(8,128)(2,1)}, bf16[96,5120]{1,0:T(8,128)(2,1)}) custom-call(s32[1]{0:T(128)} %bitcast.me_ref, s32[128,4]{1,0:T(8,128)} %copy-done.9, bf16[40,5120]{1,0:T(8,128)(2,1)} %get-tuple-element.35.refs_0_, bf16[40,5120]{1,0:T(8,128)(2,1)} %copy-done.11, bf16[40,5120]{1,0:T(8,128)(2,1)} %copy-done.12, bf16[40,5120]{1,0:T(8,128)(2,1)} %copy-done.13), custom_call_target="tpu_custom_call" | custom-call | flops 1 | bytes 1 | tf_op jit(solution)/shard_map/combine/pallas_call | solution.py:337
  185.3 4.7 %collective-permute-start.4 = (bf16[32,5120]{1,0:T(8,128)(2,1)}, bf16[32,5120]{1,0:T(8,128)(2,1)S(1)}, u32[]{:S(2)}, u32[]{:S(2)}) collective-permute-start(bf16[32,5120]{1,0:T(8,128)(2,1)} %get-tuple-element.39.refs_5_), channel_id=1, source_target_pairs={{0,4},{1,5},{2,6},{3,7},{4,0},{5,1},{6,2},{7,3},{8,12},{9,13},{10,... | collective-permute-start | bytes 983048 | tf_op jit(solution)/shard_map/ppermute | solution.py:411
  190.1 16.3 %expert_backward.1 = (bf16[80,5120]{1,0:T(8,128)(2,1)}, bf16[80,5120]{1,0:T(8,128)(2,1)}, bf16[80,5120]{1,0:T(8,128)(2,1)}, bf16[80,5120]{1,0:T(8,128)(2,1)}, bf...) custom-call(s32[1]{0:T(128)} %bitcast.me_ref, ...), custom_call_target="tpu_custom_call", output_to_operand_aliasing={{8}: (9, {})} | custom-call | flops 1 | bytes 1 | tf_op jit(solution)/shard_map/expert_backward/pallas_call | solution.py:263
  207.1 5.3 %all-to-all-start.2 = ((bf16[4,640,1280]{2,1,0:T(8,128)(2,1)}), bf16[4,640,1280]{2,1,0:T(8,128)(2,1)}, u32[]{:S(2)}, u32[]{:S(2)}) async-start(bf16[4,640,1280]{2,1,0:T(8,128)(2,1)} %after.21), calls=%async_computation.2 | async-start | bytes 13107200 | tf_op jit(solution)/shard_map/all_to_all | solution.py:461
  213.1 1.5 collective-permute-start.7
  215.2 1.4 collective-permute-start.5
  216.6 27.7 %collective-permute-done.7.refs_3_ = bf16[40,5120]{1,0:T(8,128)(2,1)S(1)} collective-permute-done((bf16[40,5120]{1,0:T(8,128)(2,1)}, bf16[40,5120]{1,0:T(8,128)(2,1)S(1)}, u32[]{:S(2)}, u32[]{:S(2)}) %collective-permute-start.7) | collective-permute-done | bytes 409632 | tf_op jit(solution)/shard_map/ppermute | solution.py:411
  244.4 8.5 %collective-permute-done.6.refs_2_ = bf16[40,5120]{1,0:T(8,128)(2,1)S(1)} collective-permute-done((bf16[40,5120]{1,0:T(8,128)(2,1)}, bf16[40,5120]{1,0:T(8,128)(2,1)S(1)}, u32[]{:S(2)}, u32[]{:S(2)}) %collective-permute-start.6) | collective-permute-done | bytes 409632 | tf_op jit(solution)/shard_map/ppermute | solution.py:411
  252.9 5.1 %collective-permute-done.11.refs_5_.refs_4_ = bf16[96,5120]{1,0:T(8,128)(2,1)S(1)} collective-permute-done((bf16[96,5120]{1,0:T(8,128)(2,1)}, bf16[96,5120]{1,0:T(8,128)(2,1)S(1)}, u32[]{:S(2)}, u32[]{:S(2)}) %collective-permute-start.11) | collective-permute-done | bytes 983072 | tf_op jit(solution)/shard_map/ppermute | solution.py:411
  259.0 4.5 %combine.6 = bf16[128,5120]{1,0:T(8,128)(2,1)} custom-call(s32[1]{0:T(128)} %bitcast.me_ref, s32[128,4]{1,0:T(8,128)} %copy-done.9, bf16[40,5120]{1,0:T(8,128)(2,1)} %after.23.refs_0_, bf16[40,5120]{1,0:T(8,128)(2,1)} %copy-done.4, bf16[40,5120]{1,0:T(8,128)(2,1)} %copy-done.3, bf16[40,5120]{1,0:T(8,128)(2,1)} %copy-done.2, bf16[96,5120]{1,0:T(8,128)(2,1)} %copy-done.5), custom_call_target="tpu_custom_call" | custom-call | flops 1 | bytes 1 | tf_op jit(solution)/shard_map/combine/pallas_call | solution.py:337
  263.5 2.8 collective-permute-start.10
  266.5 1.5 collective-permute-start.8
  268.0 28.4 %all-to-all-done.2.traded_ref = bf16[4,640,1280]{2,1,0:T(8,128)(2,1)} async-done(((bf16[4,640,1280]{2,1,0:T(8,128)(2,1)}), bf16[4,640,1280]{2,1,0:T(8,128)(2,1)}, u32[]{:S(2)}, u32[]{:S(2)}) %all-to-all-start.2) | async-done | bytes 6553632 | tf_op jit(solution)/shard_map/all_to_all | solution.py:461
  296.4 12.5 %weight_grads.1 = (bf16[1,1280,768]{2,1,0:T(8,128)(2,1)}, bf16[1,1280,768]{2,1,0:T(8,128)(2,1)}) custom-call(bf16[4,640,1280]{2,1,0:T(8,128)(2,1)} %all-to-all-done.2.traded_ref, bf16[1280,768]{1,0:T(8,128)(2,1)} %all-gather.9.cloned.1.call-done.pre_ref, bf16[1280,768]{1,0:T(8,128)(2,1)} %all-gather.11.cloned.1.call-done.hidden_ref), custom_call_target="tpu_custom_call" | custom-call | flops 1 | bytes 1 | tf_op jit(solution)/shard_map/weight_grads/pallas_call | solution.py:380
  308.9 1.6 collective-permute-done.10.refs_3_
  310.5 20.1 %collective-permute-done.9.refs_2_ = bf16[80,5120]{1,0:T(8,128)(2,1)S(1)} collective-permute-done((bf16[80,5120]{1,0:T(8,128)(2,1)}, bf16[80,5120]{1,0:T(8,128)(2,1)S(1)}, u32[]{:S(2)}, u32[]{:S(2)}) %collective-permute-start.9) | collective-permute-done | bytes 819232 | tf_op jit(solution)/shard_map/ppermute | solution.py:411
  331.8 5.3 %combine.5.refs_5_ = bf16[128,5120]{1,0:T(8,128)(2,1)} custom-call(s32[1]{0:T(128)} %bitcast.me_ref, s32[128,4]{1,0:T(8,128)} %copy-done.10, bf16[80,5120]{1,0:T(8,128)(2,1)} %after.16.refs_0_, bf16[80,5120]{1,0:T(8,128)(2,1)} %copy-done.8, bf16[80,5120]{1,0:T(8,128)(2,1)} %copy-done.7, bf16[80,5120]{1,0:T(8,128)(2,1)} %copy-done.6, ...), custom_call_target="tpu_custom_call" | custom-call | flops 1 | bytes 1 | tf_op jit(solution)/shard_map/combine/pallas_call | solution.py:337
  337.1 5.1 %combine.7 = bf16[128,5120]{1,0:T(8,128)(2,1)} custom-call(s32[1]{0:T(128)} %bitcast.me_ref, s32[128,4]{1,0:T(8,128)} %copy-done.10, bf16[80,5120]{1,0:T(8,128)(2,1)} %after.16.refs_0_, bf16[80,5120]{1,0:T(8,128)(2,1)} %copy-done.8, bf16[80,5120]{1,0:T(8,128)(2,1)} %copy-done.7, bf16[80,5120]{1,0:T(8,128)(2,1)} %copy-done.6, ...), custom_call_target="tpu_custom_call" | custom-call | flops 1 | bytes 1 | tf_op jit(solution)/shard_map/combine/pallas_call | solution.py:337
  (68 shorter events, 8.6 us)
Async XLA Ops:
  7.2 1.5 copy-start.15
  7.2 1.5 copy-start.14
  7.2 102.2 %all-gather.5.cloned.1.call-start = ((), (), s32[]{:S(2)}) async-start(), calls=%async_computation.3 | async-start | bytes 9830400 | tf_op jit(solution)/shard_map/all_gather | solution.py:438
  7.9 116.7 %all-gather.7.cloned.1.call-start = ((), (), s32[]{:S(2)}) async-start(), calls=%async_computation.4 | async-start | bytes 9830400 | tf_op jit(solution)/shard_map/all_gather | solution.py:437
  14.0 89.1 %all-to-all-start = ((bf16[8,40,5120]{2,1,0:T(8,128)(2,1)}), bf16[8,40,5120]{2,1,0:T(8,128)(2,1)S(1)}, u32[]{:S(2)}, u32[]{:S(2)}) async-start(bf16[8,40,5120]{2,1,0:T(8,128)(2,1)} %dispatch.2.refs_1_), calls=%async_computation | async-start | bytes 6553600 | tf_op jit(solution)/shard_map/all_to_all | solution.py:433
  21.4 83.5 %copy-start.10 = (s32[128,4]{1,0:T(8,128)}, s32[128,4]{1,0:T(8,128)S(1)}, u32[]{:S(2)}) copy-start(s32[128,4]{1,0:T(8,128)S(1)} %copy.28.routing_ref) | copy-start | bytes 6148
  21.4 76.2 %collective-permute-start = (s32[128,4]{1,0:T(8,128)S(1)}, s32[128,4]{1,0:T(8,128)S(1)}, u32[]{:S(2)}, u32[]{:S(2)}) collective-permute-start(s32[128,4]{1,0:T(8,128)S(1)} %copy.28.routing_ref), channel_id=1, source_target_pairs={{0,4},{1,5},{2,6},{3,7},{4,0},{5,1},{6,2},{7,3},{8,12},{9,13},{10,... | collective-permute-start | bytes 6152 | tf_op jit(solution)/shard_map/ppermute | solution.py:411
  103.1 1.7 copy-start
  104.8 85.2 %all-to-all-start.1 = ((bf16[8,40,5120]{2,1,0:T(8,128)(2,1)}), bf16[8,40,5120]{2,1,0:T(8,128)(2,1)}, u32[]{:S(2)}, u32[]{:S(2)}) async-start(bf16[8,40,5120]{2,1,0:T(8,128)(2,1)} %after.12), calls=%async_computation.1 | async-start | bytes 6553600 | tf_op jit(solution)/shard_map/all_to_all | solution.py:433
  109.3 158.7 %all-gather.11.cloned.1.call-start = ((), (), s32[]{:S(2)}) async-start(), calls=%async_computation.6 | async-start | bytes 2457600 | tf_op jit(solution)/shard_map/all_gather | solution.py:465
  139.5 26.1 %collective-permute-start.1 = (bf16[40,5120]{1,0:T(8,128)(2,1)}, bf16[40,5120]{1,0:T(8,128)(2,1)S(1)}, u32[]{:S(2)}, u32[]{:S(2)}) collective-permute-start(bf16[40,5120]{1,0:T(8,128)(2,1)} %get-tuple-element.36), channel_id=1, source_target_pairs={{0,1},{1,0},{2,3},{3,2},{4,5},{5,4},{6,7},{7,6},{8,9},{9,8},{10,11... | collective-permute-start | bytes 1228808 | tf_op jit(solution)/shard_map/ppermute | solution.py:411
  141.0 32.0 %collective-permute-start.2 = (bf16[40,5120]{1,0:T(8,128)(2,1)}, bf16[40,5120]{1,0:T(8,128)(2,1)S(1)}, u32[]{:S(2)}, u32[]{:S(2)}) collective-permute-start(bf16[40,5120]{1,0:T(8,128)(2,1)} %get-tuple-element.37), channel_id=1, source_target_pairs={{0,2},{1,3},{2,0},{3,1},{4,6},{5,7},{6,4},{7,5},{8,10},{9,11},{10,... | collective-permute-start | bytes 1228808 | tf_op jit(solution)/shard_map/ppermute | solution.py:411
  142.5 37.5 %collective-permute-start.3 = (bf16[40,5120]{1,0:T(8,128)(2,1)}, bf16[40,5120]{1,0:T(8,128)(2,1)S(1)}, u32[]{:S(2)}, u32[]{:S(2)}) collective-permute-start(bf16[40,5120]{1,0:T(8,128)(2,1)} %get-tuple-element.38), channel_id=1, source_target_pairs={{0,3},{1,2},{2,1},{3,0},{4,7},{5,6},{6,5},{7,4},{8,11},{9,10},{10,... | collective-permute-start | bytes 1228808 | tf_op jit(solution)/shard_map/ppermute | solution.py:411
  165.6 14.4 %copy-start.11 = (bf16[40,5120]{1,0:T(8,128)(2,1)}, bf16[40,5120]{1,0:T(8,128)(2,1)S(1)}, u32[]{:S(2)}) copy-start(bf16[40,5120]{1,0:T(8,128)(2,1)S(1)} %collective-permute-done.1.refs_1_) | copy-start | bytes 1228804
  173.0 7.0 %copy-start.12 = (bf16[40,5120]{1,0:T(8,128)(2,1)}, bf16[40,5120]{1,0:T(8,128)(2,1)S(1)}, u32[]{:S(2)}) copy-start(bf16[40,5120]{1,0:T(8,128)(2,1)S(1)} %collective-permute-done.2.refs_2_) | copy-start | bytes 1228804
  185.3 21.0 %collective-permute-start.4 = (bf16[32,5120]{1,0:T(8,128)(2,1)}, bf16[32,5120]{1,0:T(8,128)(2,1)S(1)}, u32[]{:S(2)}, u32[]{:S(2)}) collective-permute-start(bf16[32,5120]{1,0:T(8,128)(2,1)} %get-tuple-element.39.refs_5_), channel_id=1, source_target_pairs={{0,4},{1,5},{2,6},{3,7},{4,0},{5,1},{6,2},{7,3},{8,12},{9,13},{10,... | collective-permute-start | bytes 983048 | tf_op jit(solution)/shard_map/ppermute | solution.py:411
  207.1 89.3 %all-to-all-start.2 = ((bf16[4,640,1280]{2,1,0:T(8,128)(2,1)}), bf16[4,640,1280]{2,1,0:T(8,128)(2,1)}, u32[]{:S(2)}, u32[]{:S(2)}) async-start(bf16[4,640,1280]{2,1,0:T(8,128)(2,1)} %after.21), calls=%async_computation.2 | async-start | bytes 13107200 | tf_op jit(solution)/shard_map/all_to_all | solution.py:461
  212.4 55.6 %all-gather.9.cloned.1.call-start = ((), (), s32[]{:S(2)}) async-start(), calls=%async_computation.5 | async-start | bytes 2457600 | tf_op jit(solution)/shard_map/all_gather | solution.py:466
  213.0 45.0 %collective-permute-start.11 = (bf16[96,5120]{1,0:T(8,128)(2,1)}, bf16[96,5120]{1,0:T(8,128)(2,1)S(1)}, u32[]{:S(2)}, u32[]{:S(2)}) collective-permute-start(bf16[96,5120]{1,0:T(8,128)(2,1)} %after.20), channel_id=1, source_target_pairs={{0,4},{1,5},{2,6},{3,7},{4,0},{5,1},{6,2},{7,3},{8,12},{9,13},{10,... | collective-permute-start | bytes 2949128 | tf_op jit(solution)/shard_map/ppermute | solution.py:411
  213.1 31.3 %collective-permute-start.7 = (bf16[40,5120]{1,0:T(8,128)(2,1)}, bf16[40,5120]{1,0:T(8,128)(2,1)S(1)}, u32[]{:S(2)}, u32[]{:S(2)}) collective-permute-start(bf16[40,5120]{1,0:T(8,128)(2,1)} %after.15), channel_id=1, source_target_pairs={{0,3},{1,2},{2,1},{3,0},{4,7},{5,6},{6,5},{7,4},{8,11},{9,10},{10,... | collective-permute-start | bytes 1228808 | tf_op jit(solution)/shard_map/ppermute | solution.py:411
  214.5 38.3 %collective-permute-start.6 = (bf16[40,5120]{1,0:T(8,128)(2,1)}, bf16[40,5120]{1,0:T(8,128)(2,1)S(1)}, u32[]{:S(2)}, u32[]{:S(2)}) collective-permute-start(bf16[40,5120]{1,0:T(8,128)(2,1)} %after.14), channel_id=1, source_target_pairs={{0,2},{1,3},{2,0},{3,1},{4,6},{5,7},{6,4},{7,5},{8,10},{9,11},{10,... | collective-permute-start | bytes 1228808 | tf_op jit(solution)/shard_map/ppermute | solution.py:411
  215.2 37.7 %collective-permute-start.5 = (bf16[40,5120]{1,0:T(8,128)(2,1)}, bf16[40,5120]{1,0:T(8,128)(2,1)S(1)}, u32[]{:S(2)}, u32[]{:S(2)}) collective-permute-start(bf16[40,5120]{1,0:T(8,128)(2,1)} %after.13), channel_id=1, source_target_pairs={{0,1},{1,0},{2,3},{3,2},{4,5},{5,4},{6,7},{7,6},{8,9},{9,8},{10,11... | collective-permute-start | bytes 1228808 | tf_op jit(solution)/shard_map/ppermute | solution.py:411
  244.4 13.6 %copy-start.2 = (bf16[40,5120]{1,0:T(8,128)(2,1)}, bf16[40,5120]{1,0:T(8,128)(2,1)S(1)}, u32[]{:S(2)}) copy-start(bf16[40,5120]{1,0:T(8,128)(2,1)S(1)} %collective-permute-done.7.refs_3_) | copy-start | bytes 1228804
  252.9 5.1 %copy-start.3 = (bf16[40,5120]{1,0:T(8,128)(2,1)}, bf16[40,5120]{1,0:T(8,128)(2,1)S(1)}, u32[]{:S(2)}) copy-start(bf16[40,5120]{1,0:T(8,128)(2,1)S(1)} %collective-permute-done.6.refs_2_) | copy-start | bytes 1228804
  252.9 5.1 %copy-start.4 = (bf16[40,5120]{1,0:T(8,128)(2,1)}, bf16[40,5120]{1,0:T(8,128)(2,1)S(1)}, u32[]{:S(2)}) copy-start(bf16[40,5120]{1,0:T(8,128)(2,1)S(1)} %collective-permute-done.5.refs_1_) | copy-start | bytes 1228804
  258.0 1.0 copy-start.5
  263.5 73.7 %collective-permute-start.12 = (bf16[128,5120]{1,0:T(8,128)(2,1)}, bf16[128,5120]{1,0:T(8,128)(2,1)}, u32[]{:S(2)}, u32[]{:S(2)}) collective-permute-start(bf16[128,5120]{1,0:T(8,128)(2,1)} %combine.6), channel_id=1, source_target_pairs={{0,4},{1,5},{2,6},{3,7},{4,0},{5,1},{6,2},{7,3},{8,12},{9,13},{10,... | collective-permute-start | bytes 3932168 | tf_op jit(solution)/shard_map/ppermute | solution.py:411
  263.5 47.0 %collective-permute-start.10 = (bf16[80,5120]{1,0:T(8,128)(2,1)}, bf16[80,5120]{1,0:T(8,128)(2,1)S(1)}, u32[]{:S(2)}, u32[]{:S(2)}) collective-permute-start(bf16[80,5120]{1,0:T(8,128)(2,1)} %after.19), channel_id=1, source_target_pairs={{0,3},{1,2},{2,1},{3,0},{4,7},{5,6},{6,5},{7,4},{8,11},{9,10},{10,... | collective-permute-start | bytes 2457608 | tf_op jit(solution)/shard_map/ppermute | solution.py:411
  266.3 64.3 %collective-permute-start.9 = (bf16[80,5120]{1,0:T(8,128)(2,1)}, bf16[80,5120]{1,0:T(8,128)(2,1)S(1)}, u32[]{:S(2)}, u32[]{:S(2)}) collective-permute-start(bf16[80,5120]{1,0:T(8,128)(2,1)} %after.18), channel_id=1, source_target_pairs={{0,2},{1,3},{2,0},{3,1},{4,6},{5,7},{6,4},{7,5},{8,10},{9,11},{10,... | collective-permute-start | bytes 2457608 | tf_op jit(solution)/shard_map/ppermute | solution.py:411
  266.5 64.1 %collective-permute-start.8 = (bf16[80,5120]{1,0:T(8,128)(2,1)}, bf16[80,5120]{1,0:T(8,128)(2,1)S(1)}, u32[]{:S(2)}, u32[]{:S(2)}) collective-permute-start(bf16[80,5120]{1,0:T(8,128)(2,1)} %after.17), channel_id=1, source_target_pairs={{0,1},{1,0},{2,3},{3,2},{4,5},{5,4},{6,7},{7,6},{8,9},{9,8},{10,11... | collective-permute-start | bytes 2457608 | tf_op jit(solution)/shard_map/ppermute | solution.py:411
  310.5 20.1 %copy-start.6 = (bf16[80,5120]{1,0:T(8,128)(2,1)}, bf16[80,5120]{1,0:T(8,128)(2,1)S(1)}, u32[]{:S(2)}) copy-start(bf16[80,5120]{1,0:T(8,128)(2,1)S(1)} %collective-permute-done.10.refs_3_) | copy-start | bytes 2457604
  330.6 1.2 copy-start.8
  (4 other events, 3.0 us)
Sparse Core Ops, SparseCore 0:
  9.6 58.1 all-gather.4
  69.3 55.3 all-gather.6
  139.6 21.8 all-gather.10
  215.0 30.9 all-gather.8

commit v3 on v2

--- a/solution.py
+++ b/solution.py
@@ -11,7 +11,7 @@
 LAYERS = 40
 OUT_SCALE = 1.0 / math.sqrt(2.0 * LAYERS)
 ROW_TILE = 8
-VMEM_LIMIT = 60 * 1024 * 1024
+VMEM_LIMIT = 64 * 1024 * 1024 - 65536
 F32, BF16, I32 = jnp.float32, jnp.bfloat16, jnp.int32
 GELU_SCALE = math.sqrt(2.0 / math.pi)
 GELU_CUBE = 0.044715
@@ -149,176 +149,132 @@
     )(me, routing_t, source, *wait_for)
 
 
-def forward_kernel(n, block, n_chunks, me_ref, rows_ref, up_ref, down_ref, *refs):
-    outs = refs[:n]
-    sent_ref, hidden_ref, pre_ref = refs[n:]
-    step = pl.program_id(0)
-
-    @pl.when(step < n_chunks)
-    def _():
-        rows = stack([rows_ref[me_ref[0] ^ k] for k in range(n)])
-        sent_ref[0] = rows
-        part = dot(rows, up_ref[...])
-
-        @pl.when(step == 0)
-        def _():
-            pre_ref[...] = part
-
-        @pl.when(step > 0)
-        def _():
-            pre_ref[...] += part
-
-        @pl.when(step == n_chunks - 1)
-        def _():
-            hidden_ref[...] = gelu(pre_ref[...]).astype(BF16)
-
-    @pl.when(step >= n_chunks)
-    def _():
-        rows = contract_columns(hidden_ref[...], down_ref[...])
+def expert_kernel(n, n_chunks, backward, *refs):
+    me_ref, rows_hbm, first_hbm, second_hbm = refs[:4]
+    at = 7 if backward else 4
+    outs = refs[at : at + n]
+    sent_hbm, middle_ref = refs[at + n : at + n + 2]
+    pre_ref = refs[4] if backward else refs[at + n + 2]
+    rows_v, first_v, second_v, out_v, in_sem, out_sem = refs[-6:]
+    rows, width = rows_v.shape
+    chunk = width // n_chunks
+    columns = [pl.ds(d * chunk, chunk) for d in range(n_chunks)]
+
+    def load(d):
+        return [
+            pltpu.make_async_copy(
+                rows_hbm.at[:, columns[d]], rows_v.at[:, columns[d]], in_sem.at[0, d]
+            ),
+            pltpu.make_async_copy(first_hbm.at[columns[d]], first_v.at[columns[d]], in_sem.at[1, d]),
+        ]
+
+    def load_second(d):
+        return pltpu.make_async_copy(
+            second_hbm.at[columns[d]], second_v.at[columns[d]], in_sem.at[2, d]
+        )
+
+    def send(d):
+        target = sent_hbm.at[d, pl.ds(rows if backward else 0, rows)]
+        return pltpu.make_async_copy(rows_v.at[:, columns[d]], target, in_sem.at[3, d])
+
+    def store(d, k):
+        return pltpu.make_async_copy(
+            out_v.at[me_ref[0] ^ k, :, columns[d]], outs[k].at[:, columns[d]], out_sem.at[d, k]
+        )
+
+    for d in range(n_chunks):
+        for copy in load(d):
+            copy.start()
+    for d in range(n_chunks):
+        load_second(d).start()
+    total = None
+    for d in range(n_chunks):
+        for copy in load(d):
+            copy.wait()
+        send(d).start()
+        part = dot(rows_v[:, columns[d]], first_v[columns[d]])
+        total = part if d == 0 else total + part
+    if backward:
+        middle = (total * gelu_slope(pre_ref[...])).astype(BF16)
+    else:
+        pre_ref[...] = total
+        middle = gelu(total).astype(BF16)
+    middle_ref[...] = middle
+    for d in range(n_chunks):
+        load_second(d).wait()
+        result = contract_columns(middle, second_v[columns[d]])
+        out_v[:, :, columns[d]] = result.reshape(n, rows // n, chunk).astype(BF16)
         for k in range(n):
-            outs[k][...] = rows[k * block : (k + 1) * block].astype(BF16)
-
-
-def forward(me, rows_in, up_weight, down_weight, n_chunks):
+            store(d, k).start()
+    for d in range(n_chunks):
+        send(d).wait()
+        for k in range(n):
+            store(d, k).wait()
+
+
+def expert(me, rows_in, first, second, n_chunks, pre=None, sent=None, wait_for=None):
     n, block, width = rows_in.shape
-    hidden = up_weight.shape[1]
+    rows = n * block
+    hidden = first.shape[1]
     chunk = width // n_chunks
-    rows = n * block
-    early = lambda i: jnp.minimum(i, n_chunks - 1)
-    late = lambda i: jnp.maximum(i - n_chunks, 0)
-    whole = pl.BlockSpec((rows, hidden), lambda i, me: (0, 0))
+    backward = pre is not None
+    anywhere = pl.BlockSpec(memory_space=pl.ANY)
+    whole = pl.BlockSpec(memory_space=pltpu.VMEM)
+    operands = (me, rows_in.reshape(rows, width), first, second)
+    in_specs = [pl.BlockSpec(memory_space=pltpu.SMEM)] + [anywhere] * 3
+    if backward:
+        operands += (pre, sent, wait_for)
+        in_specs += [whole, anywhere, anywhere]
     results = pl.pallas_call(
-        functools.partial(forward_kernel, n, block, n_chunks),
-        grid_spec=pltpu.PrefetchScalarGridSpec(
-            num_scalar_prefetch=1,
-            grid=(2 * n_chunks,),
-            in_specs=[
-                pl.BlockSpec((n, block, chunk), lambda i, me: (0, 0, early(i))),
-                pl.BlockSpec((chunk, hidden), lambda i, me: (early(i), 0)),
-                pl.BlockSpec((chunk, hidden), lambda i, me: (late(i), 0)),
-            ],
-            out_specs=[
-                pl.BlockSpec((block, chunk), lambda i, me: (0, late(i))) for _ in range(n)
-            ]
-            + [pl.BlockSpec((1, rows, chunk), lambda i, me: (early(i), 0, 0)), whole, whole],
-        ),
-        out_shape=[jax.ShapeDtypeStruct((block, width), BF16) for _ in range(n)]
+        functools.partial(expert_kernel, n, n_chunks, backward),
+        in_specs=in_specs,
+        out_specs=[anywhere] * (n + 1) + [whole] * (1 if backward else 2),
+        out_shape=[jax.ShapeDtypeStruct((block, width), BF16)] * n
         + [
             jax.ShapeDtypeStruct((n_chunks, 2 * rows, chunk), BF16),
             jax.ShapeDtypeStruct((rows, hidden), BF16),
-            jax.ShapeDtypeStruct((rows, hidden), F32),
+        ]
+        + ([] if backward else [jax.ShapeDtypeStruct((rows, hidden), F32)]),
+        scratch_shapes=[
+            pltpu.VMEM((rows, width), BF16),
+            pltpu.VMEM((width, hidden), BF16),
+            pltpu.VMEM((width, hidden), BF16),
+            pltpu.VMEM((n, block, width), BF16),
+            pltpu.SemaphoreType.DMA((4, n_chunks)),
+            pltpu.SemaphoreType.DMA((n_chunks, n)),
         ],
+        input_output_aliases={5: n} if backward else {},
         compiler_params=params(),
         cost_estimate=SHORT,
-        name="expert_forward",
-    )(me, rows_in, up_weight, down_weight)
+        name="expert_backward" if backward else "expert_forward",
+    )(*operands)
     return (results[:n],) + tuple(results[n:])
 
 
-def backward_kernel(n, block, n_chunks, me_ref, grads_ref, down_ref, up_ref, pre_ref, *refs):
-    carried = refs[: n // 2]
-    outs = refs[n // 2 + 2 : -3]
-    sent_ref, middle_ref, sum_ref = refs[-3:]
-    step = pl.program_id(0)
-    half = n // 2
-
-    @pl.when(step < n_chunks)
-    def _():
-        rows = stack([grads_ref[me_ref[0] ^ k] for k in range(n)])
-        sent_ref[0] = rows
-        part = dot(rows, down_ref[...])
-
-        @pl.when(step == 0)
-        def _():
-            sum_ref[...] = part
-
-        @pl.when(step > 0)
-        def _():
-            sum_ref[...] += part
-
-        @pl.when(step == n_chunks - 1)
-        def _():
-            middle_ref[...] = (sum_ref[...] * gelu_slope(pre_ref[...])).astype(BF16)
-
-    @pl.when(step >= n_chunks)
-    def _():
-        rows = contract_columns(middle_ref[...], up_ref[...])
-        for k in range(n):
-            piece = rows[k * block : (k + 1) * block]
-            if k < half:
-                piece = jnp.concatenate([carried[k][...].astype(F32), piece], axis=0)
-            outs[k][...] = piece.astype(BF16)
-
-
-def backward(me, grads, pre_act, down_weight, up_weight, n_chunks, carried, sent, wait_for):
-    n, block, width = grads.shape
-    half = n // 2
-    chunk = width // n_chunks
-    rows = n * block
-    hidden = up_weight.shape[1]
-    early = lambda i: jnp.minimum(i, n_chunks - 1)
-    late = lambda i: jnp.maximum(i - n_chunks, 0)
-    whole = pl.BlockSpec((rows, hidden), lambda i, me: (0, 0))
-    depths = [2 * block if k < half else block for k in range(n)]
-    results = pl.pallas_call(
-        functools.partial(backward_kernel, n, block, n_chunks),
-        grid_spec=pltpu.PrefetchScalarGridSpec(
-            num_scalar_prefetch=1,
-            grid=(2 * n_chunks,),
-            in_specs=[
-                pl.BlockSpec((n, block, chunk), lambda i, me: (0, 0, early(i))),
-                pl.BlockSpec((chunk, hidden), lambda i, me: (early(i), 0)),
-                pl.BlockSpec((chunk, hidden), lambda i, me: (late(i), 0)),
-                whole,
-            ]
-            + [pl.BlockSpec((block, chunk), lambda i, me: (0, late(i))) for _ in carried]
-            + [pl.BlockSpec(memory_space=pl.ANY)] * 2,
-            out_specs=[
-                pl.BlockSpec((depth, chunk), lambda i, me: (0, late(i))) for depth in depths
-            ]
-            + [
-                pl.BlockSpec((1, rows, chunk), lambda i, me: (early(i), 1, 0)),
-                whole,
-            ],
-            scratch_shapes=[pltpu.VMEM((rows, hidden), F32)],
-        ),
-        out_shape=[jax.ShapeDtypeStruct((depth, width), BF16) for depth in depths]
-        + [
-            jax.ShapeDtypeStruct(sent.shape, BF16),
-            jax.ShapeDtypeStruct((rows, hidden), BF16),
-        ],
-        input_output_aliases={5 + len(carried): n},
-        compiler_params=params(),
-        cost_estimate=SHORT,
-        name="expert_backward",
-    )(me, grads, down_weight, up_weight, pre_act, *carried, sent, wait_for)
-    return results[:half], results[half:n], results[n], results[n + 1]
-
-
-def combine_kernel(groups, block, offset, gated, n_arrived, n_after, me_ref, routing_ref, *refs):
+def combine_kernel(groups, block, gated, n_arrived, n_after, me_ref, routing_ref, *refs):
     n_blocks = groups
     blocks = refs[:n_blocks]
     arrived = refs[n_blocks : n_blocks + n_arrived]
-    outs = refs[n_blocks + n_arrived + n_after : -3]
-    hot_refs = refs[-3:-1]
-    gate_ref = refs[-1]
+    outs = refs[n_blocks + n_arrived + n_after : -2]
+    hot_ref, gate_ref = refs[-2:]
 
     @pl.when(pl.program_id(0) == 0)
     def _():
         hot, gates = slots_by_column(routing_ref[...], me_ref[0], groups, block)
         if gated:
+            hot_ref[...] = jnp.concatenate(hot, axis=0)
             for k in (0, 1):
-                hot_refs[k][...] = hot[k]
                 gate_ref[:, k * 128 : (k + 1) * 128] = jnp.broadcast_to(
                     OUT_SCALE * gates[k], (gates[k].shape[0], 128)
                 )
         else:
-            hot_refs[0][...] = (hot[0].astype(F32) + hot[1].astype(F32)).astype(BF16)
-
-    rows = stack([ref[...].astype(F32)[offset : offset + block] for ref in blocks])
-    total = dot(hot_refs[0][...], rows)
+            hot_ref[...] = (hot[0].astype(F32) + hot[1].astype(F32)).astype(BF16)
+
+    rows = stack([ref[...] for ref in blocks])
+    n_rows = routing_ref.shape[0]
+    total = dot(hot_ref[...], rows)
     if gated:
-        total = gate_ref[:, :1] * total + gate_ref[:, 128:129] * dot(hot_refs[1][...], rows)
+        total = gate_ref[:, :1] * total[:n_rows] + gate_ref[:, 128:129] * total[n_rows:]
     if arrived:
         total = total + jnp.concatenate([ref[...].astype(F32) for ref in arrived], axis=0)
     at = 0
@@ -328,27 +284,26 @@
 
 
 def combine(
-    me, routing, blocks, block, chunk, gated=False, offset=0, arrived=(), wait_for=(), parts=None
+    me, routing, blocks, block, chunk, gated=False, arrived=(), wait_for=(), parts=None
 ):
     n_rows = routing.shape[0]
     groups = len(blocks)
-    depth, width = blocks[0].shape
+    width = blocks[0].shape[1]
     by_rows = lambda n: pl.BlockSpec((n, chunk), lambda d, me: (0, d))
     results = pl.pallas_call(
         functools.partial(
-            combine_kernel, groups, block, offset, gated, len(arrived), len(wait_for)
+            combine_kernel, groups, block, gated, len(arrived), len(wait_for)
         ),
         grid_spec=pltpu.PrefetchScalarGridSpec(
             num_scalar_prefetch=1,
             grid=(width // chunk,),
             in_specs=[pl.BlockSpec(routing.shape, lambda d, me: (0, 0))]
-            + [by_rows(depth) for _ in blocks]
-            + [by_rows(part.shape[0]) for part in arrived]
+            + [by_rows(block) for _ in blocks]
+            + [by_rows(rows.shape[0]) for rows in arrived]
             + [pl.BlockSpec(memory_space=pl.ANY) for _ in wait_for],
             out_specs=[by_rows(n) for n in parts or (n_rows,)],
             scratch_shapes=[
-                pltpu.VMEM((n_rows, groups * block), BF16),
-                pltpu.VMEM((n_rows, groups * block), BF16),
+                pltpu.VMEM(((2 if gated else 1) * n_rows, groups * block), BF16),
                 pltpu.VMEM((n_rows, 256), F32),
             ],
         ),
@@ -360,17 +315,16 @@
     return results if parts else results[0]
 
 
-def weight_kernel(n_dp, rows, traded_ref, pre_ref, hidden_ref, up_ref, down_ref):
-    sums = [None, None]
-    for d in range(n_dp):
-        for i, factor_ref in enumerate((pre_ref, hidden_ref)):
+def weight_kernel(n_dp, rows, traded_ref, pre_ref, hidden_ref, *outs):
+    for i, factor_ref in enumerate((pre_ref, hidden_ref)):
+        total = None
+        for d in range(n_dp):
             part = contract_rows(
                 traded_ref[d, i * rows : (i + 1) * rows, :],
                 factor_ref[d * rows : (d + 1) * rows, :],
             )
-            sums[i] = part if d == 0 else sums[i] + part
-    up_ref[0] = sums[0].astype(BF16)
-    down_ref[0] = sums[1].astype(BF16)
+            total = part if d == 0 else total + part
+        outs[i][0] = total.astype(BF16)
 
 
 def weight_grads(traded, pre_all, hidden_all, lanes):
@@ -422,7 +376,7 @@
     capacity = max(2, 12 * n_rows // (5 * n_expert))
     block = -(-capacity // ROW_TILE) * ROW_TILE
     half = n_expert // 2
-    chunk = width // n_dp
+    chunk = width // 2
     me = lax.axis_index("expert").astype(I32).reshape(1)
     first = jnp.zeros((1,), I32)
 
@@ -440,10 +394,10 @@
     place = (first, turned(routing))
     rows_out = dispatch(*place, tokens, n_expert, block, chunk)
     rows_in = swap_direct(rows_out)
-    grads_out = dispatch(*place, grad_out, n_expert, block, chunk, gated=True, wait_for=(rows_out, far_routing))
-    grads_in = swap_direct(after(grads_out, rows_in))
-
-    out, sent, hidden, pre_act = forward(me, rows_in, up_weight, down_weight, n_dp)
+    grads_out = dispatch(*place, grad_out, n_expert, block, chunk, gated=True, wait_for=(rows_out,))
+    grads_in = swap_direct(after(grads_out, far_routing))
+
+    out, sent, hidden, pre_act = expert(me, rows_in, up_weight, down_weight, n_dp)
     parts = (n_rows // 4, n_rows - n_rows // 4)
     far_mixed = combine(
         me, far_routing, exchange(out[half:]), block, chunk, gated=True, parts=parts
@@ -451,21 +405,21 @@
     mixed_in = [permute_xor(far_mixed[0], "expert", half)]
     mixed_in.append(permute_xor(after(far_mixed[1], mixed_in[0]), "expert", half))
 
-    near_back, far_back, sent, pre_grad = backward(
-        me, grads_in, pre_act, down_weight, up_weight, n_dp, out[:half], sent, far_mixed[0]
-    )
-    far_back = exchange([after(rows, mixed_in[0]) for rows in far_back])
+    row_grads, sent, pre_grad = expert(
+        me, grads_in, down_weight, up_weight, n_dp, pre=pre_act, sent=sent, wait_for=far_mixed[0]
+    )
+    far_back = exchange([after(rows, mixed_in[0]) for rows in row_grads[half:]])
     far_sum = combine(me, far_routing, far_back, block, chunk, wait_for=(mixed_in[1],))
     sum_in = permute_xor(far_sum, "expert", half)
-    near_back = exchange([after(rows, *far_back[1:]) for rows in near_back])
+    near_back = exchange([after(rows, *far_back[1:]) for rows in out[:half]])
+    near_grad = exchange([after(rows, far_sum) for rows in row_grads[:half]])
     traded = lax.all_to_all(
         after(sent, mixed_in[0]), "dp", split_axis=0, concat_axis=0, tiled=True
     )
-    pre_grad = after(pre_grad, mixed_in[0])
     hidden_all = lax.all_gather(hidden, "dp", axis=0, tiled=True)
-    pre_all = lax.all_gather(pre_grad, "dp", axis=0, tiled=True)
-
-    grad_up, grad_down = weight_grads(traded, pre_all, hidden_all, chunk // 5)
+    pre_all = lax.all_gather(after(pre_grad, mixed_in[0]), "dp", axis=0, tiled=True)
+
+    grad_up, grad_down = weight_grads(traded, pre_all, hidden_all, 256)
     layer_output = combine(
         me,
         routing,
@@ -477,14 +431,7 @@
         wait_for=(grad_up, grad_down),
     )
     grad_tokens = combine(
-        me,
-        routing,
-        near_back,
-        block,
-        chunk,
-        offset=block,
-        arrived=(sum_in,),
-        wait_for=(layer_output,),
+        me, routing, near_grad, block, chunk, arrived=(sum_in,), wait_for=(layer_output,)
     )
     return (layer_output, grad_tokens, grad_up, grad_down)
 

time: 350 us -> 330 us (0.943)
  waiting for transfers between devices: 219 us -> 200 us
  starting transfers between devices: 36.6 us -> 51.5 us
  Pallas kernels: 72.8 us -> 61.2 us
  local copies, waits for them, and re-layouts: 6.63 us -> 1.34 us
    all_to_all x1, waiting for transfers between devices: 28.4 us -> 0.01 us  [local(): lax.all_to_all(after(sent, mixed_in[0]), 'dp', split_axis=0, concat_axis=...]
    all_gather x1, waiting for transfers between devices: 0.02 us -> 22.7 us  [local(): down_weight = lax.all_gather(w_down, 'dp', axis=1, tiled=True)[0]]
    all_gather x1, waiting for transfers between devices: 15.2 us -> 0.02 us  [local(): up_weight = lax.all_gather(w_up, 'dp', axis=1, tiled=True)[0]]
    ppermute x13 -> x16, starting transfers between devices: 19.4 us -> 34.2 us  [permute_xor(): return lax.ppermute(values, axis, [(i, i ^ mask) for i in range(size)])]
    pallas_call x6, Pallas kernels: 50.6 us -> 41.1 us  [the longest x2 27 us: expert(): pl.pallas_call(functools.partial(expert_kernel, n, n_chunks, backward), i...]
    unnamed x32 -> x10, local copies, waits for them, and re-layouts: 5.92 us -> 0.02 us
    ppermute x13 -> x16, waiting for transfers between devices: 173 us -> 176 us  [permute_xor(): return lax.ppermute(values, axis, [(i, i ^ mask) for i in range(size)])]
  transfers between devices with their start and end apart: 20 -> 23, of which waited for: 11 -> 11; matrix products, arithmetic and copies ran while one was open for 0% -> 1% of each run, Pallas kernels for 19% -> 18%
where the time goes in v3:
time: 330 us; the launch traced here: 329 us
  waiting for transfers between devices  200 us (61%)
  Pallas kernels  61.2 us (19%)
  starting transfers between devices  51.5 us (16%)
  between operations  13.9 us (4%)
    ppermute x16, waiting for transfers between devices, permute_xor(): return lax.ppermute(values, axis, [(i, i ^ mask) for i in range(size)])  176 us
    ppermute x16, starting transfers between devices, permute_xor(): return lax.ppermute(values, axis, [(i, i ^ mask) for i in range(size)])  34.2 us
    pallas_call x2, Pallas kernels, expert(): pl.pallas_call(functools.partial(expert_kernel, n, n_chunks, backward), i...  27 us
    all_gather x1, waiting for transfers between devices, local(): down_weight = lax.all_gather(w_down, 'dp', axis=1, tiled=True)[0]  22.7 us
    pallas_call x4, Pallas kernels, combine(): pl.pallas_call(functools.partial(combine_kernel, groups, block, gated, le...  14.1 us
    pallas_call x1, Pallas kernels, weight_grads(): pl.pallas_call(functools.partial(weight_kernel, n_dp, depth // 2), grid=(...  12.6 us
    all_to_all x2, starting transfers between devices, swap_direct(): lax.all_to_all(blocks, 'expert', split_axis=0, concat_axis=0, tiled=True)  11.9 us
    pallas_call x2, Pallas kernels, dispatch(): pl.pallas_call(functools.partial(dispatch_kernel, groups, block, gated, l...  7.44 us
  transfers between devices with their start and end apart: 23, of which 11 were waited for; matrix products, arithmetic and copies ran while one was open for 1% of the time, Pallas kernels for 18%

profile of v3, /device:TPU:0, one launch (start us, length us, event | category | flops | bytes accessed | tf_op | source)
XLA Modules:
  0.0 329.1 jit_solution(4870506014824708892)
XLA Ops:
  9.9 3.6 %dispatch.2.refs_1_ = bf16[8,40,5120]{2,1,0:T(8,128)(2,1)} custom-call(s32[1]{0:T(128)} %constant.1.clone.1.me_ref, s32[8,128]{1,0:T(8,128)} %pad.4.routing_ref, bf16[128,5120]{1,0:T(8,128)(2,1)} %refs_0_.2), custom_call_target="tpu_custom_call" | custom-call | flops 1 | bytes 1 | tf_op jit(solution)/shard_map/dispatch/pallas_call | solution.py:129
  13.5 7.4 %all-to-all-start = ((bf16[8,40,5120]{2,1,0:T(8,128)(2,1)}), bf16[8,40,5120]{2,1,0:T(8,128)(2,1)}, u32[]{:S(2)}, u32[]{:S(2)}) async-start(bf16[8,40,5120]{2,1,0:T(8,128)(2,1)} %dispatch.2.refs_1_), calls=%async_computation | async-start | bytes 6553600 | tf_op jit(solution)/shard_map/all_to_all | solution.py:387
  21.6 2.9 collective-permute-start
  24.5 3.8 %dispatch.3.refs_0_ = bf16[8,40,5120]{2,1,0:T(8,128)(2,1)} custom-call(s32[1]{0:T(128)} %constant.1.clone.1.me_ref, s32[8,128]{1,0:T(8,128)} %pad.4.routing_ref, bf16[128,5120]{1,0:T(8,128)(2,1)} %refs_0_.3, bf16[8,40,5120]{2,1,0:T(8,128)(2,1)} %dispatch.2.refs_1_), custom_call_target="tpu_custom_call" | custom-call | flops 1 | bytes 1 | tf_op jit(solution)/shard_map/dispatch/pallas_call | solution.py:129
  28.4 69.0 %collective-permute-done.refs_1_.routing_ref = s32[128,4]{1,0:T(8,128)} collective-permute-done((s32[128,4]{1,0:T(8,128)}, s32[128,4]{1,0:T(8,128)}, u32[]{:S(2)}, u32[]{:S(2)}) %collective-permute-start) | collective-permute-done | bytes 2080 | tf_op jit(solution)/shard_map/ppermute | solution.py:365
  97.3 4.5 %all-to-all-start.1 = ((bf16[8,40,5120]{2,1,0:T(8,128)(2,1)}), bf16[8,40,5120]{2,1,0:T(8,128)(2,1)}, u32[]{:S(2)}, u32[]{:S(2)}) async-start(bf16[8,40,5120]{2,1,0:T(8,128)(2,1)} %after.16), calls=%async_computation.1 | async-start | bytes 6553600 | tf_op jit(solution)/shard_map/all_to_all | solution.py:387
  101.9 22.7 %all-gather.7.cloned.1.call-done = bf16[1,5120,768]{2,1,0:T(8,128)(2,1)} async-done(((bf16[1,1280,768]{2,1,0:T(8,128)(2,1)}), bf16[1,5120,768]{2,1,0:T(8,128)(2,1)}) %all-gather.7.cloned.1.call-update) | async-done | bytes 7864336 | tf_op jit(solution)/shard_map/all_gather | solution.py:392
  124.5 13.0 %expert_forward.1 = (bf16[40,5120]{1,0:T(8,128)(2,1)}, bf16[40,5120]{1,0:T(8,128)(2,1)}, bf16[40,5120]{1,0:T(8,128)(2,1)}, bf16[40,5120]{1,0:T(8,128)(2,1)}, bf1...) custom-call(s32[1]{0:T(128)} %bitcast.refs_0_.me_ref, ...), custom_call_target="tpu_custom_call" | custom-call | flops 1 | bytes 1 | tf_op jit(solution)/shard_map/expert_forward/pallas_call | solution.py:228
  137.6 1.5 collective-permute-start.1
  139.1 1.5 collective-permute-start.2
  141.1 16.6 %collective-permute-done.1.refs_1_ = bf16[40,5120]{1,0:T(8,128)(2,1)} collective-permute-done((bf16[40,5120]{1,0:T(8,128)(2,1)}, bf16[40,5120]{1,0:T(8,128)(2,1)}, u32[]{:S(2)}, u32[]{:S(2)}) %collective-permute-start.1) | collective-permute-done | bytes 409632 | tf_op jit(solution)/shard_map/ppermute | solution.py:365
  157.7 7.8 %collective-permute-done.2.refs_2_ = bf16[40,5120]{1,0:T(8,128)(2,1)} collective-permute-done((bf16[40,5120]{1,0:T(8,128)(2,1)}, bf16[40,5120]{1,0:T(8,128)(2,1)}, u32[]{:S(2)}, u32[]{:S(2)}) %collective-permute-start.2) | collective-permute-done | bytes 409632 | tf_op jit(solution)/shard_map/ppermute | solution.py:365
  165.5 10.4 %collective-permute-done.3.refs_3_ = bf16[40,5120]{1,0:T(8,128)(2,1)} collective-permute-done((bf16[40,5120]{1,0:T(8,128)(2,1)}, bf16[40,5120]{1,0:T(8,128)(2,1)}, u32[]{:S(2)}, u32[]{:S(2)}) %collective-permute-start.3) | collective-permute-done | bytes 409632 | tf_op jit(solution)/shard_map/ppermute | solution.py:365
  175.8 3.5 %combine.4 = (bf16[32,5120]{1,0:T(8,128)(2,1)}, bf16[96,5120]{1,0:T(8,128)(2,1)}) custom-call(s32[1]{0:T(128)} %bitcast.refs_0_.me_ref, s32[128,4]{1,0:T(8,128)} %collective-permute-done.refs_1_.routing_ref, bf16[40,5120]{1,0:T(8,128)(2,1)} %get-tuple-element.32.refs_0_, bf16[40,5120]{1,0:T(8,128)(2,1)} %collective-permute-done.1.refs_1_, ...), custom_call_target="tpu_custom_call" | custom-call | flops 1 | bytes 1 | tf_op jit(solution)/shard_map/combine/pallas_call | solution.py:293
  179.4 2.7 collective-permute-start.4
  182.0 14.0 %expert_backward.1 = (bf16[40,5120]{1,0:T(8,128)(2,1)}, bf16[40,5120]{1,0:T(8,128)(2,1)}, bf16[40,5120]{1,0:T(8,128)(2,1)}, bf16[40,5120]{1,0:T(8,128)(2,1)}, bf...) custom-call(s32[1]{0:T(128)} %bitcast.refs_0_.me_ref, ...), custom_call_target="tpu_custom_call", output_to_operand_aliasing={{8}: (5, {})} | custom-call | flops 1 | bytes 1 | tf_op jit(solution)/shard_map/expert_backward/pallas_call | solution.py:228
  196.1 5.3 %all-to-all-start.2 = ((bf16[4,640,1280]{2,1,0:T(8,128)(2,1)}), bf16[4,640,1280]{2,1,0:T(8,128)(2,1)}, u32[]{:S(2)}, u32[]{:S(2)}) async-start(bf16[4,640,1280]{2,1,0:T(8,128)(2,1)} %after.25), calls=%async_computation.2 | async-start | bytes 13107200 | tf_op jit(solution)/shard_map/all_to_all | solution.py:416
  202.3 3.2 collective-permute-start.7
  206.2 27.4 %collective-permute-done.7.refs_3_ = bf16[40,5120]{1,0:T(8,128)(2,1)} collective-permute-done((bf16[40,5120]{1,0:T(8,128)(2,1)}, bf16[40,5120]{1,0:T(8,128)(2,1)}, u32[]{:S(2)}, u32[]{:S(2)}) %collective-permute-start.7) | collective-permute-done | bytes 409632 | tf_op jit(solution)/shard_map/ppermute | solution.py:365
  233.5 8.3 %collective-permute-done.6.refs_2_ = bf16[40,5120]{1,0:T(8,128)(2,1)} collective-permute-done((bf16[40,5120]{1,0:T(8,128)(2,1)}, bf16[40,5120]{1,0:T(8,128)(2,1)}, u32[]{:S(2)}, u32[]{:S(2)}) %collective-permute-start.6) | collective-permute-done | bytes 409632 | tf_op jit(solution)/shard_map/ppermute | solution.py:365
  241.9 4.0 %collective-permute-done.11.refs_5_.refs_4_ = bf16[96,5120]{1,0:T(8,128)(2,1)} collective-permute-done((bf16[96,5120]{1,0:T(8,128)(2,1)}, bf16[96,5120]{1,0:T(8,128)(2,1)}, u32[]{:S(2)}, u32[]{:S(2)}) %collective-permute-start.11) | collective-permute-done | bytes 983072 | tf_op jit(solution)/shard_map/ppermute | solution.py:365
  245.9 3.2 combine.6.refs_1_
  249.1 5.9 %collective-permute-start.10 = (bf16[40,5120]{1,0:T(8,128)(2,1)}, bf16[40,5120]{1,0:T(8,128)(2,1)S(1)}, u32[]{:S(2)}, u32[]{:S(2)}) collective-permute-start(bf16[40,5120]{1,0:T(8,128)(2,1)} %after.23), channel_id=1, source_target_pairs={{0,3},{1,2},{2,1},{3,0},{4,7},{5,6},{6,5},{7,4},{8,11},{9,10},{10,... | collective-permute-start | bytes 1228808 | tf_op jit(solution)/shard_map/ppermute | solution.py:365
  255.6 2.9 collective-permute-start.14
  258.5 28.8 %collective-permute-done.10.refs_3_ = bf16[40,5120]{1,0:T(8,128)(2,1)S(1)} collective-permute-done((bf16[40,5120]{1,0:T(8,128)(2,1)}, bf16[40,5120]{1,0:T(8,128)(2,1)S(1)}, u32[]{:S(2)}, u32[]{:S(2)}) %collective-permute-start.10) | collective-permute-done | bytes 409632 | tf_op jit(solution)/shard_map/ppermute | solution.py:365
  287.3 6.6 %collective-permute-start.13 = (bf16[40,5120]{1,0:T(8,128)(2,1)}, bf16[40,5120]{1,0:T(8,128)(2,1)}, u32[]{:S(2)}, u32[]{:S(2)}) collective-permute-start(bf16[40,5120]{1,0:T(8,128)(2,1)} %after.30), channel_id=1, source_target_pairs={{0,2},{1,3},{2,0},{3,1},{4,6},{5,7},{6,4},{7,5},{8,10},{9,11},{10,... | collective-permute-start | bytes 1228808 | tf_op jit(solution)/shard_map/ppermute | solution.py:365
  294.0 2.1 collective-permute-done.9.refs_2_
  296.1 4.8 %collective-permute-start.12 = (bf16[40,5120]{1,0:T(8,128)(2,1)}, bf16[40,5120]{1,0:T(8,128)(2,1)}, u32[]{:S(2)}, u32[]{:S(2)}) collective-permute-start(bf16[40,5120]{1,0:T(8,128)(2,1)} %after.29), channel_id=1, source_target_pairs={{0,1},{1,0},{2,3},{3,2},{4,5},{5,4},{6,7},{7,6},{8,9},{9,8},{10,11... | collective-permute-start | bytes 1228808 | tf_op jit(solution)/shard_map/ppermute | solution.py:365
  301.0 12.6 %weight_grads.1 = (bf16[1,1280,768]{2,1,0:T(8,128)(2,1)}, bf16[1,1280,768]{2,1,0:T(8,128)(2,1)}) custom-call(bf16[4,640,1280]{2,1,0:T(8,128)(2,1)} %all-to-all-done.2.traded_ref, bf16[1280,768]{1,0:T(8,128)(2,1)} %all-gather.9.cloned.1.call-done.pre_ref, bf16[1280,768]{1,0:T(8,128)(2,1)} %all-gather.11.cloned.1.call-done.hidden_ref), custom_call_target="tpu_custom_call" | custom-call | flops 1 | bytes 1 | tf_op jit(solution)/shard_map/weight_grads/pallas_call | solution.py:334
  313.6 3.9 %combine.5.refs_5_ = bf16[128,5120]{1,0:T(8,128)(2,1)} custom-call(s32[1]{0:T(128)} %bitcast.refs_0_.me_ref, s32[128,4]{1,0:T(8,128)} %copy.32.routing_ref, bf16[40,5120]{1,0:T(8,128)(2,1)} %after.20.refs_0_, bf16[40,5120]{1,0:T(8,128)(2,1)} %collective-permute-done.8.refs_1_, bf16[40,5120]{1,0:T(8,128)(2,1)} %copy-done.1, bf16[40,5120]{1,0:T(8,128)(2,1)} %copy-done, ...), custom_call_target="tpu_custom_call" | custom-call | flops 1 | bytes 1 | tf_op jit(solution)/shard_map/combine/pallas_call | solution.py:293
  317.5 1.5 collective-permute-done.13.refs_2_
  319.1 3.5 %combine.7 = bf16[128,5120]{1,0:T(8,128)(2,1)} custom-call(s32[1]{0:T(128)} %bitcast.refs_0_.me_ref, s32[128,4]{1,0:T(8,128)} %copy.32.routing_ref, bf16[40,5120]{1,0:T(8,128)(2,1)} %after.28.refs_0_, bf16[40,5120]{1,0:T(8,128)(2,1)} %collective-permute-done.12.refs_1_, bf16[40,5120]{1,0:T(8,128)(2,1)} %collective-permute-done.13.refs_2_, ...), custom_call_target="tpu_custom_call" | custom-call | flops 1 | bytes 1 | tf_op jit(solution)/shard_map/combine/pallas_call | solution.py:293
  (56 shorter events, 6.2 us)
Async XLA Ops:
  7.2 1.5 copy-start.4
  7.2 1.5 copy-start.3
  7.2 94.7 %all-gather.5.cloned.1.call-start = ((), (), s32[]{:S(2)}) async-start(), calls=%async_computation.3 | async-start | bytes 9830400 | tf_op jit(solution)/shard_map/all_gather | solution.py:391
  7.9 116.6 %all-gather.7.cloned.1.call-start = ((), (), s32[]{:S(2)}) async-start(), calls=%async_computation.4 | async-start | bytes 9830400 | tf_op jit(solution)/shard_map/all_gather | solution.py:392
  13.5 7.4 %copy-start.2 = (s32[128,4]{0,1:T(4,128)S(1)}, s32[128,4]{0,1:T(4,128)}, u32[]{:S(2)}) copy-start(s32[128,4]{0,1:T(4,128)} %get-tuple-element.55) | copy-start | bytes 6148
  13.5 83.8 %all-to-all-start = ((bf16[8,40,5120]{2,1,0:T(8,128)(2,1)}), bf16[8,40,5120]{2,1,0:T(8,128)(2,1)}, u32[]{:S(2)}, u32[]{:S(2)}) async-start(bf16[8,40,5120]{2,1,0:T(8,128)(2,1)} %dispatch.2.refs_1_), calls=%async_computation | async-start | bytes 6553600 | tf_op jit(solution)/shard_map/all_to_all | solution.py:387
  21.6 75.7 %collective-permute-start = (s32[128,4]{1,0:T(8,128)}, s32[128,4]{1,0:T(8,128)}, u32[]{:S(2)}, u32[]{:S(2)}) collective-permute-start(s32[128,4]{1,0:T(8,128)} %copy.32.routing_ref), channel_id=1, source_target_pairs={{0,4},{1,5},{2,6},{3,7},{4,0},{5,1},{6,2},{7,3},{8,12},{9,13},{10,... | collective-permute-start | bytes 6152 | tf_op jit(solution)/shard_map/ppermute | solution.py:365
  97.3 84.7 %all-to-all-start.1 = ((bf16[8,40,5120]{2,1,0:T(8,128)(2,1)}), bf16[8,40,5120]{2,1,0:T(8,128)(2,1)}, u32[]{:S(2)}, u32[]{:S(2)}) async-start(bf16[8,40,5120]{2,1,0:T(8,128)(2,1)} %after.16), calls=%async_computation.1 | async-start | bytes 6553600 | tf_op jit(solution)/shard_map/all_to_all | solution.py:387
  101.8 199.2 %all-gather.11.cloned.1.call-start = ((), (), s32[]{:S(2)}) async-start(), calls=%async_computation.6 | async-start | bytes 2457600 | tf_op jit(solution)/shard_map/all_gather | solution.py:419
  137.6 20.1 %collective-permute-start.1 = (bf16[40,5120]{1,0:T(8,128)(2,1)}, bf16[40,5120]{1,0:T(8,128)(2,1)}, u32[]{:S(2)}, u32[]{:S(2)}) collective-permute-start(bf16[40,5120]{1,0:T(8,128)(2,1)} %get-tuple-element.33), channel_id=1, source_target_pairs={{0,1},{1,0},{2,3},{3,2},{4,5},{5,4},{6,7},{7,6},{8,9},{9,8},{10,11... | collective-permute-start | bytes 1228808 | tf_op jit(solution)/shard_map/ppermute | solution.py:365
  139.1 26.4 %collective-permute-start.2 = (bf16[40,5120]{1,0:T(8,128)(2,1)}, bf16[40,5120]{1,0:T(8,128)(2,1)}, u32[]{:S(2)}, u32[]{:S(2)}) collective-permute-start(bf16[40,5120]{1,0:T(8,128)(2,1)} %get-tuple-element.34), channel_id=1, source_target_pairs={{0,2},{1,3},{2,0},{3,1},{4,6},{5,7},{6,4},{7,5},{8,10},{9,11},{10,... | collective-permute-start | bytes 1228808 | tf_op jit(solution)/shard_map/ppermute | solution.py:365
  140.6 35.3 %collective-permute-start.3 = (bf16[40,5120]{1,0:T(8,128)(2,1)}, bf16[40,5120]{1,0:T(8,128)(2,1)}, u32[]{:S(2)}, u32[]{:S(2)}) collective-permute-start(bf16[40,5120]{1,0:T(8,128)(2,1)} %get-tuple-element.35), channel_id=1, source_target_pairs={{0,3},{1,2},{2,1},{3,0},{4,7},{5,6},{6,5},{7,4},{8,11},{9,10},{10,... | collective-permute-start | bytes 1228808 | tf_op jit(solution)/shard_map/ppermute | solution.py:365
  179.4 16.7 %collective-permute-start.4 = (bf16[32,5120]{1,0:T(8,128)(2,1)}, bf16[32,5120]{1,0:T(8,128)(2,1)}, u32[]{:S(2)}, u32[]{:S(2)}) collective-permute-start(bf16[32,5120]{1,0:T(8,128)(2,1)} %get-tuple-element.36.refs_6_), channel_id=1, source_target_pairs={{0,4},{1,5},{2,6},{3,7},{4,0},{5,1},{6,2},{7,3},{8,12},{9,13},{10,... | collective-permute-start | bytes 983048 | tf_op jit(solution)/shard_map/ppermute | solution.py:365
  196.1 104.9 %all-to-all-start.2 = ((bf16[4,640,1280]{2,1,0:T(8,128)(2,1)}), bf16[4,640,1280]{2,1,0:T(8,128)(2,1)}, u32[]{:S(2)}, u32[]{:S(2)}) async-start(bf16[4,640,1280]{2,1,0:T(8,128)(2,1)} %after.25), calls=%async_computation.2 | async-start | bytes 13107200 | tf_op jit(solution)/shard_map/all_to_all | solution.py:416
  201.4 99.6 %all-gather.9.cloned.1.call-start = ((), (), s32[]{:S(2)}) async-start(), calls=%async_computation.5 | async-start | bytes 2457600 | tf_op jit(solution)/shard_map/all_gather | solution.py:420
  202.0 43.9 %collective-permute-start.11 = (bf16[96,5120]{1,0:T(8,128)(2,1)}, bf16[96,5120]{1,0:T(8,128)(2,1)}, u32[]{:S(2)}, u32[]{:S(2)}) collective-permute-start(bf16[96,5120]{1,0:T(8,128)(2,1)} %after.24), channel_id=1, source_target_pairs={{0,4},{1,5},{2,6},{3,7},{4,0},{5,1},{6,2},{7,3},{8,12},{9,13},{10,... | collective-permute-start | bytes 2949128 | tf_op jit(solution)/shard_map/ppermute | solution.py:365
  202.3 31.2 %collective-permute-start.7 = (bf16[40,5120]{1,0:T(8,128)(2,1)}, bf16[40,5120]{1,0:T(8,128)(2,1)}, u32[]{:S(2)}, u32[]{:S(2)}) collective-permute-start(bf16[40,5120]{1,0:T(8,128)(2,1)} %after.19), channel_id=1, source_target_pairs={{0,3},{1,2},{2,1},{3,0},{4,7},{5,6},{6,5},{7,4},{8,11},{9,10},{10,... | collective-permute-start | bytes 1228808 | tf_op jit(solution)/shard_map/ppermute | solution.py:365
  205.5 36.4 %collective-permute-start.6 = (bf16[40,5120]{1,0:T(8,128)(2,1)}, bf16[40,5120]{1,0:T(8,128)(2,1)}, u32[]{:S(2)}, u32[]{:S(2)}) collective-permute-start(bf16[40,5120]{1,0:T(8,128)(2,1)} %after.18), channel_id=1, source_target_pairs={{0,2},{1,3},{2,0},{3,1},{4,6},{5,7},{6,4},{7,5},{8,10},{9,11},{10,... | collective-permute-start | bytes 1228808 | tf_op jit(solution)/shard_map/ppermute | solution.py:365
  205.8 36.1 %collective-permute-start.5 = (bf16[40,5120]{1,0:T(8,128)(2,1)}, bf16[40,5120]{1,0:T(8,128)(2,1)}, u32[]{:S(2)}, u32[]{:S(2)}) collective-permute-start(bf16[40,5120]{1,0:T(8,128)(2,1)} %after.17), channel_id=1, source_target_pairs={{0,1},{1,0},{2,3},{3,2},{4,5},{5,4},{6,7},{7,6},{8,9},{9,8},{10,11... | collective-permute-start | bytes 1228808 | tf_op jit(solution)/shard_map/ppermute | solution.py:365
  249.1 70.0 %collective-permute-start.15 = (bf16[128,5120]{1,0:T(8,128)(2,1)}, bf16[128,5120]{1,0:T(8,128)(2,1)}, u32[]{:S(2)}, u32[]{:S(2)}) collective-permute-start(bf16[128,5120]{1,0:T(8,128)(2,1)} %combine.6.refs_1_), channel_id=1, source_target_pairs={{0,4},{1,5},{2,6},{3,7},{4,0},{5,1},{6,2},{7,3},{8,12},{9,13},{10,... | collective-permute-start | bytes 3932168 | tf_op jit(solution)/shard_map/ppermute | solution.py:365
  249.1 38.2 %collective-permute-start.10 = (bf16[40,5120]{1,0:T(8,128)(2,1)}, bf16[40,5120]{1,0:T(8,128)(2,1)S(1)}, u32[]{:S(2)}, u32[]{:S(2)}) collective-permute-start(bf16[40,5120]{1,0:T(8,128)(2,1)} %after.23), channel_id=1, source_target_pairs={{0,3},{1,2},{2,1},{3,0},{4,7},{5,6},{6,5},{7,4},{8,11},{9,10},{10,... | collective-permute-start | bytes 1228808 | tf_op jit(solution)/shard_map/ppermute | solution.py:365
  255.0 41.1 %collective-permute-start.9 = (bf16[40,5120]{1,0:T(8,128)(2,1)}, bf16[40,5120]{1,0:T(8,128)(2,1)S(1)}, u32[]{:S(2)}, u32[]{:S(2)}) collective-permute-start(bf16[40,5120]{1,0:T(8,128)(2,1)} %after.22), channel_id=1, source_target_pairs={{0,2},{1,3},{2,0},{3,1},{4,6},{5,7},{6,4},{7,5},{8,10},{9,11},{10,... | collective-permute-start | bytes 1228808 | tf_op jit(solution)/shard_map/ppermute | solution.py:365
  255.4 58.3 %collective-permute-start.8 = (bf16[40,5120]{1,0:T(8,128)(2,1)}, bf16[40,5120]{1,0:T(8,128)(2,1)}, u32[]{:S(2)}, u32[]{:S(2)}) collective-permute-start(bf16[40,5120]{1,0:T(8,128)(2,1)} %after.21), channel_id=1, source_target_pairs={{0,1},{1,0},{2,3},{3,2},{4,5},{5,4},{6,7},{7,6},{8,9},{9,8},{10,11... | collective-permute-start | bytes 1228808 | tf_op jit(solution)/shard_map/ppermute | solution.py:365
  255.6 62.0 %collective-permute-start.14 = (bf16[40,5120]{1,0:T(8,128)(2,1)}, bf16[40,5120]{1,0:T(8,128)(2,1)}, u32[]{:S(2)}, u32[]{:S(2)}) collective-permute-start(bf16[40,5120]{1,0:T(8,128)(2,1)} %after.31), channel_id=1, source_target_pairs={{0,3},{1,2},{2,1},{3,0},{4,7},{5,6},{6,5},{7,4},{8,11},{9,10},{10,... | collective-permute-start | bytes 1228808 | tf_op jit(solution)/shard_map/ppermute | solution.py:365
  287.3 13.6 %copy-start = (bf16[40,5120]{1,0:T(8,128)(2,1)}, bf16[40,5120]{1,0:T(8,128)(2,1)S(1)}, u32[]{:S(2)}) copy-start(bf16[40,5120]{1,0:T(8,128)(2,1)S(1)} %collective-permute-done.10.refs_3_) | copy-start | bytes 1228804
  287.3 31.7 %collective-permute-start.13 = (bf16[40,5120]{1,0:T(8,128)(2,1)}, bf16[40,5120]{1,0:T(8,128)(2,1)}, u32[]{:S(2)}, u32[]{:S(2)}) collective-permute-start(bf16[40,5120]{1,0:T(8,128)(2,1)} %after.30), channel_id=1, source_target_pairs={{0,2},{1,3},{2,0},{3,1},{4,6},{5,7},{6,4},{7,5},{8,10},{9,11},{10,... | collective-permute-start | bytes 1228808 | tf_op jit(solution)/shard_map/ppermute | solution.py:365
  296.1 4.8 %copy-start.1 = (bf16[40,5120]{1,0:T(8,128)(2,1)}, bf16[40,5120]{1,0:T(8,128)(2,1)S(1)}, u32[]{:S(2)}) copy-start(bf16[40,5120]{1,0:T(8,128)(2,1)S(1)} %collective-permute-done.9.refs_2_) | copy-start | bytes 1228804
  296.1 23.0 %collective-permute-start.12 = (bf16[40,5120]{1,0:T(8,128)(2,1)}, bf16[40,5120]{1,0:T(8,128)(2,1)}, u32[]{:S(2)}, u32[]{:S(2)}) collective-permute-start(bf16[40,5120]{1,0:T(8,128)(2,1)} %after.29), channel_id=1, source_target_pairs={{0,1},{1,0},{2,3},{3,2},{4,5},{5,4},{6,7},{7,6},{8,9},{9,8},{10,11... | collective-permute-start | bytes 1228808 | tf_op jit(solution)/shard_map/ppermute | solution.py:365
Sparse Core Ops, SparseCore 0:
  9.6 58.0 all-gather.4
  69.2 55.3 all-gather.6
  137.7 21.8 all-gather.10
  204.1 33.0 all-gather.8

commit v4 on v3

--- a/solution.py
+++ b/solution.py
@@ -399,25 +399,25 @@
 
     out, sent, hidden, pre_act = expert(me, rows_in, up_weight, down_weight, n_dp)
     parts = (n_rows // 4, n_rows - n_rows // 4)
-    far_mixed = combine(
-        me, far_routing, exchange(out[half:]), block, chunk, gated=True, parts=parts
-    )
+    far_out = exchange(out[half:])
+    far_mixed = combine(me, far_routing, far_out, block, chunk, gated=True, parts=parts)
+    near_back = exchange([after(rows, far_out[1]) for rows in out[:half]])
     mixed_in = [permute_xor(far_mixed[0], "expert", half)]
     mixed_in.append(permute_xor(after(far_mixed[1], mixed_in[0]), "expert", half))
 
     row_grads, sent, pre_grad = expert(
         me, grads_in, down_weight, up_weight, n_dp, pre=pre_act, sent=sent, wait_for=far_mixed[0]
     )
-    far_back = exchange([after(rows, mixed_in[0]) for rows in row_grads[half:]])
+    ready = (mixed_in[0], *near_back[1:])
+    far_back = exchange([after(rows, *ready) for rows in row_grads[half:]])
     far_sum = combine(me, far_routing, far_back, block, chunk, wait_for=(mixed_in[1],))
     sum_in = permute_xor(far_sum, "expert", half)
-    near_back = exchange([after(rows, *far_back[1:]) for rows in out[:half]])
     near_grad = exchange([after(rows, far_sum) for rows in row_grads[:half]])
     traded = lax.all_to_all(
-        after(sent, mixed_in[0]), "dp", split_axis=0, concat_axis=0, tiled=True
+        after(sent, *ready), "dp", split_axis=0, concat_axis=0, tiled=True
     )
     hidden_all = lax.all_gather(hidden, "dp", axis=0, tiled=True)
-    pre_all = lax.all_gather(after(pre_grad, mixed_in[0]), "dp", axis=0, tiled=True)
+    pre_all = lax.all_gather(after(pre_grad, *ready), "dp", axis=0, tiled=True)
 
     grad_up, grad_down = weight_grads(traded, pre_all, hidden_all, 256)
     layer_output = combine(

time: 330 us -> 325 us (0.985)
  starting transfers between devices: 51.5 us -> 40.7 us
  waiting for transfers between devices: 200 us -> 206 us
    all_to_all x1, waiting for transfers between devices: 0.01 us -> 30.3 us  [local(): lax.all_to_all(after(sent, *ready), 'dp', split_axis=0, concat_axis=0, ti...]
    ppermute x16, waiting for transfers between devices: 176 us -> 151 us  [permute_xor(): return lax.ppermute(values, axis, [(i, i ^ mask) for i in range(size)])]
    ppermute x16, starting transfers between devices: 34.2 us -> 23.4 us  [permute_xor(): return lax.ppermute(values, axis, [(i, i ^ mask) for i in range(size)])]
  transfers between devices with their start and end apart: 23 -> 23, of which waited for: 11 -> 12; matrix products, arithmetic and copies ran while one was open for 1% -> 1% of each run, Pallas kernels for 18% -> 18%
where the time goes in v4:
time: 325 us; the launch traced here: 324 us
  waiting for transfers between devices  206 us (63%)
  Pallas kernels  61.1 us (19%)
  starting transfers between devices  40.7 us (13%)
  between operations  13.9 us (4%)
    ppermute x16, waiting for transfers between devices, permute_xor(): return lax.ppermute(values, axis, [(i, i ^ mask) for i in range(size)])  151 us
    all_to_all x1, waiting for transfers between devices, local(): lax.all_to_all(after(sent, *ready), 'dp', split_axis=0, concat_axis=0, ti...  30.3 us
    pallas_call x2, Pallas kernels, expert(): pl.pallas_call(functools.partial(expert_kernel, n, n_chunks, backward), i...  27 us
    ppermute x16, starting transfers between devices, permute_xor(): return lax.ppermute(values, axis, [(i, i ^ mask) for i in range(size)])  23.4 us
    all_gather x1, waiting for transfers between devices, local(): down_weight = lax.all_gather(w_down, 'dp', axis=1, tiled=True)[0]  22.7 us
    pallas_call x4, Pallas kernels, combine(): pl.pallas_call(functools.partial(combine_kernel, groups, block, gated, le...  14.1 us
    pallas_call x1, Pallas kernels, weight_grads(): pl.pallas_call(functools.partial(weight_kernel, n_dp, depth // 2), grid=(...  12.6 us
    all_to_all x2, starting transfers between devices, swap_direct(): lax.all_to_all(blocks, 'expert', split_axis=0, concat_axis=0, tiled=True)  11.9 us
  transfers between devices with their start and end apart: 23, of which 12 were waited for; matrix products, arithmetic and copies ran while one was open for 1% of the time, Pallas kernels for 18%

profile of v4, /device:TPU:0, one launch (start us, length us, event | category | flops | bytes accessed | tf_op | source)
XLA Modules:
  0.0 324.2 jit_solution(11772019848368567037)
XLA Ops:
  9.9 3.6 %dispatch.2.refs_1_ = bf16[8,40,5120]{2,1,0:T(8,128)(2,1)} custom-call(s32[1]{0:T(128)} %constant.1.clone.1.me_ref, s32[8,128]{1,0:T(8,128)} %pad.4.routing_ref, bf16[128,5120]{1,0:T(8,128)(2,1)} %refs_0_.2), custom_call_target="tpu_custom_call" | custom-call | flops 1 | bytes 1 | tf_op jit(solution)/shard_map/dispatch/pallas_call | solution.py:129
  13.5 7.4 %all-to-all-start = ((bf16[8,40,5120]{2,1,0:T(8,128)(2,1)}), bf16[8,40,5120]{2,1,0:T(8,128)(2,1)}, u32[]{:S(2)}, u32[]{:S(2)}) async-start(bf16[8,40,5120]{2,1,0:T(8,128)(2,1)} %dispatch.2.refs_1_), calls=%async_computation | async-start | bytes 6553600 | tf_op jit(solution)/shard_map/all_to_all | solution.py:387
  21.6 2.9 collective-permute-start.4
  24.5 3.8 %dispatch.3.refs_0_ = bf16[8,40,5120]{2,1,0:T(8,128)(2,1)} custom-call(s32[1]{0:T(128)} %constant.1.clone.1.me_ref, s32[8,128]{1,0:T(8,128)} %pad.4.routing_ref, bf16[128,5120]{1,0:T(8,128)(2,1)} %refs_0_.3, bf16[8,40,5120]{2,1,0:T(8,128)(2,1)} %dispatch.2.refs_1_), custom_call_target="tpu_custom_call" | custom-call | flops 1 | bytes 1 | tf_op jit(solution)/shard_map/dispatch/pallas_call | solution.py:129
  28.3 68.9 %collective-permute-done.4.routing_ref.refs_1_ = s32[128,4]{1,0:T(8,128)} collective-permute-done((s32[128,4]{1,0:T(8,128)}, s32[128,4]{1,0:T(8,128)}, u32[]{:S(2)}, u32[]{:S(2)}) %collective-permute-start.4) | collective-permute-done | bytes 2080 | tf_op jit(solution)/shard_map/ppermute | solution.py:365
  97.3 4.5 %all-to-all-start.1 = ((bf16[8,40,5120]{2,1,0:T(8,128)(2,1)}), bf16[8,40,5120]{2,1,0:T(8,128)(2,1)}, u32[]{:S(2)}, u32[]{:S(2)}) async-start(bf16[8,40,5120]{2,1,0:T(8,128)(2,1)} %after.21), calls=%async_computation.1 | async-start | bytes 6553600 | tf_op jit(solution)/shard_map/all_to_all | solution.py:387
  101.8 22.7 %all-gather.7.cloned.1.call-done = bf16[1,5120,768]{2,1,0:T(8,128)(2,1)} async-done(((bf16[1,1280,768]{2,1,0:T(8,128)(2,1)}), bf16[1,5120,768]{2,1,0:T(8,128)(2,1)}) %all-gather.7.cloned.1.call-update) | async-done | bytes 7864336 | tf_op jit(solution)/shard_map/all_gather | solution.py:392
  124.5 13.0 %expert_forward.1 = (bf16[40,5120]{1,0:T(8,128)(2,1)}, bf16[40,5120]{1,0:T(8,128)(2,1)}, bf16[40,5120]{1,0:T(8,128)(2,1)}, bf16[40,5120]{1,0:T(8,128)(2,1)}, bf1...) custom-call(s32[1]{0:T(128)} %bitcast.refs_0_.me_ref, ...), custom_call_target="tpu_custom_call" | custom-call | flops 1 | bytes 1 | tf_op jit(solution)/shard_map/expert_forward/pallas_call | solution.py:228
  137.6 1.5 collective-permute-start
  141.1 16.5 %collective-permute-done.refs_1_ = bf16[40,5120]{1,0:T(8,128)(2,1)S(1)} collective-permute-done((bf16[40,5120]{1,0:T(8,128)(2,1)}, bf16[40,5120]{1,0:T(8,128)(2,1)S(1)}, u32[]{:S(2)}, u32[]{:S(2)}) %collective-permute-start) | collective-permute-done | bytes 409632 | tf_op jit(solution)/shard_map/ppermute | solution.py:365
  158.3 2.1 collective-permute-start.2
  161.8 3.6 %collective-permute-done.5.refs_2_ = bf16[40,5120]{1,0:T(8,128)(2,1)} collective-permute-done((bf16[40,5120]{1,0:T(8,128)(2,1)}, bf16[40,5120]{1,0:T(8,128)(2,1)}, u32[]{:S(2)}, u32[]{:S(2)}) %collective-permute-start.5) | collective-permute-done | bytes 409632 | tf_op jit(solution)/shard_map/ppermute | solution.py:365
  165.5 10.9 %collective-permute-done.6.refs_3_ = bf16[40,5120]{1,0:T(8,128)(2,1)} collective-permute-done((bf16[40,5120]{1,0:T(8,128)(2,1)}, bf16[40,5120]{1,0:T(8,128)(2,1)}, u32[]{:S(2)}, u32[]{:S(2)}) %collective-permute-start.6) | collective-permute-done | bytes 409632 | tf_op jit(solution)/shard_map/ppermute | solution.py:365
  176.4 3.5 %combine.4 = (bf16[32,5120]{1,0:T(8,128)(2,1)}, bf16[96,5120]{1,0:T(8,128)(2,1)}) custom-call(s32[1]{0:T(128)} %bitcast.refs_0_.me_ref, s32[128,4]{1,0:T(8,128)} %collective-permute-done.4.routing_ref.refs_1_, bf16[40,5120]{1,0:T(8,128)(2,1)} %get-tuple-element.34.refs_0_, bf16[40,5120]{1,0:T(8,128)(2,1)} %copy-done, ...), custom_call_target="tpu_custom_call" | custom-call | flops 1 | bytes 1 | tf_op jit(solution)/shard_map/combine/pallas_call | solution.py:293
  179.9 3.2 collective-permute-start.7
  183.0 14.0 %expert_backward.1 = (bf16[40,5120]{1,0:T(8,128)(2,1)}, bf16[40,5120]{1,0:T(8,128)(2,1)}, bf16[40,5120]{1,0:T(8,128)(2,1)}, bf16[40,5120]{1,0:T(8,128)(2,1)}, bf...) custom-call(s32[1]{0:T(128)} %bitcast.refs_0_.me_ref, ...), custom_call_target="tpu_custom_call", output_to_operand_aliasing={{8}: (5, {})} | custom-call | flops 1 | bytes 1 | tf_op jit(solution)/shard_map/expert_backward/pallas_call | solution.py:228
  197.1 3.3 %collective-permute-done.3.refs_4_.refs_3_ = bf16[40,5120]{1,0:T(8,128)(2,1)} collective-permute-done((bf16[40,5120]{1,0:T(8,128)(2,1)}, bf16[40,5120]{1,0:T(8,128)(2,1)}, u32[]{:S(2)}, u32[]{:S(2)}) %collective-permute-start.3) | collective-permute-done | bytes 409632 | tf_op jit(solution)/shard_map/ppermute | solution.py:365
  200.4 5.3 %all-to-all-start.2 = ((bf16[4,640,1280]{2,1,0:T(8,128)(2,1)}), bf16[4,640,1280]{2,1,0:T(8,128)(2,1)}, u32[]{:S(2)}, u32[]{:S(2)}) async-start(bf16[4,640,1280]{2,1,0:T(8,128)(2,1)} %after.22), calls=%async_computation.2 | async-start | bytes 13107200 | tf_op jit(solution)/shard_map/all_to_all | solution.py:416
  206.4 2.7 collective-permute-start.8
  209.1 3.9 %collective-permute-start.10 = (bf16[40,5120]{1,0:T(8,128)(2,1)}, bf16[40,5120]{1,0:T(8,128)(2,1)}, u32[]{:S(2)}, u32[]{:S(2)}) collective-permute-start(bf16[40,5120]{1,0:T(8,128)(2,1)} %after.26), channel_id=1, source_target_pairs={{0,2},{1,3},{2,0},{3,1},{4,6},{5,7},{6,4},{7,5},{8,10},{9,11},{10,... | collective-permute-start | bytes 1228808 | tf_op jit(solution)/shard_map/ppermute | solution.py:365
  213.1 7.9 %collective-permute-done.9.refs_1_ = bf16[40,5120]{1,0:T(8,128)(2,1)} collective-permute-done((bf16[40,5120]{1,0:T(8,128)(2,1)}, bf16[40,5120]{1,0:T(8,128)(2,1)}, u32[]{:S(2)}, u32[]{:S(2)}) %collective-permute-start.9) | collective-permute-done | bytes 409632 | tf_op jit(solution)/shard_map/ppermute | solution.py:365
  220.9 19.4 %collective-permute-done.10.refs_2_ = bf16[40,5120]{1,0:T(8,128)(2,1)} collective-permute-done((bf16[40,5120]{1,0:T(8,128)(2,1)}, bf16[40,5120]{1,0:T(8,128)(2,1)}, u32[]{:S(2)}, u32[]{:S(2)}) %collective-permute-start.10) | collective-permute-done | bytes 409632 | tf_op jit(solution)/shard_map/ppermute | solution.py:365
  240.3 8.3 %collective-permute-done.11.refs_3_ = bf16[40,5120]{1,0:T(8,128)(2,1)} collective-permute-done((bf16[40,5120]{1,0:T(8,128)(2,1)}, bf16[40,5120]{1,0:T(8,128)(2,1)}, u32[]{:S(2)}, u32[]{:S(2)}) %collective-permute-start.11) | collective-permute-done | bytes 409632 | tf_op jit(solution)/shard_map/ppermute | solution.py:365
  248.6 4.2 %collective-permute-done.8.refs_5_.refs_4_ = bf16[96,5120]{1,0:T(8,128)(2,1)} collective-permute-done((bf16[96,5120]{1,0:T(8,128)(2,1)}, bf16[96,5120]{1,0:T(8,128)(2,1)}, u32[]{:S(2)}, u32[]{:S(2)}) %collective-permute-start.8) | collective-permute-done | bytes 983072 | tf_op jit(solution)/shard_map/ppermute | solution.py:365
  252.8 3.2 combine.6.refs_1_
  256.0 1.6 collective-permute-start.12
  257.6 1.7 collective-permute-start.13
  259.6 30.3 %all-to-all-done.2.traded_ref = bf16[4,640,1280]{2,1,0:T(8,128)(2,1)} async-done(((bf16[4,640,1280]{2,1,0:T(8,128)(2,1)}), bf16[4,640,1280]{2,1,0:T(8,128)(2,1)}, u32[]{:S(2)}, u32[]{:S(2)}) %all-to-all-start.2) | async-done | bytes 6553632 | tf_op jit(solution)/shard_map/all_to_all | solution.py:416
  289.8 12.6 %weight_grads.1 = (bf16[1,1280,768]{2,1,0:T(8,128)(2,1)}, bf16[1,1280,768]{2,1,0:T(8,128)(2,1)}) custom-call(bf16[4,640,1280]{2,1,0:T(8,128)(2,1)} %all-to-all-done.2.traded_ref, bf16[1280,768]{1,0:T(8,128)(2,1)} %all-gather.9.cloned.1.call-done.pre_ref, bf16[1280,768]{1,0:T(8,128)(2,1)} %all-gather.11.cloned.1.call-done.hidden_ref), custom_call_target="tpu_custom_call" | custom-call | flops 1 | bytes 1 | tf_op jit(solution)/shard_map/weight_grads/pallas_call | solution.py:334
  302.4 3.9 %combine.5.refs_5_ = bf16[128,5120]{1,0:T(8,128)(2,1)} custom-call(s32[1]{0:T(128)} %bitcast.refs_0_.me_ref, s32[128,4]{1,0:T(8,128)} %copy.32.routing_ref, bf16[40,5120]{1,0:T(8,128)(2,1)} %after.16.refs_0_, bf16[40,5120]{1,0:T(8,128)(2,1)} %collective-permute-done.1.refs_2_.refs_1_, bf16[40,5120]{1,0:T(8,128)(2,1)} %collective-permute-done.2.refs_3_.refs_2_, ...), custom_call_target="tpu_custom_call" | custom-call | flops 1 | bytes 1 | tf_op jit(solution)/shard_map/combine/pallas_call | solution.py:293
  306.3 7.9 %collective-permute-done.15.refs_4_ = bf16[128,5120]{1,0:T(8,128)(2,1)} collective-permute-done((bf16[128,5120]{1,0:T(8,128)(2,1)}, bf16[128,5120]{1,0:T(8,128)(2,1)}, u32[]{:S(2)}, u32[]{:S(2)}) %collective-permute-start.15) | collective-permute-done | bytes 1310752 | tf_op jit(solution)/shard_map/ppermute | solution.py:365
  314.2 3.5 %combine.7 = bf16[128,5120]{1,0:T(8,128)(2,1)} custom-call(s32[1]{0:T(128)} %bitcast.refs_0_.me_ref, s32[128,4]{1,0:T(8,128)} %copy.32.routing_ref, bf16[40,5120]{1,0:T(8,128)(2,1)} %after.28.refs_0_, bf16[40,5120]{1,0:T(8,128)(2,1)} %collective-permute-done.12.refs_1_, bf16[40,5120]{1,0:T(8,128)(2,1)} %collective-permute-done.13.refs_2_, ...), custom_call_target="tpu_custom_call" | custom-call | flops 1 | bytes 1 | tf_op jit(solution)/shard_map/combine/pallas_call | solution.py:293
  (54 shorter events, 8.4 us)
Async XLA Ops:
  7.2 1.5 copy-start.2
  7.2 1.5 copy-start.3
  7.2 94.7 %all-gather.5.cloned.1.call-start = ((), (), s32[]{:S(2)}) async-start(), calls=%async_computation.3 | async-start | bytes 9830400 | tf_op jit(solution)/shard_map/all_gather | solution.py:391
  7.9 116.6 %all-gather.7.cloned.1.call-start = ((), (), s32[]{:S(2)}) async-start(), calls=%async_computation.4 | async-start | bytes 9830400 | tf_op jit(solution)/shard_map/all_gather | solution.py:392
  13.5 7.4 %copy-start.1 = (s32[128,4]{0,1:T(4,128)S(1)}, s32[128,4]{0,1:T(4,128)}, u32[]{:S(2)}) copy-start(s32[128,4]{0,1:T(4,128)} %get-tuple-element.55) | copy-start | bytes 6148
  13.5 83.8 %all-to-all-start = ((bf16[8,40,5120]{2,1,0:T(8,128)(2,1)}), bf16[8,40,5120]{2,1,0:T(8,128)(2,1)}, u32[]{:S(2)}, u32[]{:S(2)}) async-start(bf16[8,40,5120]{2,1,0:T(8,128)(2,1)} %dispatch.2.refs_1_), calls=%async_computation | async-start | bytes 6553600 | tf_op jit(solution)/shard_map/all_to_all | solution.py:387
  21.6 75.7 %collective-permute-start.4 = (s32[128,4]{1,0:T(8,128)}, s32[128,4]{1,0:T(8,128)}, u32[]{:S(2)}, u32[]{:S(2)}) collective-permute-start(s32[128,4]{1,0:T(8,128)} %copy.32.routing_ref), channel_id=1, source_target_pairs={{0,4},{1,5},{2,6},{3,7},{4,0},{5,1},{6,2},{7,3},{8,12},{9,13},{10,... | collective-permute-start | bytes 6152 | tf_op jit(solution)/shard_map/ppermute | solution.py:365
  97.3 85.8 %all-to-all-start.1 = ((bf16[8,40,5120]{2,1,0:T(8,128)(2,1)}), bf16[8,40,5120]{2,1,0:T(8,128)(2,1)}, u32[]{:S(2)}, u32[]{:S(2)}) async-start(bf16[8,40,5120]{2,1,0:T(8,128)(2,1)} %after.21), calls=%async_computation.1 | async-start | bytes 6553600 | tf_op jit(solution)/shard_map/all_to_all | solution.py:387
  101.8 157.8 %all-gather.11.cloned.1.call-start = ((), (), s32[]{:S(2)}) async-start(), calls=%async_computation.6 | async-start | bytes 2457600 | tf_op jit(solution)/shard_map/all_gather | solution.py:419
  137.6 20.0 %collective-permute-start = (bf16[40,5120]{1,0:T(8,128)(2,1)}, bf16[40,5120]{1,0:T(8,128)(2,1)S(1)}, u32[]{:S(2)}, u32[]{:S(2)}) collective-permute-start(bf16[40,5120]{1,0:T(8,128)(2,1)} %get-tuple-element.30), channel_id=1, source_target_pairs={{0,1},{1,0},{2,3},{3,2},{4,5},{5,4},{6,7},{7,6},{8,9},{9,8},{10,11... | collective-permute-start | bytes 1228808 | tf_op jit(solution)/shard_map/ppermute | solution.py:365
  139.1 26.4 %collective-permute-start.5 = (bf16[40,5120]{1,0:T(8,128)(2,1)}, bf16[40,5120]{1,0:T(8,128)(2,1)}, u32[]{:S(2)}, u32[]{:S(2)}) collective-permute-start(bf16[40,5120]{1,0:T(8,128)(2,1)} %get-tuple-element.35), channel_id=1, source_target_pairs={{0,2},{1,3},{2,0},{3,1},{4,6},{5,7},{6,4},{7,5},{8,10},{9,11},{10,... | collective-permute-start | bytes 1228808 | tf_op jit(solution)/shard_map/ppermute | solution.py:365
  140.6 35.8 %collective-permute-start.6 = (bf16[40,5120]{1,0:T(8,128)(2,1)}, bf16[40,5120]{1,0:T(8,128)(2,1)}, u32[]{:S(2)}, u32[]{:S(2)}) collective-permute-start(bf16[40,5120]{1,0:T(8,128)(2,1)} %get-tuple-element.36), channel_id=1, source_target_pairs={{0,3},{1,2},{2,1},{3,0},{4,7},{5,6},{6,5},{7,4},{8,11},{9,10},{10,... | collective-permute-start | bytes 1228808 | tf_op jit(solution)/shard_map/ppermute | solution.py:365
  157.6 0.8 copy-start
  158.3 38.7 %collective-permute-start.1 = (bf16[40,5120]{1,0:T(8,128)(2,1)}, bf16[40,5120]{1,0:T(8,128)(2,1)}, u32[]{:S(2)}, u32[]{:S(2)}) collective-permute-start(bf16[40,5120]{1,0:T(8,128)(2,1)} %after.17), channel_id=1, source_target_pairs={{0,1},{1,0},{2,3},{3,2},{4,5},{5,4},{6,7},{7,6},{8,9},{9,8},{10,11... | collective-permute-start | bytes 1228808 | tf_op jit(solution)/shard_map/ppermute | solution.py:365
  158.3 38.8 %collective-permute-start.2 = (bf16[40,5120]{1,0:T(8,128)(2,1)}, bf16[40,5120]{1,0:T(8,128)(2,1)}, u32[]{:S(2)}, u32[]{:S(2)}) collective-permute-start(bf16[40,5120]{1,0:T(8,128)(2,1)} %after.18), channel_id=1, source_target_pairs={{0,2},{1,3},{2,0},{3,1},{4,6},{5,7},{6,4},{7,5},{8,10},{9,11},{10,... | collective-permute-start | bytes 1228808 | tf_op jit(solution)/shard_map/ppermute | solution.py:365
  160.4 40.0 %collective-permute-start.3 = (bf16[40,5120]{1,0:T(8,128)(2,1)}, bf16[40,5120]{1,0:T(8,128)(2,1)}, u32[]{:S(2)}, u32[]{:S(2)}) collective-permute-start(bf16[40,5120]{1,0:T(8,128)(2,1)} %after.19), channel_id=1, source_target_pairs={{0,3},{1,2},{2,1},{3,0},{4,7},{5,6},{6,5},{7,4},{8,11},{9,10},{10,... | collective-permute-start | bytes 1228808 | tf_op jit(solution)/shard_map/ppermute | solution.py:365
  179.9 17.2 %collective-permute-start.7 = (bf16[32,5120]{1,0:T(8,128)(2,1)}, bf16[32,5120]{1,0:T(8,128)(2,1)}, u32[]{:S(2)}, u32[]{:S(2)}) collective-permute-start(bf16[32,5120]{1,0:T(8,128)(2,1)} %get-tuple-element.37.refs_6_), channel_id=1, source_target_pairs={{0,4},{1,5},{2,6},{3,7},{4,0},{5,1},{6,2},{7,3},{8,12},{9,13},{10,... | collective-permute-start | bytes 983048 | tf_op jit(solution)/shard_map/ppermute | solution.py:365
  200.4 89.4 %all-to-all-start.2 = ((bf16[4,640,1280]{2,1,0:T(8,128)(2,1)}), bf16[4,640,1280]{2,1,0:T(8,128)(2,1)}, u32[]{:S(2)}, u32[]{:S(2)}) async-start(bf16[4,640,1280]{2,1,0:T(8,128)(2,1)} %after.22), calls=%async_computation.2 | async-start | bytes 13107200 | tf_op jit(solution)/shard_map/all_to_all | solution.py:416
  205.8 53.8 %all-gather.9.cloned.1.call-start = ((), (), s32[]{:S(2)}) async-start(), calls=%async_computation.5 | async-start | bytes 2457600 | tf_op jit(solution)/shard_map/all_gather | solution.py:420
  206.4 46.4 %collective-permute-start.8 = (bf16[96,5120]{1,0:T(8,128)(2,1)}, bf16[96,5120]{1,0:T(8,128)(2,1)}, u32[]{:S(2)}, u32[]{:S(2)}) collective-permute-start(bf16[96,5120]{1,0:T(8,128)(2,1)} %after.20), channel_id=1, source_target_pairs={{0,4},{1,5},{2,6},{3,7},{4,0},{5,1},{6,2},{7,3},{8,12},{9,13},{10,... | collective-permute-start | bytes 2949128 | tf_op jit(solution)/shard_map/ppermute | solution.py:365
  209.1 11.8 %collective-permute-start.9 = (bf16[40,5120]{1,0:T(8,128)(2,1)}, bf16[40,5120]{1,0:T(8,128)(2,1)}, u32[]{:S(2)}, u32[]{:S(2)}) collective-permute-start(bf16[40,5120]{1,0:T(8,128)(2,1)} %after.25), channel_id=1, source_target_pairs={{0,1},{1,0},{2,3},{3,2},{4,5},{5,4},{6,7},{7,6},{8,9},{9,8},{10,11... | collective-permute-start | bytes 1228808 | tf_op jit(solution)/shard_map/ppermute | solution.py:365
  209.1 31.2 %collective-permute-start.10 = (bf16[40,5120]{1,0:T(8,128)(2,1)}, bf16[40,5120]{1,0:T(8,128)(2,1)}, u32[]{:S(2)}, u32[]{:S(2)}) collective-permute-start(bf16[40,5120]{1,0:T(8,128)(2,1)} %after.26), channel_id=1, source_target_pairs={{0,2},{1,3},{2,0},{3,1},{4,6},{5,7},{6,4},{7,5},{8,10},{9,11},{10,... | collective-permute-start | bytes 1228808 | tf_op jit(solution)/shard_map/ppermute | solution.py:365
  213.0 35.6 %collective-permute-start.11 = (bf16[40,5120]{1,0:T(8,128)(2,1)}, bf16[40,5120]{1,0:T(8,128)(2,1)}, u32[]{:S(2)}, u32[]{:S(2)}) collective-permute-start(bf16[40,5120]{1,0:T(8,128)(2,1)} %after.27), channel_id=1, source_target_pairs={{0,3},{1,2},{2,1},{3,0},{4,7},{5,6},{6,5},{7,4},{8,11},{9,10},{10,... | collective-permute-start | bytes 1228808 | tf_op jit(solution)/shard_map/ppermute | solution.py:365
  256.0 58.2 %collective-permute-start.15 = (bf16[128,5120]{1,0:T(8,128)(2,1)}, bf16[128,5120]{1,0:T(8,128)(2,1)}, u32[]{:S(2)}, u32[]{:S(2)}) collective-permute-start(bf16[128,5120]{1,0:T(8,128)(2,1)} %combine.6.refs_1_), channel_id=1, source_target_pairs={{0,4},{1,5},{2,6},{3,7},{4,0},{5,1},{6,2},{7,3},{8,12},{9,13},{10,... | collective-permute-start | bytes 3932168 | tf_op jit(solution)/shard_map/ppermute | solution.py:365
  256.0 50.3 %collective-permute-start.12 = (bf16[40,5120]{1,0:T(8,128)(2,1)}, bf16[40,5120]{1,0:T(8,128)(2,1)}, u32[]{:S(2)}, u32[]{:S(2)}) collective-permute-start(bf16[40,5120]{1,0:T(8,128)(2,1)} %after.29), channel_id=1, source_target_pairs={{0,1},{1,0},{2,3},{3,2},{4,5},{5,4},{6,7},{7,6},{8,9},{9,8},{10,11... | collective-permute-start | bytes 1228808 | tf_op jit(solution)/shard_map/ppermute | solution.py:365
  257.6 48.7 %collective-permute-start.13 = (bf16[40,5120]{1,0:T(8,128)(2,1)}, bf16[40,5120]{1,0:T(8,128)(2,1)}, u32[]{:S(2)}, u32[]{:S(2)}) collective-permute-start(bf16[40,5120]{1,0:T(8,128)(2,1)} %after.30), channel_id=1, source_target_pairs={{0,2},{1,3},{2,0},{3,1},{4,6},{5,7},{6,4},{7,5},{8,10},{9,11},{10,... | collective-permute-start | bytes 1228808 | tf_op jit(solution)/shard_map/ppermute | solution.py:365
  259.3 47.0 %collective-permute-start.14 = (bf16[40,5120]{1,0:T(8,128)(2,1)}, bf16[40,5120]{1,0:T(8,128)(2,1)}, u32[]{:S(2)}, u32[]{:S(2)}) collective-permute-start(bf16[40,5120]{1,0:T(8,128)(2,1)} %after.31), channel_id=1, source_target_pairs={{0,3},{1,2},{2,1},{3,0},{4,7},{5,6},{6,5},{7,4},{8,11},{9,10},{10,... | collective-permute-start | bytes 1228808 | tf_op jit(solution)/shard_map/ppermute | solution.py:365
Sparse Core Ops, SparseCore 0:
  9.6 58.0 all-gather.4
  69.2 55.3 all-gather.6
  137.7 21.8 all-gather.10
  208.4 35.1 all-gather.8

commit v5 on v4

--- a/solution.py
+++ b/solution.py
@@ -59,14 +59,19 @@
     return pltpu.CompilerParams(vmem_limit_bytes=VMEM_LIMIT, **kwargs)
 
 
-def slots_by_row(routing_t, me, half, block):
-    n_rows = routing_t.shape[1]
-    ids = [routing_t[k : k + 1, :] for k in (0, 1)]
-    codes = [routing_t[k : k + 1, :].astype(F32) for k in (2, 3)]
+def slots_by_row(routing, half, block):
+    n_rows = routing.shape[0]
+    lane = iota((n_rows, 128), 1)
+    wide = jnp.zeros((n_rows, 128), F32)
+    for k in range(4):
+        wide = jnp.where(lane == k, routing[:, k : k + 1].astype(F32), wide)
+    turned = wide.T
+    ids = [turned[k : k + 1, :].astype(I32) for k in (0, 1)]
+    codes = [turned[k : k + 1, :] for k in (2, 3)]
     total = codes[0] + codes[1]
     gates = [code / total for code in codes]
     height = -(-half // 8) * 8
-    expert = me ^ iota((height, n_rows), 0)
+    expert = iota((height, n_rows), 0)
     named = [ids[k] == expert for k in (0, 1)]
     either = named[0] | named[1]
     earlier = as_bf16(iota((n_rows, n_rows), 0) < iota((n_rows, n_rows), 1))
@@ -107,13 +112,13 @@
     return hot, gates
 
 
-def dispatch_kernel(groups, block, gated, n_after, me_ref, routing_ref, *refs):
+def dispatch_kernel(groups, block, gated, n_after, routing_ref, *refs):
     source = refs[0]
     out_ref, hot_ref, gate_ref = refs[1 + n_after :]
 
     @pl.when(pl.program_id(0) == 0)
     def _():
-        hot, gate = slots_by_row(routing_ref[...], me_ref[0], groups, block)
+        hot, gate = slots_by_row(routing_ref[...], groups, block)
         hot_ref[...] = hot
         gate_ref[...] = jnp.broadcast_to(gate, gate_ref.shape)
 
@@ -124,29 +129,26 @@
         out_ref[k] = rows[k * block : (k + 1) * block].astype(BF16)
 
 
-def dispatch(me, routing_t, source, groups, block, chunk, gated=False, wait_for=()):
+def dispatch(routing, source, groups, block, chunk, gated=False, wait_for=()):
     n_rows, width = source.shape
     return pl.pallas_call(
         functools.partial(dispatch_kernel, groups, block, gated, len(wait_for)),
-        grid_spec=pltpu.PrefetchScalarGridSpec(
-            num_scalar_prefetch=1,
-            grid=(width // chunk,),
-            in_specs=[
-                pl.BlockSpec(routing_t.shape, lambda d, me: (0, 0)),
-                pl.BlockSpec((n_rows, chunk), lambda d, me: (0, d)),
-            ]
-            + [pl.BlockSpec(memory_space=pl.ANY) for _ in wait_for],
-            out_specs=pl.BlockSpec((groups, block, chunk), lambda d, me: (0, 0, d)),
-            scratch_shapes=[
-                pltpu.VMEM((groups * block, n_rows), BF16),
-                pltpu.VMEM((groups * block, 128), F32),
-            ],
-        ),
+        grid=(width // chunk,),
+        in_specs=[
+            pl.BlockSpec(routing.shape, lambda d: (0, 0)),
+            pl.BlockSpec((n_rows, chunk), lambda d: (0, d)),
+        ]
+        + [pl.BlockSpec(memory_space=pl.ANY) for _ in wait_for],
+        out_specs=pl.BlockSpec((groups, block, chunk), lambda d: (0, 0, d)),
         out_shape=jax.ShapeDtypeStruct((groups, block, width), BF16),
+        scratch_shapes=[
+            pltpu.VMEM((groups * block, n_rows), BF16),
+            pltpu.VMEM((groups * block, 128), F32),
+        ],
         compiler_params=params(),
         cost_estimate=SHORT,
         name="dispatch",
-    )(me, routing_t, source, *wait_for)
+    )(routing, source, *wait_for)
 
 
 def expert_kernel(n, n_chunks, backward, *refs):
@@ -155,7 +157,7 @@
     outs = refs[at : at + n]
     sent_hbm, middle_ref = refs[at + n : at + n + 2]
     pre_ref = refs[4] if backward else refs[at + n + 2]
-    rows_v, first_v, second_v, out_v, in_sem, out_sem = refs[-6:]
+    rows_v, first_v, second_v, out_v, pre_v, middle_v, in_sem, out_sem, own_sem = refs[-9:]
     rows, width = rows_v.shape
     chunk = width // n_chunks
     columns = [pl.ds(d * chunk, chunk) for d in range(n_chunks)]
@@ -182,9 +184,16 @@
             out_v.at[me_ref[0] ^ k, :, columns[d]], outs[k].at[:, columns[d]], out_sem.at[d, k]
         )
 
+    keep_middle = pltpu.make_async_copy(middle_v, middle_ref, own_sem.at[0])
+    if backward:
+        move_pre = pltpu.make_async_copy(pre_ref, pre_v, own_sem.at[1])
+    else:
+        move_pre = pltpu.make_async_copy(pre_v, pre_ref, own_sem.at[1])
     for d in range(n_chunks):
         for copy in load(d):
             copy.start()
+    if backward:
+        move_pre.start()
     for d in range(n_chunks):
         load_second(d).start()
     total = None
@@ -195,11 +204,14 @@
         part = dot(rows_v[:, columns[d]], first_v[columns[d]])
         total = part if d == 0 else total + part
     if backward:
-        middle = (total * gelu_slope(pre_ref[...])).astype(BF16)
+        move_pre.wait()
+        middle = (total * gelu_slope(pre_v[...])).astype(BF16)
     else:
-        pre_ref[...] = total
+        pre_v[...] = total
+        move_pre.start()
         middle = gelu(total).astype(BF16)
-    middle_ref[...] = middle
+    middle_v[...] = middle
+    keep_middle.start()
     for d in range(n_chunks):
         load_second(d).wait()
         result = contract_columns(middle, second_v[columns[d]])
@@ -210,6 +222,9 @@
         send(d).wait()
         for k in range(n):
             store(d, k).wait()
+    keep_middle.wait()
+    if not backward:
+        move_pre.wait()
 
 
 def expert(me, rows_in, first, second, n_chunks, pre=None, sent=None, wait_for=None):
@@ -219,16 +234,15 @@
     chunk = width // n_chunks
     backward = pre is not None
     anywhere = pl.BlockSpec(memory_space=pl.ANY)
-    whole = pl.BlockSpec(memory_space=pltpu.VMEM)
     operands = (me, rows_in.reshape(rows, width), first, second)
     in_specs = [pl.BlockSpec(memory_space=pltpu.SMEM)] + [anywhere] * 3
     if backward:
         operands += (pre, sent, wait_for)
-        in_specs += [whole, anywhere, anywhere]
+        in_specs += [anywhere] * 3
     results = pl.pallas_call(
         functools.partial(expert_kernel, n, n_chunks, backward),
         in_specs=in_specs,
-        out_specs=[anywhere] * (n + 1) + [whole] * (1 if backward else 2),
+        out_specs=[anywhere] * (n + 2 if backward else n + 3),
         out_shape=[jax.ShapeDtypeStruct((block, width), BF16)] * n
         + [
             jax.ShapeDtypeStruct((n_chunks, 2 * rows, chunk), BF16),
@@ -240,8 +254,11 @@
             pltpu.VMEM((width, hidden), BF16),
             pltpu.VMEM((width, hidden), BF16),
             pltpu.VMEM((n, block, width), BF16),
+            pltpu.VMEM((rows, hidden), F32),
+            pltpu.VMEM((rows, hidden), BF16),
             pltpu.SemaphoreType.DMA((4, n_chunks)),
             pltpu.SemaphoreType.DMA((n_chunks, n)),
+            pltpu.SemaphoreType.DMA((2,)),
         ],
         input_output_aliases={5: n} if backward else {},
         compiler_params=params(),
@@ -251,27 +268,46 @@
     return (results[:n],) + tuple(results[n:])
 
 
-def combine_kernel(groups, block, gated, n_arrived, n_after, me_ref, routing_ref, *refs):
-    n_blocks = groups
-    blocks = refs[:n_blocks]
-    arrived = refs[n_blocks : n_blocks + n_arrived]
-    outs = refs[n_blocks + n_arrived + n_after : -2]
-    hot_ref, gate_ref = refs[-2:]
-
-    @pl.when(pl.program_id(0) == 0)
-    def _():
-        hot, gates = slots_by_column(routing_ref[...], me_ref[0], groups, block)
-        if gated:
-            hot_ref[...] = jnp.concatenate(hot, axis=0)
-            for k in (0, 1):
-                gate_ref[:, k * 128 : (k + 1) * 128] = jnp.broadcast_to(
-                    OUT_SCALE * gates[k], (gates[k].shape[0], 128)
-                )
-        else:
-            hot_ref[...] = (hot[0].astype(F32) + hot[1].astype(F32)).astype(BF16)
-
+def plan_kernel(groups, block, me_ref, routing_ref, hot_ref, sum_ref, gate_ref):
+    hot, gates = slots_by_column(routing_ref[...], me_ref[0], groups, block)
+    hot_ref[...] = jnp.concatenate(hot, axis=0)
+    sum_ref[...] = (hot[0].astype(F32) + hot[1].astype(F32)).astype(BF16)
+    for k in (0, 1):
+        gate_ref[:, k * 128 : (k + 1) * 128] = jnp.broadcast_to(
+            OUT_SCALE * gates[k], (gates[k].shape[0], 128)
+        )
+
+
+def plan(me, routing, groups, block, wait_for=()):
+    n_rows = routing.shape[0]
+    whole = pl.BlockSpec(memory_space=pltpu.VMEM)
+    n_after = len(wait_for)
+
+    def kernel(me_ref, routing_ref, *refs):
+        plan_kernel(groups, block, me_ref, routing_ref, *refs[n_after:])
+
+    return pl.pallas_call(
+        kernel,
+        in_specs=[pl.BlockSpec(memory_space=pltpu.SMEM), whole]
+        + [pl.BlockSpec(memory_space=pl.ANY) for _ in wait_for],
+        out_specs=[whole] * 3,
+        out_shape=[
+            jax.ShapeDtypeStruct((2 * n_rows, groups * block), BF16),
+            jax.ShapeDtypeStruct((n_rows, groups * block), BF16),
+            jax.ShapeDtypeStruct((n_rows, 256), F32),
+        ],
+        compiler_params=params(),
+        cost_estimate=SHORT,
+        name="plan",
+    )(me, routing, *wait_for)
+
+
+def combine_kernel(groups, gated, n_arrived, n_after, hot_ref, gate_ref, *refs):
+    blocks = refs[:groups]
+    arrived = refs[groups : groups + n_arrived]
+    outs = refs[groups + n_arrived + n_after :]
     rows = stack([ref[...] for ref in blocks])
-    n_rows = routing_ref.shape[0]
+    n_rows = gate_ref.shape[0]
     total = dot(hot_ref[...], rows)
     if gated:
         total = gate_ref[:, :1] * total[:n_rows] + gate_ref[:, 128:129] * total[n_rows:]
@@ -283,35 +319,28 @@
         at += ref.shape[0]
 
 
-def combine(
-    me, routing, blocks, block, chunk, gated=False, arrived=(), wait_for=(), parts=None
-):
-    n_rows = routing.shape[0]
-    groups = len(blocks)
-    width = blocks[0].shape[1]
-    by_rows = lambda n: pl.BlockSpec((n, chunk), lambda d, me: (0, d))
+def combine(slots, blocks, chunk, gated=False, arrived=(), wait_for=(), parts=None):
+    hot = slots[0] if gated else slots[1]
+    gate = slots[2]
+    n_rows = gate.shape[0]
+    block, width = blocks[0].shape
+    by_rows = lambda n: pl.BlockSpec((n, chunk), lambda d: (0, d))
     results = pl.pallas_call(
-        functools.partial(
-            combine_kernel, groups, block, gated, len(arrived), len(wait_for)
-        ),
-        grid_spec=pltpu.PrefetchScalarGridSpec(
-            num_scalar_prefetch=1,
-            grid=(width // chunk,),
-            in_specs=[pl.BlockSpec(routing.shape, lambda d, me: (0, 0))]
-            + [by_rows(block) for _ in blocks]
-            + [by_rows(rows.shape[0]) for rows in arrived]
-            + [pl.BlockSpec(memory_space=pl.ANY) for _ in wait_for],
-            out_specs=[by_rows(n) for n in parts or (n_rows,)],
-            scratch_shapes=[
-                pltpu.VMEM(((2 if gated else 1) * n_rows, groups * block), BF16),
-                pltpu.VMEM((n_rows, 256), F32),
-            ],
-        ),
+        functools.partial(combine_kernel, len(blocks), gated, len(arrived), len(wait_for)),
+        grid=(width // chunk,),
+        in_specs=[
+            pl.BlockSpec(hot.shape, lambda d: (0, 0)),
+            pl.BlockSpec(gate.shape, lambda d: (0, 0)),
+        ]
+        + [by_rows(block) for _ in blocks]
+        + [by_rows(rows.shape[0]) for rows in arrived]
+        + [pl.BlockSpec(memory_space=pl.ANY) for _ in wait_for],
+        out_specs=[by_rows(n) for n in parts or (n_rows,)],
         out_shape=[jax.ShapeDtypeStruct((n, width), BF16) for n in parts or (n_rows,)],
         compiler_params=params(),
         cost_estimate=SHORT,
         name="combine",
-    )(me, routing, *blocks, *arrived, *wait_for)
+    )(hot, gate, *blocks, *arrived, *wait_for)
     return results if parts else results[0]
 
 
@@ -378,10 +407,6 @@
     half = n_expert // 2
     chunk = width // 2
     me = lax.axis_index("expert").astype(I32).reshape(1)
-    first = jnp.zeros((1,), I32)
-
-    def turned(routing):
-        return jnp.pad(routing.T, ((0, 4), (0, 0)))
 
     def swap_direct(blocks):
         return lax.all_to_all(blocks, "expert", split_axis=0, concat_axis=0, tiled=True)
@@ -391,17 +416,20 @@
     up_weight = lax.all_gather(w_up, "dp", axis=1, tiled=True)[0]
     down_weight = lax.all_gather(w_down, "dp", axis=1, tiled=True)[0]
 
-    place = (first, turned(routing))
-    rows_out = dispatch(*place, tokens, n_expert, block, chunk)
+    rows_out = dispatch(routing, tokens, n_expert, block, chunk)
     rows_in = swap_direct(rows_out)
-    grads_out = dispatch(*place, grad_out, n_expert, block, chunk, gated=True, wait_for=(rows_out,))
+    grads_out = dispatch(
+        routing, grad_out, n_expert, block, chunk, gated=True, wait_for=(rows_out,)
+    )
     grads_in = swap_direct(after(grads_out, far_routing))
 
     out, sent, hidden, pre_act = expert(me, rows_in, up_weight, down_weight, n_dp)
     parts = (n_rows // 4, n_rows - n_rows // 4)
     far_out = exchange(out[half:])
-    far_mixed = combine(me, far_routing, far_out, block, chunk, gated=True, parts=parts)
-    near_back = exchange([after(rows, far_out[1]) for rows in out[:half]])
+    far_slots = plan(me, far_routing, half, block, (out[0],))
+    near_slots = plan(me, routing, half, block, (out[0],))
+    far_mixed = combine(far_slots, far_out, chunk, gated=True, parts=parts)
+    near_back = exchange(out[:half])
     mixed_in = [permute_xor(far_mixed[0], "expert", half)]
     mixed_in.append(permute_xor(after(far_mixed[1], mixed_in[0]), "expert", half))
 
@@ -410,7 +438,7 @@
     )
     ready = (mixed_in[0], *near_back[1:])
     far_back = exchange([after(rows, *ready) for rows in row_grads[half:]])
-    far_sum = combine(me, far_routing, far_back, block, chunk, wait_for=(mixed_in[1],))
+    far_sum = combine(far_slots, far_back, chunk, wait_for=(mixed_in[1],))
     sum_in = permute_xor(far_sum, "expert", half)
     near_grad = exchange([after(rows, far_sum) for rows in row_grads[:half]])
     traded = lax.all_to_all(
@@ -421,17 +449,15 @@
 
     grad_up, grad_down = weight_grads(traded, pre_all, hidden_all, 256)
     layer_output = combine(
-        me,
-        routing,
+        near_slots,
         near_back,
-        block,
         chunk,
         gated=True,
         arrived=mixed_in,
         wait_for=(grad_up, grad_down),
     )
     grad_tokens = combine(
-        me, routing, near_grad, block, chunk, arrived=(sum_in,), wait_for=(layer_output,)
+        near_slots, near_grad, chunk, arrived=(sum_in,), wait_for=(layer_output,)
     )
     return (layer_output, grad_tokens, grad_up, grad_down)
 

time: 325 us -> 324 us (level)
    pallas_call x4 -> x6, Pallas kernels: 14.1 us -> 16.8 us  [the longest x4 12.9 us: combine(): pl.pallas_call(functools.partial(combine_kernel, len(blocks), gated, len(...]
  transfers between devices with their start and end apart: 23 -> 23, of which waited for: 12 -> 11; matrix products, arithmetic and copies ran while one was open for 1% -> 0% of each run, Pallas kernels for 18% -> 18%
where the time goes in v5:
time: 324 us; the launch traced here: 323 us
  waiting for transfers between devices  205 us (63%)
  Pallas kernels  62.9 us (19%)
  starting transfers between devices  41.2 us (13%)
  between operations  13.9 us (4%)
    ppermute x16, waiting for transfers between devices, permute_xor(): return lax.ppermute(values, axis, [(i, i ^ mask) for i in range(size)])  151 us
    all_to_all x1, waiting for transfers between devices, local(): lax.all_to_all(after(sent, *ready), 'dp', split_axis=0, concat_axis=0, ti...  28.5 us
    pallas_call x2, Pallas kernels, expert(): pl.pallas_call(functools.partial(expert_kernel, n, n_chunks, backward), i...  25.6 us
    ppermute x16, starting transfers between devices, permute_xor(): return lax.ppermute(values, axis, [(i, i ^ mask) for i in range(size)])  24 us
    all_gather x1, waiting for transfers between devices, local(): down_weight = lax.all_gather(w_down, 'dp', axis=1, tiled=True)[0]  23 us
    pallas_call x4, Pallas kernels, combine(): pl.pallas_call(functools.partial(combine_kernel, len(blocks), gated, len(...  12.9 us
    pallas_call x1, Pallas kernels, weight_grads(): pl.pallas_call(functools.partial(weight_kernel, n_dp, depth // 2), grid=(...  12.6 us
    all_to_all x2, starting transfers between devices, swap_direct(): lax.all_to_all(blocks, 'expert', split_axis=0, concat_axis=0, tiled=True)  11.7 us
  transfers between devices with their start and end apart: 23, of which 11 were waited for; matrix products, arithmetic and copies ran while one was open for 0% of the time, Pallas kernels for 18%

profile of v5, /device:TPU:0, one launch (start us, length us, event | category | flops | bytes accessed | tf_op | source)
XLA Modules:
  0.0 323.2 jit_solution(15568852281240195050)
XLA Ops:
  9.4 3.8 %dispatch.2.refs_1_ = bf16[8,40,5120]{2,1,0:T(8,128)(2,1)} custom-call(s32[128,4]{1,0:T(8,128)} %copy.26.routing_ref, bf16[128,5120]{1,0:T(8,128)(2,1)} %refs_0_.2), custom_call_target="tpu_custom_call" | custom-call | flops 1 | bytes 1 | tf_op jit(solution)/shard_map/dispatch/pallas_call | solution.py:134
  13.3 7.2 %all-to-all-start = ((bf16[8,40,5120]{2,1,0:T(8,128)(2,1)}), bf16[8,40,5120]{2,1,0:T(8,128)(2,1)}, u32[]{:S(2)}, u32[]{:S(2)}) async-start(bf16[8,40,5120]{2,1,0:T(8,128)(2,1)} %dispatch.2.refs_1_), calls=%async_computation | async-start | bytes 6553600 | tf_op jit(solution)/shard_map/all_to_all | solution.py:412
  20.5 2.9 collective-permute-start.3
  23.4 4.1 %dispatch.3.refs_0_ = bf16[8,40,5120]{2,1,0:T(8,128)(2,1)} custom-call(s32[128,4]{1,0:T(8,128)} %copy.26.routing_ref, bf16[128,5120]{1,0:T(8,128)(2,1)} %refs_0_.3, bf16[8,40,5120]{2,1,0:T(8,128)(2,1)} %dispatch.2.refs_1_), custom_call_target="tpu_custom_call" | custom-call | flops 1 | bytes 1 | tf_op jit(solution)/shard_map/dispatch/pallas_call | solution.py:134
  27.5 69.4 %collective-permute-done.3.routing_ref.refs_1_ = s32[128,4]{1,0:T(8,128)} collective-permute-done((s32[128,4]{1,0:T(8,128)}, s32[128,4]{1,0:T(8,128)}, u32[]{:S(2)}, u32[]{:S(2)}) %collective-permute-start.3) | collective-permute-done | bytes 2080 | tf_op jit(solution)/shard_map/ppermute | solution.py:394
  97.0 4.5 %all-to-all-start.1 = ((bf16[8,40,5120]{2,1,0:T(8,128)(2,1)}), bf16[8,40,5120]{2,1,0:T(8,128)(2,1)}, u32[]{:S(2)}, u32[]{:S(2)}) async-start(bf16[8,40,5120]{2,1,0:T(8,128)(2,1)} %after.13), calls=%async_computation.1 | async-start | bytes 6553600 | tf_op jit(solution)/shard_map/all_to_all | solution.py:412
  101.5 23.0 %all-gather.7.cloned.1.call-done = bf16[1,5120,768]{2,1,0:T(8,128)(2,1)} async-done(((bf16[1,1280,768]{2,1,0:T(8,128)(2,1)}), bf16[1,5120,768]{2,1,0:T(8,128)(2,1)}) %all-gather.7.cloned.1.call-update) | async-done | bytes 7864336 | tf_op jit(solution)/shard_map/all_gather | solution.py:417
  124.5 11.9 %expert_forward.1 = (bf16[40,5120]{1,0:T(8,128)(2,1)}, bf16[40,5120]{1,0:T(8,128)(2,1)}, bf16[40,5120]{1,0:T(8,128)(2,1)}, bf16[40,5120]{1,0:T(8,128)(2,1)}, bf1...) custom-call(s32[1]{0:T(128)} %bitcast.refs_0_.me_ref, ...), custom_call_target="tpu_custom_call" | custom-call | flops 1 | bytes 1 | tf_op jit(solution)/shard_map/expert_forward/pallas_call | solution.py:242
  136.5 1.5 collective-permute-start.4
  138.0 1.5 collective-permute-start.5
  143.0 14.5 %collective-permute-done.4.refs_1_ = bf16[40,5120]{1,0:T(8,128)(2,1)} collective-permute-done((bf16[40,5120]{1,0:T(8,128)(2,1)}, bf16[40,5120]{1,0:T(8,128)(2,1)}, u32[]{:S(2)}, u32[]{:S(2)}) %collective-permute-start.4) | collective-permute-done | bytes 409632 | tf_op jit(solution)/shard_map/ppermute | solution.py:394
  158.8 2.0 plan.3
  160.8 4.4 %collective-permute-done.5.refs_2_ = bf16[40,5120]{1,0:T(8,128)(2,1)} collective-permute-done((bf16[40,5120]{1,0:T(8,128)(2,1)}, bf16[40,5120]{1,0:T(8,128)(2,1)}, u32[]{:S(2)}, u32[]{:S(2)}) %collective-permute-start.5) | collective-permute-done | bytes 409632 | tf_op jit(solution)/shard_map/ppermute | solution.py:394
  165.1 10.5 %collective-permute-done.6.refs_3_ = bf16[40,5120]{1,0:T(8,128)(2,1)} collective-permute-done((bf16[40,5120]{1,0:T(8,128)(2,1)}, bf16[40,5120]{1,0:T(8,128)(2,1)}, u32[]{:S(2)}, u32[]{:S(2)}) %collective-permute-start.6) | collective-permute-done | bytes 409632 | tf_op jit(solution)/shard_map/ppermute | solution.py:394
  175.6 3.2 %combine.4 = (bf16[32,5120]{1,0:T(8,128)(2,1)}, bf16[96,5120]{1,0:T(8,128)(2,1)}) custom-call(bf16[256,160]{1,0:T(8,128)(2,1)} %get-tuple-element.41.hot_ref, f32[128,256]{1,0:T(8,128)} %get-tuple-element.42.gate_ref, bf16[40,5120]{1,0:T(8,128)(2,1)} %get-tuple-element.43.refs_0_, bf16[40,5120]{1,0:T(8,128)(2,1)} %collective-permute-done.4.refs_1_, ...), custom_call_target="tpu_custom_call" | custom-call | flops 1 | bytes 1 | tf_op jit(solution)/shard_map/combine/pallas_call | solution.py:328
  178.9 3.2 collective-permute-start.7
  182.1 13.7 %expert_backward.1 = (bf16[40,5120]{1,0:T(8,128)(2,1)}, bf16[40,5120]{1,0:T(8,128)(2,1)}, bf16[40,5120]{1,0:T(8,128)(2,1)}, bf16[40,5120]{1,0:T(8,128)(2,1)}, bf...) custom-call(s32[1]{0:T(128)} %bitcast.refs_0_.me_ref, ...), custom_call_target="tpu_custom_call", output_to_operand_aliasing={{8}: (5, {})} | custom-call | flops 1 | bytes 1 | tf_op jit(solution)/shard_map/expert_backward/pallas_call | solution.py:242
  195.8 3.9 %collective-permute-done.2.refs_4_.refs_3_ = bf16[40,5120]{1,0:T(8,128)(2,1)} collective-permute-done((bf16[40,5120]{1,0:T(8,128)(2,1)}, bf16[40,5120]{1,0:T(8,128)(2,1)}, u32[]{:S(2)}, u32[]{:S(2)}) %collective-permute-start.2) | collective-permute-done | bytes 409632 | tf_op jit(solution)/shard_map/ppermute | solution.py:394
  199.7 5.3 %all-to-all-start.2 = ((bf16[4,640,1280]{2,1,0:T(8,128)(2,1)}), bf16[4,640,1280]{2,1,0:T(8,128)(2,1)}, u32[]{:S(2)}, u32[]{:S(2)}) async-start(bf16[4,640,1280]{2,1,0:T(8,128)(2,1)} %after.14), calls=%async_computation.2 | async-start | bytes 13107200 | tf_op jit(solution)/shard_map/all_to_all | solution.py:444
  205.6 2.4 collective-permute-start.8
  208.0 3.4 %collective-permute-start.11 = (bf16[40,5120]{1,0:T(8,128)(2,1)}, bf16[40,5120]{1,0:T(8,128)(2,1)}, u32[]{:S(2)}, u32[]{:S(2)}) collective-permute-start(bf16[40,5120]{1,0:T(8,128)(2,1)} %after.19), channel_id=1, source_target_pairs={{0,3},{1,2},{2,1},{3,0},{4,7},{5,6},{6,5},{7,4},{8,11},{9,10},{10,... | collective-permute-start | bytes 1228808 | tf_op jit(solution)/shard_map/ppermute | solution.py:394
  211.9 27.3 %collective-permute-done.11.refs_3_ = bf16[40,5120]{1,0:T(8,128)(2,1)} collective-permute-done((bf16[40,5120]{1,0:T(8,128)(2,1)}, bf16[40,5120]{1,0:T(8,128)(2,1)}, u32[]{:S(2)}, u32[]{:S(2)}) %collective-permute-start.11) | collective-permute-done | bytes 409632 | tf_op jit(solution)/shard_map/ppermute | solution.py:394
  239.2 8.3 %collective-permute-done.10.refs_2_ = bf16[40,5120]{1,0:T(8,128)(2,1)} collective-permute-done((bf16[40,5120]{1,0:T(8,128)(2,1)}, bf16[40,5120]{1,0:T(8,128)(2,1)}, u32[]{:S(2)}, u32[]{:S(2)}) %collective-permute-start.10) | collective-permute-done | bytes 409632 | tf_op jit(solution)/shard_map/ppermute | solution.py:394
  247.5 4.5 %collective-permute-done.8.refs_5_.refs_4_ = bf16[96,5120]{1,0:T(8,128)(2,1)} collective-permute-done((bf16[96,5120]{1,0:T(8,128)(2,1)}, bf16[96,5120]{1,0:T(8,128)(2,1)}, u32[]{:S(2)}, u32[]{:S(2)}) %collective-permute-start.8) | collective-permute-done | bytes 983072 | tf_op jit(solution)/shard_map/ppermute | solution.py:394
  252.1 2.9 combine.6.refs_1_
  255.0 3.1 collective-permute-start.14
  258.6 2.0 plan.2
  260.6 28.5 %all-to-all-done.2.traded_ref = bf16[4,640,1280]{2,1,0:T(8,128)(2,1)} async-done(((bf16[4,640,1280]{2,1,0:T(8,128)(2,1)}), bf16[4,640,1280]{2,1,0:T(8,128)(2,1)}, u32[]{:S(2)}, u32[]{:S(2)}) %all-to-all-start.2) | async-done | bytes 6553632 | tf_op jit(solution)/shard_map/all_to_all | solution.py:444
  289.1 12.6 %weight_grads.1 = (bf16[1,1280,768]{2,1,0:T(8,128)(2,1)}, bf16[1,1280,768]{2,1,0:T(8,128)(2,1)}) custom-call(bf16[4,640,1280]{2,1,0:T(8,128)(2,1)} %all-to-all-done.2.traded_ref, bf16[1280,768]{1,0:T(8,128)(2,1)} %all-gather.9.cloned.1.call-done.pre_ref, bf16[1280,768]{1,0:T(8,128)(2,1)} %all-gather.11.cloned.1.call-done.hidden_ref), custom_call_target="tpu_custom_call" | custom-call | flops 1 | bytes 1 | tf_op jit(solution)/shard_map/weight_grads/pallas_call | solution.py:363
  301.7 3.6 %combine.5.refs_5_ = bf16[128,5120]{1,0:T(8,128)(2,1)} custom-call(bf16[256,160]{1,0:T(8,128)(2,1)} %get-tuple-element.36.hot_ref, f32[128,256]{1,0:T(8,128)} %get-tuple-element.37.gate_ref, bf16[40,5120]{1,0:T(8,128)(2,1)} %get-tuple-element.35.refs_0_, bf16[40,5120]{1,0:T(8,128)(2,1)} %collective-permute-done.refs_2_.refs_1_, ...), custom_call_target="tpu_custom_call" | custom-call | flops 1 | bytes 1 | tf_op jit(solution)/shard_map/combine/pallas_call | solution.py:328
  305.3 8.3 %collective-permute-done.15.refs_4_ = bf16[128,5120]{1,0:T(8,128)(2,1)} collective-permute-done((bf16[128,5120]{1,0:T(8,128)(2,1)}, bf16[128,5120]{1,0:T(8,128)(2,1)}, u32[]{:S(2)}, u32[]{:S(2)}) %collective-permute-start.15) | collective-permute-done | bytes 1310752 | tf_op jit(solution)/shard_map/ppermute | solution.py:394
  313.6 3.1 combine.7
  (47 shorter events, 8.8 us)
Async XLA Ops:
  7.2 1.5 copy-start.1
  7.2 1.5 copy-start
  7.2 94.3 %all-gather.5.cloned.1.call-start = ((), (), s32[]{:S(2)}) async-start(), calls=%async_computation.3 | async-start | bytes 9830400 | tf_op jit(solution)/shard_map/all_gather | solution.py:416
  7.9 116.6 %all-gather.7.cloned.1.call-start = ((), (), s32[]{:S(2)}) async-start(), calls=%async_computation.4 | async-start | bytes 9830400 | tf_op jit(solution)/shard_map/all_gather | solution.py:417
  13.3 83.7 %all-to-all-start = ((bf16[8,40,5120]{2,1,0:T(8,128)(2,1)}), bf16[8,40,5120]{2,1,0:T(8,128)(2,1)}, u32[]{:S(2)}, u32[]{:S(2)}) async-start(bf16[8,40,5120]{2,1,0:T(8,128)(2,1)} %dispatch.2.refs_1_), calls=%async_computation | async-start | bytes 6553600 | tf_op jit(solution)/shard_map/all_to_all | solution.py:412
  20.5 76.4 %collective-permute-start.3 = (s32[128,4]{1,0:T(8,128)}, s32[128,4]{1,0:T(8,128)}, u32[]{:S(2)}, u32[]{:S(2)}) collective-permute-start(s32[128,4]{1,0:T(8,128)} %copy.26.routing_ref), channel_id=1, source_target_pairs={{0,4},{1,5},{2,6},{3,7},{4,0},{5,1},{6,2},{7,3},{8,12},{9,13},{10,... | collective-permute-start | bytes 6152 | tf_op jit(solution)/shard_map/ppermute | solution.py:394
  97.0 85.2 %all-to-all-start.1 = ((bf16[8,40,5120]{2,1,0:T(8,128)(2,1)}), bf16[8,40,5120]{2,1,0:T(8,128)(2,1)}, u32[]{:S(2)}, u32[]{:S(2)}) async-start(bf16[8,40,5120]{2,1,0:T(8,128)(2,1)} %after.13), calls=%async_computation.1 | async-start | bytes 6553600 | tf_op jit(solution)/shard_map/all_to_all | solution.py:412
  101.4 159.2 %all-gather.11.cloned.1.call-start = ((), (), s32[]{:S(2)}) async-start(), calls=%async_computation.6 | async-start | bytes 2457600 | tf_op jit(solution)/shard_map/all_gather | solution.py:447
  136.5 21.0 %collective-permute-start.4 = (bf16[40,5120]{1,0:T(8,128)(2,1)}, bf16[40,5120]{1,0:T(8,128)(2,1)}, u32[]{:S(2)}, u32[]{:S(2)}) collective-permute-start(bf16[40,5120]{1,0:T(8,128)(2,1)} %get-tuple-element.44), channel_id=1, source_target_pairs={{0,1},{1,0},{2,3},{3,2},{4,5},{5,4},{6,7},{7,6},{8,9},{9,8},{10,11... | collective-permute-start | bytes 1228808 | tf_op jit(solution)/shard_map/ppermute | solution.py:394
  138.0 27.1 %collective-permute-start.5 = (bf16[40,5120]{1,0:T(8,128)(2,1)}, bf16[40,5120]{1,0:T(8,128)(2,1)}, u32[]{:S(2)}, u32[]{:S(2)}) collective-permute-start(bf16[40,5120]{1,0:T(8,128)(2,1)} %get-tuple-element.45), channel_id=1, source_target_pairs={{0,2},{1,3},{2,0},{3,1},{4,6},{5,7},{6,4},{7,5},{8,10},{9,11},{10,... | collective-permute-start | bytes 1228808 | tf_op jit(solution)/shard_map/ppermute | solution.py:394
  139.5 36.2 %collective-permute-start.6 = (bf16[40,5120]{1,0:T(8,128)(2,1)}, bf16[40,5120]{1,0:T(8,128)(2,1)}, u32[]{:S(2)}, u32[]{:S(2)}) collective-permute-start(bf16[40,5120]{1,0:T(8,128)(2,1)} %get-tuple-element.46), channel_id=1, source_target_pairs={{0,3},{1,2},{2,1},{3,0},{4,7},{5,6},{6,5},{7,4},{8,11},{9,10},{10,... | collective-permute-start | bytes 1228808 | tf_op jit(solution)/shard_map/ppermute | solution.py:394
  140.0 55.8 %collective-permute-start = (bf16[40,5120]{1,0:T(8,128)(2,1)}, bf16[40,5120]{1,0:T(8,128)(2,1)}, u32[]{:S(2)}, u32[]{:S(2)}) collective-permute-start(bf16[40,5120]{1,0:T(8,128)(2,1)} %get-tuple-element.38), channel_id=1, source_target_pairs={{0,1},{1,0},{2,3},{3,2},{4,5},{5,4},{6,7},{7,6},{8,9},{9,8},{10,11... | collective-permute-start | bytes 1228808 | tf_op jit(solution)/shard_map/ppermute | solution.py:394
  141.5 54.3 %collective-permute-start.1 = (bf16[40,5120]{1,0:T(8,128)(2,1)}, bf16[40,5120]{1,0:T(8,128)(2,1)}, u32[]{:S(2)}, u32[]{:S(2)}) collective-permute-start(bf16[40,5120]{1,0:T(8,128)(2,1)} %get-tuple-element.39), channel_id=1, source_target_pairs={{0,2},{1,3},{2,0},{3,1},{4,6},{5,7},{6,4},{7,5},{8,10},{9,11},{10,... | collective-permute-start | bytes 1228808 | tf_op jit(solution)/shard_map/ppermute | solution.py:394
  157.5 42.3 %collective-permute-start.2 = (bf16[40,5120]{1,0:T(8,128)(2,1)}, bf16[40,5120]{1,0:T(8,128)(2,1)}, u32[]{:S(2)}, u32[]{:S(2)}) collective-permute-start(bf16[40,5120]{1,0:T(8,128)(2,1)} %get-tuple-element.40), channel_id=1, source_target_pairs={{0,3},{1,2},{2,1},{3,0},{4,7},{5,6},{6,5},{7,4},{8,11},{9,10},{10,... | collective-permute-start | bytes 1228808 | tf_op jit(solution)/shard_map/ppermute | solution.py:394
  178.9 20.9 %collective-permute-start.7 = (bf16[32,5120]{1,0:T(8,128)(2,1)}, bf16[32,5120]{1,0:T(8,128)(2,1)}, u32[]{:S(2)}, u32[]{:S(2)}) collective-permute-start(bf16[32,5120]{1,0:T(8,128)(2,1)} %get-tuple-element.47.refs_6_), channel_id=1, source_target_pairs={{0,4},{1,5},{2,6},{3,7},{4,0},{5,1},{6,2},{7,3},{8,12},{9,13},{10,... | collective-permute-start | bytes 983048 | tf_op jit(solution)/shard_map/ppermute | solution.py:394
  199.7 89.4 %all-to-all-start.2 = ((bf16[4,640,1280]{2,1,0:T(8,128)(2,1)}), bf16[4,640,1280]{2,1,0:T(8,128)(2,1)}, u32[]{:S(2)}, u32[]{:S(2)}) async-start(bf16[4,640,1280]{2,1,0:T(8,128)(2,1)} %after.14), calls=%async_computation.2 | async-start | bytes 13107200 | tf_op jit(solution)/shard_map/all_to_all | solution.py:444
  205.0 55.6 %all-gather.9.cloned.1.call-start = ((), (), s32[]{:S(2)}) async-start(), calls=%async_computation.5 | async-start | bytes 2457600 | tf_op jit(solution)/shard_map/all_gather | solution.py:448
  205.6 46.4 %collective-permute-start.8 = (bf16[96,5120]{1,0:T(8,128)(2,1)}, bf16[96,5120]{1,0:T(8,128)(2,1)}, u32[]{:S(2)}, u32[]{:S(2)}) collective-permute-start(bf16[96,5120]{1,0:T(8,128)(2,1)} %after.12), channel_id=1, source_target_pairs={{0,4},{1,5},{2,6},{3,7},{4,0},{5,1},{6,2},{7,3},{8,12},{9,13},{10,... | collective-permute-start | bytes 2949128 | tf_op jit(solution)/shard_map/ppermute | solution.py:394
  208.0 31.2 %collective-permute-start.11 = (bf16[40,5120]{1,0:T(8,128)(2,1)}, bf16[40,5120]{1,0:T(8,128)(2,1)}, u32[]{:S(2)}, u32[]{:S(2)}) collective-permute-start(bf16[40,5120]{1,0:T(8,128)(2,1)} %after.19), channel_id=1, source_target_pairs={{0,3},{1,2},{2,1},{3,0},{4,7},{5,6},{6,5},{7,4},{8,11},{9,10},{10,... | collective-permute-start | bytes 1228808 | tf_op jit(solution)/shard_map/ppermute | solution.py:394
  211.4 36.2 %collective-permute-start.10 = (bf16[40,5120]{1,0:T(8,128)(2,1)}, bf16[40,5120]{1,0:T(8,128)(2,1)}, u32[]{:S(2)}, u32[]{:S(2)}) collective-permute-start(bf16[40,5120]{1,0:T(8,128)(2,1)} %after.18), channel_id=1, source_target_pairs={{0,2},{1,3},{2,0},{3,1},{4,6},{5,7},{6,4},{7,5},{8,10},{9,11},{10,... | collective-permute-start | bytes 1228808 | tf_op jit(solution)/shard_map/ppermute | solution.py:394
  211.4 36.2 %collective-permute-start.9 = (bf16[40,5120]{1,0:T(8,128)(2,1)}, bf16[40,5120]{1,0:T(8,128)(2,1)}, u32[]{:S(2)}, u32[]{:S(2)}) collective-permute-start(bf16[40,5120]{1,0:T(8,128)(2,1)} %after.17), channel_id=1, source_target_pairs={{0,1},{1,0},{2,3},{3,2},{4,5},{5,4},{6,7},{7,6},{8,9},{9,8},{10,11... | collective-permute-start | bytes 1228808 | tf_op jit(solution)/shard_map/ppermute | solution.py:394
  255.0 58.6 %collective-permute-start.15 = (bf16[128,5120]{1,0:T(8,128)(2,1)}, bf16[128,5120]{1,0:T(8,128)(2,1)}, u32[]{:S(2)}, u32[]{:S(2)}) collective-permute-start(bf16[128,5120]{1,0:T(8,128)(2,1)} %combine.6.refs_1_), channel_id=1, source_target_pairs={{0,4},{1,5},{2,6},{3,7},{4,0},{5,1},{6,2},{7,3},{8,12},{9,13},{10,... | collective-permute-start | bytes 3932168 | tf_op jit(solution)/shard_map/ppermute | solution.py:394
  255.0 50.3 %collective-permute-start.14 = (bf16[40,5120]{1,0:T(8,128)(2,1)}, bf16[40,5120]{1,0:T(8,128)(2,1)}, u32[]{:S(2)}, u32[]{:S(2)}) collective-permute-start(bf16[40,5120]{1,0:T(8,128)(2,1)} %after.23), channel_id=1, source_target_pairs={{0,3},{1,2},{2,1},{3,0},{4,7},{5,6},{6,5},{7,4},{8,11},{9,10},{10,... | collective-permute-start | bytes 1228808 | tf_op jit(solution)/shard_map/ppermute | solution.py:394
  258.1 47.2 %collective-permute-start.13 = (bf16[40,5120]{1,0:T(8,128)(2,1)}, bf16[40,5120]{1,0:T(8,128)(2,1)}, u32[]{:S(2)}, u32[]{:S(2)}) collective-permute-start(bf16[40,5120]{1,0:T(8,128)(2,1)} %after.22), channel_id=1, source_target_pairs={{0,2},{1,3},{2,0},{3,1},{4,6},{5,7},{6,4},{7,5},{8,10},{9,11},{10,... | collective-permute-start | bytes 1228808 | tf_op jit(solution)/shard_map/ppermute | solution.py:394
  258.1 47.2 %collective-permute-start.12 = (bf16[40,5120]{1,0:T(8,128)(2,1)}, bf16[40,5120]{1,0:T(8,128)(2,1)}, u32[]{:S(2)}, u32[]{:S(2)}) collective-permute-start(bf16[40,5120]{1,0:T(8,128)(2,1)} %after.21), channel_id=1, source_target_pairs={{0,1},{1,0},{2,3},{3,2},{4,5},{5,4},{6,7},{7,6},{8,9},{9,8},{10,11... | collective-permute-start | bytes 1228808 | tf_op jit(solution)/shard_map/ppermute | solution.py:394
Sparse Core Ops, SparseCore 0:
  9.6 58.0 all-gather.4
  69.2 55.3 all-gather.6
  136.6 21.8 all-gather.10
  207.7 34.7 all-gather.8

commit v6 on v5

--- a/solution.py
+++ b/solution.py
@@ -438,8 +438,8 @@
     )
     ready = (mixed_in[0], *near_back[1:])
     far_back = exchange([after(rows, *ready) for rows in row_grads[half:]])
-    far_sum = combine(far_slots, far_back, chunk, wait_for=(mixed_in[1],))
-    sum_in = permute_xor(far_sum, "expert", half)
+    far_sum = combine(far_slots, far_back, chunk)
+    sum_in = permute_xor(after(far_sum, mixed_in[1]), "expert", half)
     near_grad = exchange([after(rows, far_sum) for rows in row_grads[:half]])
     traded = lax.all_to_all(
         after(sent, *ready), "dp", split_axis=0, concat_axis=0, tiled=True

time: 324 us -> 322 us (level)
    ppermute x16, waiting for transfers between devices: 151 us -> 147 us  [permute_xor(): return lax.ppermute(values, axis, [(i, i ^ mask) for i in range(size)])]
  transfers between devices with their start and end apart: 23 -> 23, of which waited for: 11 -> 11; matrix products, arithmetic and copies ran while one was open for 0% -> 0% of each run, Pallas kernels for 18% -> 19%
where the time goes in v6:
time: 322 us
  waiting for transfers between devices  202 us (63%)
  Pallas kernels  62.9 us (20%)
  starting transfers between devices  42.1 us (13%)
  between operations  13.9 us (4%)
    ppermute x16, waiting for transfers between devices, permute_xor(): return lax.ppermute(values, axis, [(i, i ^ mask) for i in range(size)])  147 us
    all_to_all x1, waiting for transfers between devices, local(): lax.all_to_all(after(sent, *ready), 'dp', split_axis=0, concat_axis=0, ti...  30.4 us
    pallas_call x2, Pallas kernels, expert(): pl.pallas_call(functools.partial(expert_kernel, n, n_chunks, backward), i...  25.6 us
    ppermute x16, starting transfers between devices, permute_xor(): return lax.ppermute(values, axis, [(i, i ^ mask) for i in range(size)])  24.9 us
    all_gather x1, waiting for transfers between devices, local(): down_weight = lax.all_gather(w_down, 'dp', axis=1, tiled=True)[0]  23 us
    pallas_call x4, Pallas kernels, combine(): pl.pallas_call(functools.partial(combine_kernel, len(blocks), gated, len(...  12.9 us
    pallas_call x1, Pallas kernels, weight_grads(): pl.pallas_call(functools.partial(weight_kernel, n_dp, depth // 2), grid=(...  12.6 us
    all_to_all x2, starting transfers between devices, swap_direct(): lax.all_to_all(blocks, 'expert', split_axis=0, concat_axis=0, tiled=True)  11.7 us
  transfers between devices with their start and end apart: 23, of which 11 were waited for; matrix products, arithmetic and copies ran while one was open for 0% of the time, Pallas kernels for 19%

profile of v6, /device:TPU:0, one launch (start us, length us, event | category | flops | bytes accessed | tf_op | source)
XLA Modules:
  0.0 321.5 jit_solution(9923624676512462054)
XLA Ops:
  9.4 3.8 %dispatch.2.refs_1_ = bf16[8,40,5120]{2,1,0:T(8,128)(2,1)} custom-call(s32[128,4]{1,0:T(8,128)} %copy.27.routing_ref, bf16[128,5120]{1,0:T(8,128)(2,1)} %refs_0_.2), custom_call_target="tpu_custom_call" | custom-call | flops 1 | bytes 1 | tf_op jit(solution)/shard_map/dispatch/pallas_call | solution.py:134
  13.3 7.2 %all-to-all-start = ((bf16[8,40,5120]{2,1,0:T(8,128)(2,1)}), bf16[8,40,5120]{2,1,0:T(8,128)(2,1)}, u32[]{:S(2)}, u32[]{:S(2)}) async-start(bf16[8,40,5120]{2,1,0:T(8,128)(2,1)} %dispatch.2.refs_1_), calls=%async_computation | async-start | bytes 6553600 | tf_op jit(solution)/shard_map/all_to_all | solution.py:412
  20.5 2.9 collective-permute-start.3
  23.4 4.1 %dispatch.3.refs_0_ = bf16[8,40,5120]{2,1,0:T(8,128)(2,1)} custom-call(s32[128,4]{1,0:T(8,128)} %copy.27.routing_ref, bf16[128,5120]{1,0:T(8,128)(2,1)} %refs_0_.3, bf16[8,40,5120]{2,1,0:T(8,128)(2,1)} %dispatch.2.refs_1_), custom_call_target="tpu_custom_call" | custom-call | flops 1 | bytes 1 | tf_op jit(solution)/shard_map/dispatch/pallas_call | solution.py:134
  27.5 69.4 %collective-permute-done.3.routing_ref.refs_1_ = s32[128,4]{1,0:T(8,128)} collective-permute-done((s32[128,4]{1,0:T(8,128)}, s32[128,4]{1,0:T(8,128)}, u32[]{:S(2)}, u32[]{:S(2)}) %collective-permute-start.3) | collective-permute-done | bytes 2080 | tf_op jit(solution)/shard_map/ppermute | solution.py:394
  97.0 4.5 %all-to-all-start.1 = ((bf16[8,40,5120]{2,1,0:T(8,128)(2,1)}), bf16[8,40,5120]{2,1,0:T(8,128)(2,1)}, u32[]{:S(2)}, u32[]{:S(2)}) async-start(bf16[8,40,5120]{2,1,0:T(8,128)(2,1)} %after.14), calls=%async_computation.1 | async-start | bytes 6553600 | tf_op jit(solution)/shard_map/all_to_all | solution.py:412
  101.5 23.0 %all-gather.7.cloned.1.call-done = bf16[1,5120,768]{2,1,0:T(8,128)(2,1)} async-done(((bf16[1,1280,768]{2,1,0:T(8,128)(2,1)}), bf16[1,5120,768]{2,1,0:T(8,128)(2,1)}) %all-gather.7.cloned.1.call-update) | async-done | bytes 7864336 | tf_op jit(solution)/shard_map/all_gather | solution.py:417
  124.5 11.9 %expert_forward.1 = (bf16[40,5120]{1,0:T(8,128)(2,1)}, bf16[40,5120]{1,0:T(8,128)(2,1)}, bf16[40,5120]{1,0:T(8,128)(2,1)}, bf16[40,5120]{1,0:T(8,128)(2,1)}, bf1...) custom-call(s32[1]{0:T(128)} %bitcast.refs_0_.me_ref, ...), custom_call_target="tpu_custom_call" | custom-call | flops 1 | bytes 1 | tf_op jit(solution)/shard_map/expert_forward/pallas_call | solution.py:242
  136.5 1.5 collective-permute-start.4
  138.0 1.5 collective-permute-start.5
  143.0 14.5 %collective-permute-done.4.refs_1_ = bf16[40,5120]{1,0:T(8,128)(2,1)} collective-permute-done((bf16[40,5120]{1,0:T(8,128)(2,1)}, bf16[40,5120]{1,0:T(8,128)(2,1)}, u32[]{:S(2)}, u32[]{:S(2)}) %collective-permute-start.4) | collective-permute-done | bytes 409632 | tf_op jit(solution)/shard_map/ppermute | solution.py:394
  158.8 2.0 plan.3
  160.8 4.4 %collective-permute-done.5.refs_2_ = bf16[40,5120]{1,0:T(8,128)(2,1)} collective-permute-done((bf16[40,5120]{1,0:T(8,128)(2,1)}, bf16[40,5120]{1,0:T(8,128)(2,1)}, u32[]{:S(2)}, u32[]{:S(2)}) %collective-permute-start.5) | collective-permute-done | bytes 409632 | tf_op jit(solution)/shard_map/ppermute | solution.py:394
  165.1 10.5 %collective-permute-done.6.refs_3_ = bf16[40,5120]{1,0:T(8,128)(2,1)} collective-permute-done((bf16[40,5120]{1,0:T(8,128)(2,1)}, bf16[40,5120]{1,0:T(8,128)(2,1)}, u32[]{:S(2)}, u32[]{:S(2)}) %collective-permute-start.6) | collective-permute-done | bytes 409632 | tf_op jit(solution)/shard_map/ppermute | solution.py:394
  175.6 3.2 %combine.4 = (bf16[32,5120]{1,0:T(8,128)(2,1)}, bf16[96,5120]{1,0:T(8,128)(2,1)}) custom-call(bf16[256,160]{1,0:T(8,128)(2,1)} %get-tuple-element.41.hot_ref, f32[128,256]{1,0:T(8,128)} %get-tuple-element.42.gate_ref, bf16[40,5120]{1,0:T(8,128)(2,1)} %get-tuple-element.43.refs_0_, bf16[40,5120]{1,0:T(8,128)(2,1)} %collective-permute-done.4.refs_1_, ...), custom_call_target="tpu_custom_call" | custom-call | flops 1 | bytes 1 | tf_op jit(solution)/shard_map/combine/pallas_call | solution.py:328
  178.9 3.2 %collective-permute-start.7 = (bf16[32,5120]{1,0:T(8,128)(2,1)}, bf16[32,5120]{1,0:T(8,128)(2,1)}, u32[]{:S(2)}, u32[]{:S(2)}) collective-permute-start(bf16[32,5120]{1,0:T(8,128)(2,1)} %get-tuple-element.47.refs_6_), channel_id=1, source_target_pairs={{0,4},{1,5},{2,6},{3,7},{4,0},{5,1},{6,2},{7,3},{8,12},{9,13},{10,... | collective-permute-start | bytes 983048 | tf_op jit(solution)/shard_map/ppermute | solution.py:394
  182.1 13.7 %expert_backward.1 = (bf16[40,5120]{1,0:T(8,128)(2,1)}, bf16[40,5120]{1,0:T(8,128)(2,1)}, bf16[40,5120]{1,0:T(8,128)(2,1)}, bf16[40,5120]{1,0:T(8,128)(2,1)}, bf...) custom-call(s32[1]{0:T(128)} %bitcast.refs_0_.me_ref, ...), custom_call_target="tpu_custom_call", output_to_operand_aliasing={{8}: (5, {})} | custom-call | flops 1 | bytes 1 | tf_op jit(solution)/shard_map/expert_backward/pallas_call | solution.py:242
  195.8 3.9 %collective-permute-done.2.refs_4_.refs_3_ = bf16[40,5120]{1,0:T(8,128)(2,1)} collective-permute-done((bf16[40,5120]{1,0:T(8,128)(2,1)}, bf16[40,5120]{1,0:T(8,128)(2,1)}, u32[]{:S(2)}, u32[]{:S(2)}) %collective-permute-start.2) | collective-permute-done | bytes 409632 | tf_op jit(solution)/shard_map/ppermute | solution.py:394
  199.7 5.3 %all-to-all-start.2 = ((bf16[4,640,1280]{2,1,0:T(8,128)(2,1)}), bf16[4,640,1280]{2,1,0:T(8,128)(2,1)}, u32[]{:S(2)}, u32[]{:S(2)}) async-start(bf16[4,640,1280]{2,1,0:T(8,128)(2,1)} %after.15), calls=%async_computation.2 | async-start | bytes 13107200 | tf_op jit(solution)/shard_map/all_to_all | solution.py:444
  205.6 2.4 collective-permute-start.8
  208.0 3.4 %collective-permute-start.11 = (bf16[40,5120]{1,0:T(8,128)(2,1)}, bf16[40,5120]{1,0:T(8,128)(2,1)}, u32[]{:S(2)}, u32[]{:S(2)}) collective-permute-start(bf16[40,5120]{1,0:T(8,128)(2,1)} %after.20), channel_id=1, source_target_pairs={{0,3},{1,2},{2,1},{3,0},{4,7},{5,6},{6,5},{7,4},{8,11},{9,10},{10,... | collective-permute-start | bytes 1228808 | tf_op jit(solution)/shard_map/ppermute | solution.py:394
  211.9 27.3 %collective-permute-done.11.refs_3_ = bf16[40,5120]{1,0:T(8,128)(2,1)} collective-permute-done((bf16[40,5120]{1,0:T(8,128)(2,1)}, bf16[40,5120]{1,0:T(8,128)(2,1)}, u32[]{:S(2)}, u32[]{:S(2)}) %collective-permute-start.11) | collective-permute-done | bytes 409632 | tf_op jit(solution)/shard_map/ppermute | solution.py:394
  239.2 8.3 %collective-permute-done.10.refs_2_ = bf16[40,5120]{1,0:T(8,128)(2,1)} collective-permute-done((bf16[40,5120]{1,0:T(8,128)(2,1)}, bf16[40,5120]{1,0:T(8,128)(2,1)}, u32[]{:S(2)}, u32[]{:S(2)}) %collective-permute-start.10) | collective-permute-done | bytes 409632 | tf_op jit(solution)/shard_map/ppermute | solution.py:394
  247.5 2.9 combine.6.refs_1_.refs_0_
  250.4 1.6 collective-permute-done.8.refs_5_.refs_1_
  252.5 2.7 collective-permute-start.14
  256.7 2.0 plan.2
  258.7 30.4 %all-to-all-done.2.traded_ref = bf16[4,640,1280]{2,1,0:T(8,128)(2,1)} async-done(((bf16[4,640,1280]{2,1,0:T(8,128)(2,1)}), bf16[4,640,1280]{2,1,0:T(8,128)(2,1)}, u32[]{:S(2)}, u32[]{:S(2)}) %all-to-all-start.2) | async-done | bytes 6553632 | tf_op jit(solution)/shard_map/all_to_all | solution.py:444
  289.1 12.6 %weight_grads.1 = (bf16[1,1280,768]{2,1,0:T(8,128)(2,1)}, bf16[1,1280,768]{2,1,0:T(8,128)(2,1)}) custom-call(bf16[4,640,1280]{2,1,0:T(8,128)(2,1)} %all-to-all-done.2.traded_ref, bf16[1280,768]{1,0:T(8,128)(2,1)} %all-gather.9.cloned.1.call-done.pre_ref, bf16[1280,768]{1,0:T(8,128)(2,1)} %all-gather.11.cloned.1.call-done.hidden_ref), custom_call_target="tpu_custom_call" | custom-call | flops 1 | bytes 1 | tf_op jit(solution)/shard_map/weight_grads/pallas_call | solution.py:363
  301.7 3.6 %combine.5.refs_5_ = bf16[128,5120]{1,0:T(8,128)(2,1)} custom-call(bf16[256,160]{1,0:T(8,128)(2,1)} %get-tuple-element.36.hot_ref, f32[128,256]{1,0:T(8,128)} %get-tuple-element.37.gate_ref, bf16[40,5120]{1,0:T(8,128)(2,1)} %get-tuple-element.35.refs_0_, bf16[40,5120]{1,0:T(8,128)(2,1)} %collective-permute-done.refs_2_.refs_1_, ...), custom_call_target="tpu_custom_call" | custom-call | flops 1 | bytes 1 | tf_op jit(solution)/shard_map/combine/pallas_call | solution.py:328
  305.3 6.6 %collective-permute-done.15.refs_4_ = bf16[128,5120]{1,0:T(8,128)(2,1)} collective-permute-done((bf16[128,5120]{1,0:T(8,128)(2,1)}, bf16[128,5120]{1,0:T(8,128)(2,1)}, u32[]{:S(2)}, u32[]{:S(2)}) %collective-permute-start.15) | collective-permute-done | bytes 1310752 | tf_op jit(solution)/shard_map/ppermute | solution.py:394
  311.9 3.1 combine.7
  (48 shorter events, 10.1 us)
Async XLA Ops:
  7.2 1.5 copy-start.1
  7.2 1.5 copy-start
  7.2 94.3 %all-gather.5.cloned.1.call-start = ((), (), s32[]{:S(2)}) async-start(), calls=%async_computation.3 | async-start | bytes 9830400 | tf_op jit(solution)/shard_map/all_gather | solution.py:416
  7.9 116.6 %all-gather.7.cloned.1.call-start = ((), (), s32[]{:S(2)}) async-start(), calls=%async_computation.4 | async-start | bytes 9830400 | tf_op jit(solution)/shard_map/all_gather | solution.py:417
  13.3 83.7 %all-to-all-start = ((bf16[8,40,5120]{2,1,0:T(8,128)(2,1)}), bf16[8,40,5120]{2,1,0:T(8,128)(2,1)}, u32[]{:S(2)}, u32[]{:S(2)}) async-start(bf16[8,40,5120]{2,1,0:T(8,128)(2,1)} %dispatch.2.refs_1_), calls=%async_computation | async-start | bytes 6553600 | tf_op jit(solution)/shard_map/all_to_all | solution.py:412
  20.5 76.4 %collective-permute-start.3 = (s32[128,4]{1,0:T(8,128)}, s32[128,4]{1,0:T(8,128)}, u32[]{:S(2)}, u32[]{:S(2)}) collective-permute-start(s32[128,4]{1,0:T(8,128)} %copy.27.routing_ref), channel_id=1, source_target_pairs={{0,4},{1,5},{2,6},{3,7},{4,0},{5,1},{6,2},{7,3},{8,12},{9,13},{10,... | collective-permute-start | bytes 6152 | tf_op jit(solution)/shard_map/ppermute | solution.py:394
  97.0 85.2 %all-to-all-start.1 = ((bf16[8,40,5120]{2,1,0:T(8,128)(2,1)}), bf16[8,40,5120]{2,1,0:T(8,128)(2,1)}, u32[]{:S(2)}, u32[]{:S(2)}) async-start(bf16[8,40,5120]{2,1,0:T(8,128)(2,1)} %after.14), calls=%async_computation.1 | async-start | bytes 6553600 | tf_op jit(solution)/shard_map/all_to_all | solution.py:412
  101.4 157.2 %all-gather.11.cloned.1.call-start = ((), (), s32[]{:S(2)}) async-start(), calls=%async_computation.6 | async-start | bytes 2457600 | tf_op jit(solution)/shard_map/all_gather | solution.py:447
  136.5 21.0 %collective-permute-start.4 = (bf16[40,5120]{1,0:T(8,128)(2,1)}, bf16[40,5120]{1,0:T(8,128)(2,1)}, u32[]{:S(2)}, u32[]{:S(2)}) collective-permute-start(bf16[40,5120]{1,0:T(8,128)(2,1)} %get-tuple-element.44), channel_id=1, source_target_pairs={{0,1},{1,0},{2,3},{3,2},{4,5},{5,4},{6,7},{7,6},{8,9},{9,8},{10,11... | collective-permute-start | bytes 1228808 | tf_op jit(solution)/shard_map/ppermute | solution.py:394
  138.0 27.1 %collective-permute-start.5 = (bf16[40,5120]{1,0:T(8,128)(2,1)}, bf16[40,5120]{1,0:T(8,128)(2,1)}, u32[]{:S(2)}, u32[]{:S(2)}) collective-permute-start(bf16[40,5120]{1,0:T(8,128)(2,1)} %get-tuple-element.45), channel_id=1, source_target_pairs={{0,2},{1,3},{2,0},{3,1},{4,6},{5,7},{6,4},{7,5},{8,10},{9,11},{10,... | collective-permute-start | bytes 1228808 | tf_op jit(solution)/shard_map/ppermute | solution.py:394
  139.5 36.2 %collective-permute-start.6 = (bf16[40,5120]{1,0:T(8,128)(2,1)}, bf16[40,5120]{1,0:T(8,128)(2,1)}, u32[]{:S(2)}, u32[]{:S(2)}) collective-permute-start(bf16[40,5120]{1,0:T(8,128)(2,1)} %get-tuple-element.46), channel_id=1, source_target_pairs={{0,3},{1,2},{2,1},{3,0},{4,7},{5,6},{6,5},{7,4},{8,11},{9,10},{10,... | collective-permute-start | bytes 1228808 | tf_op jit(solution)/shard_map/ppermute | solution.py:394
  140.0 55.8 %collective-permute-start = (bf16[40,5120]{1,0:T(8,128)(2,1)}, bf16[40,5120]{1,0:T(8,128)(2,1)}, u32[]{:S(2)}, u32[]{:S(2)}) collective-permute-start(bf16[40,5120]{1,0:T(8,128)(2,1)} %get-tuple-element.38), channel_id=1, source_target_pairs={{0,1},{1,0},{2,3},{3,2},{4,5},{5,4},{6,7},{7,6},{8,9},{9,8},{10,11... | collective-permute-start | bytes 1228808 | tf_op jit(solution)/shard_map/ppermute | solution.py:394
  141.5 54.3 %collective-permute-start.1 = (bf16[40,5120]{1,0:T(8,128)(2,1)}, bf16[40,5120]{1,0:T(8,128)(2,1)}, u32[]{:S(2)}, u32[]{:S(2)}) collective-permute-start(bf16[40,5120]{1,0:T(8,128)(2,1)} %get-tuple-element.39), channel_id=1, source_target_pairs={{0,2},{1,3},{2,0},{3,1},{4,6},{5,7},{6,4},{7,5},{8,10},{9,11},{10,... | collective-permute-start | bytes 1228808 | tf_op jit(solution)/shard_map/ppermute | solution.py:394
  157.5 42.3 %collective-permute-start.2 = (bf16[40,5120]{1,0:T(8,128)(2,1)}, bf16[40,5120]{1,0:T(8,128)(2,1)}, u32[]{:S(2)}, u32[]{:S(2)}) collective-permute-start(bf16[40,5120]{1,0:T(8,128)(2,1)} %get-tuple-element.40), channel_id=1, source_target_pairs={{0,3},{1,2},{2,1},{3,0},{4,7},{5,6},{6,5},{7,4},{8,11},{9,10},{10,... | collective-permute-start | bytes 1228808 | tf_op jit(solution)/shard_map/ppermute | solution.py:394
  178.9 20.9 %collective-permute-start.7 = (bf16[32,5120]{1,0:T(8,128)(2,1)}, bf16[32,5120]{1,0:T(8,128)(2,1)}, u32[]{:S(2)}, u32[]{:S(2)}) collective-permute-start(bf16[32,5120]{1,0:T(8,128)(2,1)} %get-tuple-element.47.refs_6_), channel_id=1, source_target_pairs={{0,4},{1,5},{2,6},{3,7},{4,0},{5,1},{6,2},{7,3},{8,12},{9,13},{10,... | collective-permute-start | bytes 983048 | tf_op jit(solution)/shard_map/ppermute | solution.py:394
  199.7 89.4 %all-to-all-start.2 = ((bf16[4,640,1280]{2,1,0:T(8,128)(2,1)}), bf16[4,640,1280]{2,1,0:T(8,128)(2,1)}, u32[]{:S(2)}, u32[]{:S(2)}) async-start(bf16[4,640,1280]{2,1,0:T(8,128)(2,1)} %after.15), calls=%async_computation.2 | async-start | bytes 13107200 | tf_op jit(solution)/shard_map/all_to_all | solution.py:444
  205.0 53.6 %all-gather.9.cloned.1.call-start = ((), (), s32[]{:S(2)}) async-start(), calls=%async_computation.5 | async-start | bytes 2457600 | tf_op jit(solution)/shard_map/all_gather | solution.py:448
  205.6 46.4 %collective-permute-start.8 = (bf16[96,5120]{1,0:T(8,128)(2,1)}, bf16[96,5120]{1,0:T(8,128)(2,1)}, u32[]{:S(2)}, u32[]{:S(2)}) collective-permute-start(bf16[96,5120]{1,0:T(8,128)(2,1)} %after.13), channel_id=1, source_target_pairs={{0,4},{1,5},{2,6},{3,7},{4,0},{5,1},{6,2},{7,3},{8,12},{9,13},{10,... | collective-permute-start | bytes 2949128 | tf_op jit(solution)/shard_map/ppermute | solution.py:394
  208.0 31.2 %collective-permute-start.11 = (bf16[40,5120]{1,0:T(8,128)(2,1)}, bf16[40,5120]{1,0:T(8,128)(2,1)}, u32[]{:S(2)}, u32[]{:S(2)}) collective-permute-start(bf16[40,5120]{1,0:T(8,128)(2,1)} %after.20), channel_id=1, source_target_pairs={{0,3},{1,2},{2,1},{3,0},{4,7},{5,6},{6,5},{7,4},{8,11},{9,10},{10,... | collective-permute-start | bytes 1228808 | tf_op jit(solution)/shard_map/ppermute | solution.py:394
  211.4 36.2 %collective-permute-start.10 = (bf16[40,5120]{1,0:T(8,128)(2,1)}, bf16[40,5120]{1,0:T(8,128)(2,1)}, u32[]{:S(2)}, u32[]{:S(2)}) collective-permute-start(bf16[40,5120]{1,0:T(8,128)(2,1)} %after.19), channel_id=1, source_target_pairs={{0,2},{1,3},{2,0},{3,1},{4,6},{5,7},{6,4},{7,5},{8,10},{9,11},{10,... | collective-permute-start | bytes 1228808 | tf_op jit(solution)/shard_map/ppermute | solution.py:394
  211.4 36.2 %collective-permute-start.9 = (bf16[40,5120]{1,0:T(8,128)(2,1)}, bf16[40,5120]{1,0:T(8,128)(2,1)}, u32[]{:S(2)}, u32[]{:S(2)}) collective-permute-start(bf16[40,5120]{1,0:T(8,128)(2,1)} %after.18), channel_id=1, source_target_pairs={{0,1},{1,0},{2,3},{3,2},{4,5},{5,4},{6,7},{7,6},{8,9},{9,8},{10,11... | collective-permute-start | bytes 1228808 | tf_op jit(solution)/shard_map/ppermute | solution.py:394
  252.1 59.8 %collective-permute-start.15 = (bf16[128,5120]{1,0:T(8,128)(2,1)}, bf16[128,5120]{1,0:T(8,128)(2,1)}, u32[]{:S(2)}, u32[]{:S(2)}) collective-permute-start(bf16[128,5120]{1,0:T(8,128)(2,1)} %after.25), channel_id=1, source_target_pairs={{0,4},{1,5},{2,6},{3,7},{4,0},{5,1},{6,2},{7,3},{8,12},{9,13},{10,... | collective-permute-start | bytes 3932168 | tf_op jit(solution)/shard_map/ppermute | solution.py:394
  252.5 52.8 %collective-permute-start.14 = (bf16[40,5120]{1,0:T(8,128)(2,1)}, bf16[40,5120]{1,0:T(8,128)(2,1)}, u32[]{:S(2)}, u32[]{:S(2)}) collective-permute-start(bf16[40,5120]{1,0:T(8,128)(2,1)} %after.24), channel_id=1, source_target_pairs={{0,3},{1,2},{2,1},{3,0},{4,7},{5,6},{6,5},{7,4},{8,11},{9,10},{10,... | collective-permute-start | bytes 1228808 | tf_op jit(solution)/shard_map/ppermute | solution.py:394
  255.2 50.1 %collective-permute-start.13 = (bf16[40,5120]{1,0:T(8,128)(2,1)}, bf16[40,5120]{1,0:T(8,128)(2,1)}, u32[]{:S(2)}, u32[]{:S(2)}) collective-permute-start(bf16[40,5120]{1,0:T(8,128)(2,1)} %after.23), channel_id=1, source_target_pairs={{0,2},{1,3},{2,0},{3,1},{4,6},{5,7},{6,4},{7,5},{8,10},{9,11},{10,... | collective-permute-start | bytes 1228808 | tf_op jit(solution)/shard_map/ppermute | solution.py:394
  256.7 48.6 %collective-permute-start.12 = (bf16[40,5120]{1,0:T(8,128)(2,1)}, bf16[40,5120]{1,0:T(8,128)(2,1)}, u32[]{:S(2)}, u32[]{:S(2)}) collective-permute-start(bf16[40,5120]{1,0:T(8,128)(2,1)} %after.22), channel_id=1, source_target_pairs={{0,1},{1,0},{2,3},{3,2},{4,5},{5,4},{6,7},{7,6},{8,9},{9,8},{10,11... | collective-permute-start | bytes 1228808 | tf_op jit(solution)/shard_map/ppermute | solution.py:394
Sparse Core Ops, SparseCore 0:
  9.6 58.0 all-gather.4
  69.2 55.3 all-gather.6
  136.6 21.8 all-gather.10
  207.7 34.7 all-gather.8

commit v7 on v6

--- a/solution.py
+++ b/solution.py
@@ -424,7 +424,7 @@
     grads_in = swap_direct(after(grads_out, far_routing))
 
     out, sent, hidden, pre_act = expert(me, rows_in, up_weight, down_weight, n_dp)
-    parts = (n_rows // 4, n_rows - n_rows // 4)
+    parts = (5 * n_rows // 16, n_rows - 5 * n_rows // 16)
     far_out = exchange(out[half:])
     far_slots = plan(me, far_routing, half, block, (out[0],))
     near_slots = plan(me, routing, half, block, (out[0],))

time: 322 us -> 320 us (level)
    ppermute x16, waiting for transfers between devices: 147 us -> 141 us  [permute_xor(): return lax.ppermute(values, axis, [(i, i ^ mask) for i in range(size)])]
  transfers between devices with their start and end apart: 23 -> 23, of which waited for: 11 -> 10; matrix products, arithmetic and copies ran while one was open for 0% -> 0% of each run, Pallas kernels for 19% -> 19%
where the time goes in v7:
time: 320 us
  waiting for transfers between devices  199 us (62%)
  Pallas kernels  62.9 us (20%)
  starting transfers between devices  43.7 us (14%)
  between operations  13.9 us (4%)
    ppermute x16, waiting for transfers between devices, permute_xor(): return lax.ppermute(values, axis, [(i, i ^ mask) for i in range(size)])  141 us
    all_to_all x1, waiting for transfers between devices, local(): lax.all_to_all(after(sent, *ready), 'dp', split_axis=0, concat_axis=0, ti...  32.2 us
    ppermute x16, starting transfers between devices, permute_xor(): return lax.ppermute(values, axis, [(i, i ^ mask) for i in range(size)])  26.5 us
    pallas_call x2, Pallas kernels, expert(): pl.pallas_call(functools.partial(expert_kernel, n, n_chunks, backward), i...  25.6 us
    all_gather x1, waiting for transfers between devices, local(): down_weight = lax.all_gather(w_down, 'dp', axis=1, tiled=True)[0]  23 us
    pallas_call x4, Pallas kernels, combine(): pl.pallas_call(functools.partial(combine_kernel, len(blocks), gated, len(...  12.9 us
    pallas_call x1, Pallas kernels, weight_grads(): pl.pallas_call(functools.partial(weight_kernel, n_dp, depth // 2), grid=(...  12.6 us
    all_to_all x2, starting transfers between devices, swap_direct(): lax.all_to_all(blocks, 'expert', split_axis=0, concat_axis=0, tiled=True)  11.7 us
  transfers between devices with their start and end apart: 23, of which 10 were waited for; matrix products, arithmetic and copies ran while one was open for 0% of the time, Pallas kernels for 19%

profile of v7, /device:TPU:0, one launch (start us, length us, event | category | flops | bytes accessed | tf_op | source)
XLA Modules:
  0.0 319.8 jit_solution(16879151225595477309)
XLA Ops:
  9.4 3.8 %dispatch.2.refs_1_ = bf16[8,40,5120]{2,1,0:T(8,128)(2,1)} custom-call(s32[128,4]{1,0:T(8,128)} %copy.27.routing_ref, bf16[128,5120]{1,0:T(8,128)(2,1)} %refs_0_.2), custom_call_target="tpu_custom_call" | custom-call | flops 1 | bytes 1 | tf_op jit(solution)/shard_map/dispatch/pallas_call | solution.py:134
  13.3 7.2 %all-to-all-start = ((bf16[8,40,5120]{2,1,0:T(8,128)(2,1)}), bf16[8,40,5120]{2,1,0:T(8,128)(2,1)}, u32[]{:S(2)}, u32[]{:S(2)}) async-start(bf16[8,40,5120]{2,1,0:T(8,128)(2,1)} %dispatch.2.refs_1_), calls=%async_computation | async-start | bytes 6553600 | tf_op jit(solution)/shard_map/all_to_all | solution.py:412
  20.5 2.9 collective-permute-start.3
  23.4 4.1 %dispatch.3.refs_0_ = bf16[8,40,5120]{2,1,0:T(8,128)(2,1)} custom-call(s32[128,4]{1,0:T(8,128)} %copy.27.routing_ref, bf16[128,5120]{1,0:T(8,128)(2,1)} %refs_0_.3, bf16[8,40,5120]{2,1,0:T(8,128)(2,1)} %dispatch.2.refs_1_), custom_call_target="tpu_custom_call" | custom-call | flops 1 | bytes 1 | tf_op jit(solution)/shard_map/dispatch/pallas_call | solution.py:134
  27.5 69.4 %collective-permute-done.3.routing_ref.refs_1_ = s32[128,4]{1,0:T(8,128)} collective-permute-done((s32[128,4]{1,0:T(8,128)}, s32[128,4]{1,0:T(8,128)}, u32[]{:S(2)}, u32[]{:S(2)}) %collective-permute-start.3) | collective-permute-done | bytes 2080 | tf_op jit(solution)/shard_map/ppermute | solution.py:394
  97.0 4.5 %all-to-all-start.1 = ((bf16[8,40,5120]{2,1,0:T(8,128)(2,1)}), bf16[8,40,5120]{2,1,0:T(8,128)(2,1)}, u32[]{:S(2)}, u32[]{:S(2)}) async-start(bf16[8,40,5120]{2,1,0:T(8,128)(2,1)} %after.14), calls=%async_computation.1 | async-start | bytes 6553600 | tf_op jit(solution)/shard_map/all_to_all | solution.py:412
  101.5 23.0 %all-gather.7.cloned.1.call-done = bf16[1,5120,768]{2,1,0:T(8,128)(2,1)} async-done(((bf16[1,1280,768]{2,1,0:T(8,128)(2,1)}), bf16[1,5120,768]{2,1,0:T(8,128)(2,1)}) %all-gather.7.cloned.1.call-update) | async-done | bytes 7864336 | tf_op jit(solution)/shard_map/all_gather | solution.py:417
  124.5 11.9 %expert_forward.1 = (bf16[40,5120]{1,0:T(8,128)(2,1)}, bf16[40,5120]{1,0:T(8,128)(2,1)}, bf16[40,5120]{1,0:T(8,128)(2,1)}, bf16[40,5120]{1,0:T(8,128)(2,1)}, bf1...) custom-call(s32[1]{0:T(128)} %bitcast.refs_0_.me_ref, ...), custom_call_target="tpu_custom_call" | custom-call | flops 1 | bytes 1 | tf_op jit(solution)/shard_map/expert_forward/pallas_call | solution.py:242
  136.5 1.5 collective-permute-start.4
  143.0 2.0 plan.3
  144.9 12.5 %collective-permute-done.4.refs_1_ = bf16[40,5120]{1,0:T(8,128)(2,1)} collective-permute-done((bf16[40,5120]{1,0:T(8,128)(2,1)}, bf16[40,5120]{1,0:T(8,128)(2,1)}, u32[]{:S(2)}, u32[]{:S(2)}) %collective-permute-start.4) | collective-permute-done | bytes 409632 | tf_op jit(solution)/shard_map/ppermute | solution.py:394
  158.8 6.3 %collective-permute-done.5.refs_2_ = bf16[40,5120]{1,0:T(8,128)(2,1)} collective-permute-done((bf16[40,5120]{1,0:T(8,128)(2,1)}, bf16[40,5120]{1,0:T(8,128)(2,1)}, u32[]{:S(2)}, u32[]{:S(2)}) %collective-permute-start.5) | collective-permute-done | bytes 409632 | tf_op jit(solution)/shard_map/ppermute | solution.py:394
  165.1 10.5 %collective-permute-done.6.refs_3_ = bf16[40,5120]{1,0:T(8,128)(2,1)} collective-permute-done((bf16[40,5120]{1,0:T(8,128)(2,1)}, bf16[40,5120]{1,0:T(8,128)(2,1)}, u32[]{:S(2)}, u32[]{:S(2)}) %collective-permute-start.6) | collective-permute-done | bytes 409632 | tf_op jit(solution)/shard_map/ppermute | solution.py:394
  175.6 3.2 %combine.4 = (bf16[40,5120]{1,0:T(8,128)(2,1)}, bf16[88,5120]{1,0:T(8,128)(2,1)}) custom-call(bf16[256,160]{1,0:T(8,128)(2,1)} %get-tuple-element.41.hot_ref, f32[128,256]{1,0:T(8,128)} %get-tuple-element.42.gate_ref, bf16[40,5120]{1,0:T(8,128)(2,1)} %get-tuple-element.43.refs_0_, bf16[40,5120]{1,0:T(8,128)(2,1)} %collective-permute-done.4.refs_1_, ...), custom_call_target="tpu_custom_call" | custom-call | flops 1 | bytes 1 | tf_op jit(solution)/shard_map/combine/pallas_call | solution.py:328
  178.9 3.2 %collective-permute-start.7 = (bf16[40,5120]{1,0:T(8,128)(2,1)}, bf16[40,5120]{1,0:T(8,128)(2,1)}, u32[]{:S(2)}, u32[]{:S(2)}) collective-permute-start(bf16[40,5120]{1,0:T(8,128)(2,1)} %get-tuple-element.47.refs_6_), channel_id=1, source_target_pairs={{0,4},{1,5},{2,6},{3,7},{4,0},{5,1},{6,2},{7,3},{8,12},{9,13},{10,... | collective-permute-start | bytes 1228808 | tf_op jit(solution)/shard_map/ppermute | solution.py:394
  182.1 13.7 %expert_backward.1 = (bf16[40,5120]{1,0:T(8,128)(2,1)}, bf16[40,5120]{1,0:T(8,128)(2,1)}, bf16[40,5120]{1,0:T(8,128)(2,1)}, bf16[40,5120]{1,0:T(8,128)(2,1)}, bf...) custom-call(s32[1]{0:T(128)} %bitcast.refs_0_.me_ref, ...), custom_call_target="tpu_custom_call", output_to_operand_aliasing={{8}: (5, {})} | custom-call | flops 1 | bytes 1 | tf_op jit(solution)/shard_map/expert_backward/pallas_call | solution.py:242
  195.8 5.7 %collective-permute-done.2.refs_4_.refs_3_ = bf16[40,5120]{1,0:T(8,128)(2,1)} collective-permute-done((bf16[40,5120]{1,0:T(8,128)(2,1)}, bf16[40,5120]{1,0:T(8,128)(2,1)}, u32[]{:S(2)}, u32[]{:S(2)}) %collective-permute-start.2) | collective-permute-done | bytes 409632 | tf_op jit(solution)/shard_map/ppermute | solution.py:394
  201.5 5.3 %all-to-all-start.2 = ((bf16[4,640,1280]{2,1,0:T(8,128)(2,1)}), bf16[4,640,1280]{2,1,0:T(8,128)(2,1)}, u32[]{:S(2)}, u32[]{:S(2)}) async-start(bf16[4,640,1280]{2,1,0:T(8,128)(2,1)} %after.15), calls=%async_computation.2 | async-start | bytes 13107200 | tf_op jit(solution)/shard_map/all_to_all | solution.py:444
  207.4 2.4 collective-permute-start.8
  209.8 3.4 %collective-permute-start.11 = (bf16[40,5120]{1,0:T(8,128)(2,1)}, bf16[40,5120]{1,0:T(8,128)(2,1)}, u32[]{:S(2)}, u32[]{:S(2)}) collective-permute-start(bf16[40,5120]{1,0:T(8,128)(2,1)} %after.20), channel_id=1, source_target_pairs={{0,3},{1,2},{2,1},{3,0},{4,7},{5,6},{6,5},{7,4},{8,11},{9,10},{10,... | collective-permute-start | bytes 1228808 | tf_op jit(solution)/shard_map/ppermute | solution.py:394
  213.7 25.5 %collective-permute-done.11.refs_3_ = bf16[40,5120]{1,0:T(8,128)(2,1)} collective-permute-done((bf16[40,5120]{1,0:T(8,128)(2,1)}, bf16[40,5120]{1,0:T(8,128)(2,1)}, u32[]{:S(2)}, u32[]{:S(2)}) %collective-permute-start.11) | collective-permute-done | bytes 409632 | tf_op jit(solution)/shard_map/ppermute | solution.py:394
  239.2 8.3 %collective-permute-done.10.refs_2_ = bf16[40,5120]{1,0:T(8,128)(2,1)} collective-permute-done((bf16[40,5120]{1,0:T(8,128)(2,1)}, bf16[40,5120]{1,0:T(8,128)(2,1)}, u32[]{:S(2)}, u32[]{:S(2)}) %collective-permute-start.10) | collective-permute-done | bytes 409632 | tf_op jit(solution)/shard_map/ppermute | solution.py:394
  247.5 2.9 combine.6.refs_1_.refs_0_
  250.5 2.0 collective-permute-start.15
  252.5 1.7 collective-permute-start.14
  254.2 2.5 collective-permute-start.13
  256.7 2.0 plan.2
  258.7 32.2 %all-to-all-done.2.traded_ref = bf16[4,640,1280]{2,1,0:T(8,128)(2,1)} async-done(((bf16[4,640,1280]{2,1,0:T(8,128)(2,1)}), bf16[4,640,1280]{2,1,0:T(8,128)(2,1)}, u32[]{:S(2)}, u32[]{:S(2)}) %all-to-all-start.2) | async-done | bytes 6553632 | tf_op jit(solution)/shard_map/all_to_all | solution.py:444
  290.8 12.6 %weight_grads.1 = (bf16[1,1280,768]{2,1,0:T(8,128)(2,1)}, bf16[1,1280,768]{2,1,0:T(8,128)(2,1)}) custom-call(bf16[4,640,1280]{2,1,0:T(8,128)(2,1)} %all-to-all-done.2.traded_ref, bf16[1280,768]{1,0:T(8,128)(2,1)} %all-gather.9.cloned.1.call-done.pre_ref, bf16[1280,768]{1,0:T(8,128)(2,1)} %all-gather.11.cloned.1.call-done.hidden_ref), custom_call_target="tpu_custom_call" | custom-call | flops 1 | bytes 1 | tf_op jit(solution)/shard_map/weight_grads/pallas_call | solution.py:363
  303.4 3.6 %combine.5.refs_5_ = bf16[128,5120]{1,0:T(8,128)(2,1)} custom-call(bf16[256,160]{1,0:T(8,128)(2,1)} %get-tuple-element.36.hot_ref, f32[128,256]{1,0:T(8,128)} %get-tuple-element.37.gate_ref, bf16[40,5120]{1,0:T(8,128)(2,1)} %get-tuple-element.35.refs_0_, bf16[40,5120]{1,0:T(8,128)(2,1)} %collective-permute-done.refs_2_.refs_1_, ...), custom_call_target="tpu_custom_call" | custom-call | flops 1 | bytes 1 | tf_op jit(solution)/shard_map/combine/pallas_call | solution.py:328
  307.1 3.1 collective-permute-done.15.refs_4_
  310.2 3.1 combine.7
  (48 shorter events, 9.8 us)
Async XLA Ops:
  7.2 1.5 copy-start.1
  7.2 1.5 copy-start
  7.2 94.3 %all-gather.5.cloned.1.call-start = ((), (), s32[]{:S(2)}) async-start(), calls=%async_computation.3 | async-start | bytes 9830400 | tf_op jit(solution)/shard_map/all_gather | solution.py:416
  7.9 116.6 %all-gather.7.cloned.1.call-start = ((), (), s32[]{:S(2)}) async-start(), calls=%async_computation.4 | async-start | bytes 9830400 | tf_op jit(solution)/shard_map/all_gather | solution.py:417
  13.3 83.7 %all-to-all-start = ((bf16[8,40,5120]{2,1,0:T(8,128)(2,1)}), bf16[8,40,5120]{2,1,0:T(8,128)(2,1)}, u32[]{:S(2)}, u32[]{:S(2)}) async-start(bf16[8,40,5120]{2,1,0:T(8,128)(2,1)} %dispatch.2.refs_1_), calls=%async_computation | async-start | bytes 6553600 | tf_op jit(solution)/shard_map/all_to_all | solution.py:412
  20.5 76.4 %collective-permute-start.3 = (s32[128,4]{1,0:T(8,128)}, s32[128,4]{1,0:T(8,128)}, u32[]{:S(2)}, u32[]{:S(2)}) collective-permute-start(s32[128,4]{1,0:T(8,128)} %copy.27.routing_ref), channel_id=1, source_target_pairs={{0,4},{1,5},{2,6},{3,7},{4,0},{5,1},{6,2},{7,3},{8,12},{9,13},{10,... | collective-permute-start | bytes 6152 | tf_op jit(solution)/shard_map/ppermute | solution.py:394
  97.0 85.2 %all-to-all-start.1 = ((bf16[8,40,5120]{2,1,0:T(8,128)(2,1)}), bf16[8,40,5120]{2,1,0:T(8,128)(2,1)}, u32[]{:S(2)}, u32[]{:S(2)}) async-start(bf16[8,40,5120]{2,1,0:T(8,128)(2,1)} %after.14), calls=%async_computation.1 | async-start | bytes 6553600 | tf_op jit(solution)/shard_map/all_to_all | solution.py:412
  101.4 157.2 %all-gather.11.cloned.1.call-start = ((), (), s32[]{:S(2)}) async-start(), calls=%async_computation.6 | async-start | bytes 2457600 | tf_op jit(solution)/shard_map/all_gather | solution.py:447
  136.5 21.0 %collective-permute-start.4 = (bf16[40,5120]{1,0:T(8,128)(2,1)}, bf16[40,5120]{1,0:T(8,128)(2,1)}, u32[]{:S(2)}, u32[]{:S(2)}) collective-permute-start(bf16[40,5120]{1,0:T(8,128)(2,1)} %get-tuple-element.44), channel_id=1, source_target_pairs={{0,1},{1,0},{2,3},{3,2},{4,5},{5,4},{6,7},{7,6},{8,9},{9,8},{10,11... | collective-permute-start | bytes 1228808 | tf_op jit(solution)/shard_map/ppermute | solution.py:394
  138.0 27.1 %collective-permute-start.5 = (bf16[40,5120]{1,0:T(8,128)(2,1)}, bf16[40,5120]{1,0:T(8,128)(2,1)}, u32[]{:S(2)}, u32[]{:S(2)}) collective-permute-start(bf16[40,5120]{1,0:T(8,128)(2,1)} %get-tuple-element.45), channel_id=1, source_target_pairs={{0,2},{1,3},{2,0},{3,1},{4,6},{5,7},{6,4},{7,5},{8,10},{9,11},{10,... | collective-permute-start | bytes 1228808 | tf_op jit(solution)/shard_map/ppermute | solution.py:394
  139.5 36.2 %collective-permute-start.6 = (bf16[40,5120]{1,0:T(8,128)(2,1)}, bf16[40,5120]{1,0:T(8,128)(2,1)}, u32[]{:S(2)}, u32[]{:S(2)}) collective-permute-start(bf16[40,5120]{1,0:T(8,128)(2,1)} %get-tuple-element.46), channel_id=1, source_target_pairs={{0,3},{1,2},{2,1},{3,0},{4,7},{5,6},{6,5},{7,4},{8,11},{9,10},{10,... | collective-permute-start | bytes 1228808 | tf_op jit(solution)/shard_map/ppermute | solution.py:394
  140.0 55.8 %collective-permute-start = (bf16[40,5120]{1,0:T(8,128)(2,1)}, bf16[40,5120]{1,0:T(8,128)(2,1)}, u32[]{:S(2)}, u32[]{:S(2)}) collective-permute-start(bf16[40,5120]{1,0:T(8,128)(2,1)} %get-tuple-element.38), channel_id=1, source_target_pairs={{0,1},{1,0},{2,3},{3,2},{4,5},{5,4},{6,7},{7,6},{8,9},{9,8},{10,11... | collective-permute-start | bytes 1228808 | tf_op jit(solution)/shard_map/ppermute | solution.py:394
  141.5 54.3 %collective-permute-start.1 = (bf16[40,5120]{1,0:T(8,128)(2,1)}, bf16[40,5120]{1,0:T(8,128)(2,1)}, u32[]{:S(2)}, u32[]{:S(2)}) collective-permute-start(bf16[40,5120]{1,0:T(8,128)(2,1)} %get-tuple-element.39), channel_id=1, source_target_pairs={{0,2},{1,3},{2,0},{3,1},{4,6},{5,7},{6,4},{7,5},{8,10},{9,11},{10,... | collective-permute-start | bytes 1228808 | tf_op jit(solution)/shard_map/ppermute | solution.py:394
  157.5 44.0 %collective-permute-start.2 = (bf16[40,5120]{1,0:T(8,128)(2,1)}, bf16[40,5120]{1,0:T(8,128)(2,1)}, u32[]{:S(2)}, u32[]{:S(2)}) collective-permute-start(bf16[40,5120]{1,0:T(8,128)(2,1)} %get-tuple-element.40), channel_id=1, source_target_pairs={{0,3},{1,2},{2,1},{3,0},{4,7},{5,6},{6,5},{7,4},{8,11},{9,10},{10,... | collective-permute-start | bytes 1228808 | tf_op jit(solution)/shard_map/ppermute | solution.py:394
  178.9 22.6 %collective-permute-start.7 = (bf16[40,5120]{1,0:T(8,128)(2,1)}, bf16[40,5120]{1,0:T(8,128)(2,1)}, u32[]{:S(2)}, u32[]{:S(2)}) collective-permute-start(bf16[40,5120]{1,0:T(8,128)(2,1)} %get-tuple-element.47.refs_6_), channel_id=1, source_target_pairs={{0,4},{1,5},{2,6},{3,7},{4,0},{5,1},{6,2},{7,3},{8,12},{9,13},{10,... | collective-permute-start | bytes 1228808 | tf_op jit(solution)/shard_map/ppermute | solution.py:394
  201.5 89.4 %all-to-all-start.2 = ((bf16[4,640,1280]{2,1,0:T(8,128)(2,1)}), bf16[4,640,1280]{2,1,0:T(8,128)(2,1)}, u32[]{:S(2)}, u32[]{:S(2)}) async-start(bf16[4,640,1280]{2,1,0:T(8,128)(2,1)} %after.15), calls=%async_computation.2 | async-start | bytes 13107200 | tf_op jit(solution)/shard_map/all_to_all | solution.py:444
  206.8 51.9 %all-gather.9.cloned.1.call-start = ((), (), s32[]{:S(2)}) async-start(), calls=%async_computation.5 | async-start | bytes 2457600 | tf_op jit(solution)/shard_map/all_gather | solution.py:448
  207.4 43.1 %collective-permute-start.8 = (bf16[88,5120]{1,0:T(8,128)(2,1)}, bf16[88,5120]{1,0:T(8,128)(2,1)}, u32[]{:S(2)}, u32[]{:S(2)}) collective-permute-start(bf16[88,5120]{1,0:T(8,128)(2,1)} %after.13), channel_id=1, source_target_pairs={{0,4},{1,5},{2,6},{3,7},{4,0},{5,1},{6,2},{7,3},{8,12},{9,13},{10,... | collective-permute-start | bytes 2703368 | tf_op jit(solution)/shard_map/ppermute | solution.py:394
  209.8 29.5 %collective-permute-start.11 = (bf16[40,5120]{1,0:T(8,128)(2,1)}, bf16[40,5120]{1,0:T(8,128)(2,1)}, u32[]{:S(2)}, u32[]{:S(2)}) collective-permute-start(bf16[40,5120]{1,0:T(8,128)(2,1)} %after.20), channel_id=1, source_target_pairs={{0,3},{1,2},{2,1},{3,0},{4,7},{5,6},{6,5},{7,4},{8,11},{9,10},{10,... | collective-permute-start | bytes 1228808 | tf_op jit(solution)/shard_map/ppermute | solution.py:394
  213.1 34.4 %collective-permute-start.10 = (bf16[40,5120]{1,0:T(8,128)(2,1)}, bf16[40,5120]{1,0:T(8,128)(2,1)}, u32[]{:S(2)}, u32[]{:S(2)}) collective-permute-start(bf16[40,5120]{1,0:T(8,128)(2,1)} %after.19), channel_id=1, source_target_pairs={{0,2},{1,3},{2,0},{3,1},{4,6},{5,7},{6,4},{7,5},{8,10},{9,11},{10,... | collective-permute-start | bytes 1228808 | tf_op jit(solution)/shard_map/ppermute | solution.py:394
  213.1 34.4 %collective-permute-start.9 = (bf16[40,5120]{1,0:T(8,128)(2,1)}, bf16[40,5120]{1,0:T(8,128)(2,1)}, u32[]{:S(2)}, u32[]{:S(2)}) collective-permute-start(bf16[40,5120]{1,0:T(8,128)(2,1)} %after.18), channel_id=1, source_target_pairs={{0,1},{1,0},{2,3},{3,2},{4,5},{5,4},{6,7},{7,6},{8,9},{9,8},{10,11... | collective-permute-start | bytes 1228808 | tf_op jit(solution)/shard_map/ppermute | solution.py:394
  250.5 59.7 %collective-permute-start.15 = (bf16[128,5120]{1,0:T(8,128)(2,1)}, bf16[128,5120]{1,0:T(8,128)(2,1)}, u32[]{:S(2)}, u32[]{:S(2)}) collective-permute-start(bf16[128,5120]{1,0:T(8,128)(2,1)} %after.25), channel_id=1, source_target_pairs={{0,4},{1,5},{2,6},{3,7},{4,0},{5,1},{6,2},{7,3},{8,12},{9,13},{10,... | collective-permute-start | bytes 3932168 | tf_op jit(solution)/shard_map/ppermute | solution.py:394
  252.5 54.6 %collective-permute-start.14 = (bf16[40,5120]{1,0:T(8,128)(2,1)}, bf16[40,5120]{1,0:T(8,128)(2,1)}, u32[]{:S(2)}, u32[]{:S(2)}) collective-permute-start(bf16[40,5120]{1,0:T(8,128)(2,1)} %after.24), channel_id=1, source_target_pairs={{0,3},{1,2},{2,1},{3,0},{4,7},{5,6},{6,5},{7,4},{8,11},{9,10},{10,... | collective-permute-start | bytes 1228808 | tf_op jit(solution)/shard_map/ppermute | solution.py:394
  254.2 52.8 %collective-permute-start.13 = (bf16[40,5120]{1,0:T(8,128)(2,1)}, bf16[40,5120]{1,0:T(8,128)(2,1)}, u32[]{:S(2)}, u32[]{:S(2)}) collective-permute-start(bf16[40,5120]{1,0:T(8,128)(2,1)} %after.23), channel_id=1, source_target_pairs={{0,2},{1,3},{2,0},{3,1},{4,6},{5,7},{6,4},{7,5},{8,10},{9,11},{10,... | collective-permute-start | bytes 1228808 | tf_op jit(solution)/shard_map/ppermute | solution.py:394
  256.7 50.4 %collective-permute-start.12 = (bf16[40,5120]{1,0:T(8,128)(2,1)}, bf16[40,5120]{1,0:T(8,128)(2,1)}, u32[]{:S(2)}, u32[]{:S(2)}) collective-permute-start(bf16[40,5120]{1,0:T(8,128)(2,1)} %after.22), channel_id=1, source_target_pairs={{0,1},{1,0},{2,3},{3,2},{4,5},{5,4},{6,7},{7,6},{8,9},{9,8},{10,11... | collective-permute-start | bytes 1228808 | tf_op jit(solution)/shard_map/ppermute | solution.py:394
Sparse Core Ops, SparseCore 0:
  9.6 58.0 all-gather.4
  69.2 55.3 all-gather.6
  136.6 21.8 all-gather.10
  209.5 34.7 all-gather.8
